TPU v7x, 128 devices: a whole 4x4x4 slice. The times are simulated.
128 devices in a mesh: dev: 2 (over x_hi), row: 32 (over z, y, x_lo), col: 2 (over core).
Axes of the slice: x: 4 (x_hi: 2, x_lo: 2; x = x_hi * 2 + x_lo), y: 4, z: 4, core: 2. Of those that a mesh axis runs over, the one named last changes fastest.
Arguments:
- tokens: bfloat16 [4, 4096, 1600], P('dev', 'row', 'col'), may hold values from -6 to 6
- segments: int32 [4, 4096], P('dev'), may hold values from 0 to 3, as said below
- first_gain: float32 [1600], P('col'), may hold values from 0.25 to 1.75
- first_bias: float32 [1600], P('col'), may hold values from -4 to 4
- attention_in: bfloat16 [1600, 3, 1600], P('row', None, 'col'), may hold values from -0.15625 to 0.15625
- attention_bias: float32 [2, 1600], P(None, 'col'), may hold values from -6 to 6
- attention_out: bfloat16 [1600, 1600], P('row', 'col'), may hold values from -2.5 to 2.5
- output_bias: float32 [1600], P('col'), may hold values from -4 to 4
- second_gain: float32 [1600], P('col'), may hold values from 0.25 to 1.75
- second_bias: float32 [1600], P('col'), may hold values from -4 to 4
- expand_weight: bfloat16 [1600, 6400], P('row', 'col'), may hold values from -0.15625 to 0.15625
- expand_bias: float32 [6400], P('col'), may hold values from -6 to 6
- contract_weight: bfloat16 [6400, 1600], P('row', 'col'), may hold values from -0.078125 to 0.078125
- contract_bias: float32 [1600], P('col'), may hold values from -4 to 4
- cotangent: bfloat16 [4, 4096, 1600], P('dev', 'row', 'col'), may hold values from -6 to 6
Outputs:
- result: bfloat16 [4, 4096, 1600], P('dev', 'row', 'col')
- gradient_tokens: bfloat16 [4, 4096, 1600], P('dev', 'row', 'col')
- gradient_first_gain: float32 [1600], P('col')
- gradient_first_bias: float32 [1600], P('col')
- gradient_attention_in: float32 [1600, 3, 1600], P('row', None, 'col')
- gradient_attention_bias: float32 [2, 1600], P(None, 'col')
- gradient_attention_out: float32 [1600, 1600], P('row', 'col')
- gradient_output_bias: float32 [1600], P('col')
- gradient_second_gain: float32 [1600], P('col')
- gradient_second_bias: float32 [1600], P('col')
- gradient_expand_weight: float32 [1600, 6400], P('row', 'col')
- gradient_expand_bias: float32 [6400], P('col')
- gradient_contract_weight: float32 [6400, 1600], P('row', 'col')
- gradient_contract_bias: float32 [1600], P('col')
Inputs may be any that keep to these rules, and one draw needn't show every extreme that they name: `segments`: segment numbers of a sequence start at 0 and never fall along it; a change marks the start of a new document.
All inputs are finite; a program needn't handle non-finite values.
Results may differ from a plain program's by a relative error of at most 0.025.
Values may be sent and summed in bfloat16 or wider, within the bound.
A program may use at most 512 MiB of HBM per device.

v0:
```python
import jax
import jax.numpy as jnp
from jax import lax
from jax.sharding import PartitionSpec as P

D = 1600
HD = 64


def width_sums(first_sum, second_sum):
    return lax.psum((first_sum, second_sum), "col")


def full_rows(values):
    return lax.all_gather(values, "col", axis=1, tiled=True)


def feature_sums(values):
    return lax.psum_scatter(
        values.astype(jnp.bfloat16), "col", scatter_dimension=1, tiled=True
    ).astype(jnp.float32)


def head_layout(values):
    return lax.all_to_all(values, "col", split_axis=1, concat_axis=3, tiled=True)


def token_layout(values):
    return lax.all_to_all(values, "col", split_axis=3, concat_axis=1, tiled=True)


def norm_forward(values, norm_gain, norm_bias):
    totals = width_sums(jnp.sum(values, axis=1), jnp.sum(values * values, axis=1))
    averages = totals[0] / D
    reciprocal = lax.rsqrt(totals[1] / D - averages * averages + 1e-05)
    normed = (values - averages[:, None]) * reciprocal[:, None]
    return (normed, reciprocal, normed * norm_gain + norm_bias)


def norm_backward(incoming, normed, reciprocal, norm_gain):
    scaled = incoming * norm_gain
    totals = width_sums(jnp.sum(scaled, axis=1), jnp.sum(scaled * normed, axis=1))
    return reciprocal[:, None] * (
        scaled - totals[0][:, None] / D - normed * (totals[1][:, None] / D)
    )


def mask_scores(queries, keys_part, seg_ids, offset):
    query_len = queries.shape[0]
    full_len = keys_part.shape[0]
    head_count = queries.shape[1] // HD
    query_heads = queries.reshape(query_len, head_count, HD)
    key_heads = keys_part.reshape(full_len, head_count, HD)
    scores = jnp.einsum(
        "qhd,khd->hqk", query_heads, key_heads, preferred_element_type=jnp.float32
    ) * HD ** (-0.5)
    seg_query = lax.dynamic_slice_in_dim(seg_ids, offset, query_len, 0)
    positions = jnp.arange(full_len)
    query_pos = offset + jnp.arange(query_len)
    allowed = (seg_query[:, None] == seg_ids[None, :]) & (positions[None, :] <= query_pos[:, None])
    return jnp.where(allowed[None], scores, -1e30)


def per_device(
    tokens,
    segments,
    first_gain,
    first_bias,
    attention_in,
    attention_bias,
    attention_out,
    output_bias,
    second_gain,
    second_bias,
    expand_weight,
    expand_bias,
    contract_weight,
    contract_bias,
    cotangent,
):
    batch_seqs, block_len, width_part = tokens.shape
    row_total = batch_seqs * block_len
    col_count = lax.axis_size("col")
    query_len = block_len // col_count
    full_len = segments.shape[1]
    head_count = D // HD
    score_scale = HD ** (-0.5)
    offset = (lax.axis_index("row") * col_count + lax.axis_index("col")) * query_len
    gathered = (
        lax.all_gather(attention_in, "row", axis=0, tiled=True),
        lax.all_gather(attention_out, "row", axis=0, tiled=True),
        lax.all_gather(expand_weight, "row", axis=0, tiled=True),
        lax.all_gather(contract_weight, "row", axis=0, tiled=True),
    )
    weight_qkv = gathered[0].reshape(D, 3 * width_part)
    weight_out = gathered[1]
    weight_expand = gathered[2]
    weight_contract = gathered[3]
    float_tokens = tokens.astype(jnp.float32).reshape(row_total, width_part)
    normed_one, recip_one, hidden_one = norm_forward(float_tokens, first_gain, first_bias)
    rows_one = full_rows(hidden_one.astype(jnp.bfloat16))
    bias_three = jnp.stack(
        (attention_bias[0], jnp.zeros_like(attention_bias[0]), attention_bias[1])
    )
    projected = jnp.dot(rows_one, weight_qkv, preferred_element_type=jnp.float32).reshape(
        row_total, 3, width_part
    )
    projected = (projected + bias_three[None]).astype(jnp.bfloat16)
    qkv_heads = head_layout(projected.reshape(batch_seqs, block_len, 3, width_part))
    keys_both = lax.all_gather(qkv_heads[:, :, 1:], ("row", "col"), axis=1, tiled=True)

    def forward_one(item):
        queries, key_pair, seg_ids = item
        scores = mask_scores(queries, key_pair[:, 0], seg_ids, offset)
        log_total = jax.nn.logsumexp(scores, axis=-1, keepdims=True)
        probs_low = jnp.exp(scores - log_total).astype(jnp.bfloat16)
        value_heads = key_pair[:, 1].reshape(full_len, head_count, HD)
        mixed = jnp.einsum(
            "hqk,khd->qhd", probs_low, value_heads, preferred_element_type=jnp.float32
        )
        return (mixed.reshape(query_len, D).astype(jnp.bfloat16), log_total)

    attended, log_totals = lax.map(forward_one, (qkv_heads[:, :, 0], keys_both, segments))
    attended_tok = token_layout(attended[:, :, None]).reshape(row_total, width_part)
    rows_attn = full_rows(attended_tok)
    middle = float_tokens + (
        jnp.dot(rows_attn, weight_out, preferred_element_type=jnp.float32) + output_bias
    )
    normed_two, recip_two, hidden_two = norm_forward(middle, second_gain, second_bias)
    rows_two = full_rows(hidden_two.astype(jnp.bfloat16))
    pre_gelu = jnp.dot(rows_two, weight_expand, preferred_element_type=jnp.float32) + expand_bias
    gelu_out = jax.nn.gelu(pre_gelu, approximate=True)
    rows_gelu = full_rows(gelu_out.astype(jnp.bfloat16))
    branch_out = (
        jnp.dot(rows_gelu, weight_contract, preferred_element_type=jnp.float32) + contract_bias
    )
    result = (middle + branch_out).astype(jnp.bfloat16).reshape(batch_seqs, block_len, width_part)
    grad_low = cotangent.reshape(row_total, width_part)
    grad_float = grad_low.astype(jnp.float32)
    part_contract = jnp.dot(rows_gelu.T, grad_low, preferred_element_type=jnp.float32)
    grad_gelu = feature_sums(
        jnp.dot(grad_low, weight_contract.T, preferred_element_type=jnp.float32)
    )
    gelu_value, gelu_back = jax.vjp(lambda inner: jax.nn.gelu(inner, approximate=True), pre_gelu)
    grad_pre = gelu_back(grad_gelu)[0].astype(jnp.bfloat16)
    part_expand = jnp.dot(rows_two.T, grad_pre, preferred_element_type=jnp.float32)
    grad_two = feature_sums(jnp.dot(grad_pre, weight_expand.T, preferred_element_type=jnp.float32))
    grad_middle = grad_float + norm_backward(grad_two, normed_two, recip_two, second_gain)
    grad_attn = grad_middle.astype(jnp.bfloat16)
    part_out = jnp.dot(rows_attn.T, grad_attn, preferred_element_type=jnp.float32)
    grad_mixed = feature_sums(jnp.dot(grad_attn, weight_out.T, preferred_element_type=jnp.float32))
    grad_heads = head_layout(
        grad_mixed.astype(jnp.bfloat16).reshape(batch_seqs, block_len, 1, width_part)
    )[:, :, 0]

    def backward_one(item):
        queries, key_pair, seg_ids, grad_out, log_total = item
        scores = mask_scores(queries, key_pair[:, 0], seg_ids, offset)
        probs_full = jnp.exp(scores - log_total)
        value_heads = key_pair[:, 1].reshape(full_len, head_count, HD)
        key_heads = key_pair[:, 0].reshape(full_len, head_count, HD)
        out_heads = grad_out.reshape(query_len, head_count, HD)
        grad_probs = jnp.einsum(
            "qhd,khd->hqk", out_heads, value_heads, preferred_element_type=jnp.float32
        )
        row_delta = jnp.sum(probs_full * grad_probs, axis=-1, keepdims=True)
        grad_scores = (probs_full * (grad_probs - row_delta)).astype(jnp.bfloat16)
        grad_query = (
            jnp.einsum("hqk,khd->qhd", grad_scores, key_heads, preferred_element_type=jnp.float32)
            * score_scale
        )
        outputs = (grad_query.reshape(query_len, D).astype(jnp.bfloat16), row_delta)
        return outputs + (grad_scores, probs_full.astype(jnp.bfloat16))

    query_part = qkv_heads[:, :, 0]
    grad_queries, row_deltas, scores_all, probs_all = lax.map(
        lambda item: backward_one(item), (query_part, keys_both, segments, grad_heads, log_totals)
    )
    query_heads = query_part.reshape(batch_seqs, query_len, head_count, HD)
    out_heads_all = grad_heads.reshape(batch_seqs, query_len, head_count, HD)
    key_grad = (
        jnp.einsum("shqk,sqhd->kshd", scores_all, query_heads, preferred_element_type=jnp.float32)
        * score_scale
    )
    value_grad = jnp.einsum(
        "shqk,sqhd->kshd", probs_all, out_heads_all, preferred_element_type=jnp.float32
    )
    key_sums = lax.psum_scatter(
        jnp.stack((key_grad, value_grad), axis=1).reshape(
            query_len * lax.axis_size(("row", "col")), 2, batch_seqs, D
        ),
        ("row", "col"),
        scatter_dimension=0,
        tiled=True,
    ).astype(jnp.bfloat16)
    key_sums = jnp.transpose(key_sums, (2, 1, 0, 3))
    grad_qkv_heads = jnp.stack((grad_queries, key_sums[:, 0], key_sums[:, 1]), axis=2)
    grad_qkv = token_layout(grad_qkv_heads).reshape(row_total, 3 * width_part)
    part_qkv = jnp.dot(rows_one.T, grad_qkv, preferred_element_type=jnp.float32)
    grad_one = feature_sums(jnp.dot(grad_qkv, weight_qkv.T, preferred_element_type=jnp.float32))
    grad_input = grad_middle + norm_backward(grad_one, normed_one, recip_one, first_gain)
    gradient_tokens = grad_input.astype(jnp.bfloat16).reshape(batch_seqs, block_len, width_part)
    qkv_sums = jnp.sum(grad_qkv.reshape(row_total, 3, width_part).astype(jnp.float32), axis=0)
    vectors = lax.psum(
        (
            jnp.sum(grad_one * normed_one, axis=0),
            jnp.sum(grad_one, axis=0),
            jnp.stack((qkv_sums[0], qkv_sums[2])),
            jnp.sum(grad_attn.astype(jnp.float32), axis=0),
            jnp.sum(grad_two * normed_two, axis=0),
            jnp.sum(grad_two, axis=0),
            jnp.sum(grad_pre.astype(jnp.float32), axis=0),
            jnp.sum(grad_float, axis=0),
        ),
        ("dev", "row"),
    )
    shares = (
        lax.psum_scatter(
            part_qkv.astype(jnp.bfloat16), "row", scatter_dimension=0, tiled=True
        ).astype(jnp.float32),
        lax.psum_scatter(
            part_out.astype(jnp.bfloat16), "row", scatter_dimension=0, tiled=True
        ).astype(jnp.float32),
        lax.psum_scatter(
            part_expand.astype(jnp.bfloat16), "row", scatter_dimension=0, tiled=True
        ).astype(jnp.float32),
        lax.psum_scatter(
            part_contract.astype(jnp.bfloat16), "row", scatter_dimension=0, tiled=True
        ).astype(jnp.float32),
    )
    summed = (
        lax.psum(shares[0].astype(jnp.bfloat16), "dev").astype(jnp.float32),
        lax.psum(shares[1].astype(jnp.bfloat16), "dev").astype(jnp.float32),
        lax.psum(shares[2].astype(jnp.bfloat16), "dev").astype(jnp.float32),
        lax.psum(shares[3].astype(jnp.bfloat16), "dev").astype(jnp.float32),
    )
    grad_qkv_weight = summed[0].reshape(summed[0].shape[0], 3, width_part)
    return (
        result,
        gradient_tokens,
        vectors[0],
        vectors[1],
        grad_qkv_weight,
        vectors[2],
        summed[1],
        vectors[3],
        vectors[4],
        vectors[5],
        summed[2],
        vectors[6],
        summed[3],
        vectors[7],
    )


def solution(mesh):
    return jax.shard_map(
        per_device,
        mesh=mesh,
        in_specs=(
            P("dev", "row", "col"),
            P("dev", None),
            P("col"),
            P("col"),
            P("row", None, "col"),
            P(None, "col"),
            P("row", "col"),
            P("col"),
            P("col"),
            P("col"),
            P("row", "col"),
            P("col"),
            P("row", "col"),
            P("col"),
            P("dev", "row", "col"),
        ),
        out_specs=(
            P("dev", "row", "col"),
            P("dev", "row", "col"),
            P("col"),
            P("col"),
            P("row", None, "col"),
            P(None, "col"),
            P("row", "col"),
            P("col"),
            P("col"),
            P("col"),
            P("row", "col"),
            P("col"),
            P("row", "col"),
            P("col"),
        ),
        check_vma=False,
    )
```

profile of v0, /device:TPU:0, one launch (start us, length us, event | category | flops | bytes accessed | tf_op | source)
XLA Modules:
  0.0 5767.2 jit_solution(13565483259649066842)
XLA Ops:
  11.2 254.9 %all-gather.15.cloned.1.call-done = bf16[6400,800]{1,0:T(8,128)(2,1)} async-done(((bf16[200,800]{1,0:T(8,128)(2,1)}), bf16[6400,800]{1,0:T(8,128)(2,1)}) %all-gather.15.cloned.1.call-update) | async-done | bytes 10240016 | tf_op jit(solution)/shard_map/all_gather | solution.py:93
  266.2 9.8 convolution_convert_fusion.3
  275.9 5.6 copy.134
  287.1 232.4 %all-gather.9.cloned.1.call-done = bf16[1600,3,800]{2,1,0:T(4,128)(2,1)} async-done(((bf16[50,3,800]{2,1,0:T(4,128)(2,1)}), bf16[1600,3,800]{2,1,0:T(4,128)(2,1)}) %all-gather.9.cloned.1.call-update) | async-done | bytes 7680016 | tf_op jit(solution)/shard_map/all_gather | solution.py:90
  519.5 20.7 copy.110
  540.3 6.7 add_convert_fusion
  552.7 4.8 all_to_all.63
  561.5 118.0 %all-gather.17.cloned.1.call-done = bf16[32,50,800]{2,1,0:T(8,128)(2,1)} async-done(((bf16[1,50,800]{2,1,0:T(8,128)(2,1)}), bf16[32,50,800]{2,1,0:T(8,128)(2,1)}) %all-gather.17.cloned.1.call-update) | async-done | bytes 2560016 | tf_op jit(solution)/shard_map/all_gather | solution.py:91
  679.5 4.8 reshape.347
  685.1 250.9 %all-gather.19.cloned.1.call-done = bf16[32,50,3200]{2,1,0:T(8,128)(2,1)} async-done(((bf16[1,50,3200]{2,1,0:T(8,128)(2,1)}), bf16[32,50,3200]{2,1,0:T(8,128)(2,1)}) %all-gather.19.cloned.1.call-update) | async-done | bytes 10240016 | tf_op jit(solution)/shard_map/all_gather | solution.py:92
  936.0 11.7 reshape.349
  952.8 295.5 %all-gather.11.cloned.1.call-done = bf16[2,4096,2,1600]{3,1,2,0:T(8,128)(2,1)} async-done(((bf16[2,64,2,1600]{3,1,2,0:T(8,128)(2,1)}), bf16[2,4096,2,1600]{3,1,2,0:T(8,128)(2,1)}) %all-gather.11.cloned.1.call-update) | async-done | bytes 52428816 | tf_op jit(solution)/shard_map/all_gather | solution.py:110
  1248.3 68.6 %copy.114 = bf16[2,4096,2,1600]{1,3,2,0:T(8,128)(2,1)} copy(bf16[2,4096,2,1600]{3,1,2,0:T(8,128)(2,1)} %all-gather.11.cloned.1.call-done) | data formatting | bytes 104857600 | tf_op jit(solution)/shard_map/while | solution.py:123
  1317.1 126.9 %while.32 = (s32[]{:T(128)}, bf16[2,64,1600]{1,2,0:T(8,128)(2,1)S(1)}, f32[2,25,64,1]{2,1,3,0:T(8,128)S(1)}, bf16[2,4096,2,1600]{1,3,2,0:T(8,128)(2,1)}, s32[2,4...) while((s32[]{:T(128)}, ...), condition=%wide.region_7.8_spmd, body=%wide.region_4.7_spmd.sunk | while | flops 1750712832 | bytes 212969120 | solution.py:123
  1317.1 12.8 dynamic-slice_bitcast_fusion.10
  1329.9 9.3 fusion.135
  1340.0 14.2 fusion.137
  1354.2 9.8 exponential_reduce_fusion.2
  1364.1 16.4 fusion.139
  1380.5 12.7 dynamic-slice_bitcast_fusion.10
  1393.3 9.3 fusion.135
  1403.5 14.2 fusion.137
  1417.7 9.8 exponential_reduce_fusion.2
  1427.5 16.4 fusion.139
  1444.0 6.8 copy.178
  1468.9 20.6 convert_reduce_fusion.1
  1494.8 11.8 reduce-scatter.17.cloned.1.call-done
  1522.1 6.9 convolution_convert_fusion
  1540.6 213.5 %while.33 = (s32[]{:T(128)}, bf16[2,64,1600]{1,2,0:T(8,128)(2,1)S(1)}, bf16[2,25,64,4096]{3,2,1,0:T(8,128)(2,1)}, bf16[2,25,64,4096]{3,2,1,0:T(8,128)(2,1)}, bf1...) while((s32[]{:T(128)}, ...), condition=%wide.region_21.22_spmd, body=%wide.region_19.21_spmd.sunk | while | flops 2596215296 | bytes 331678656 | solution.py:176
  1540.9 13.5 dynamic-slice_bitcast_fusion.12
  1554.4 9.4 fusion.146
  1564.3 16.9 fusion.147
  1582.1 25.6 multiply_reduce_fusion.3
  1607.6 29.8 bitcast_dynamic-update-slice_fusion.2
  1637.4 10.4 fusion.149
  1647.9 12.7 dynamic-slice_bitcast_fusion.12
  1660.6 9.4 fusion.146
  1670.5 16.9 fusion.147
  1688.3 25.6 multiply_reduce_fusion.3
  1713.9 29.8 bitcast_dynamic-update-slice_fusion.2
  1743.7 10.4 fusion.149
  1754.2 26.1 fusion.83
  1780.3 77.9 %copy.127 = f32[4096,1,2,1600]{3,2,1,0:T(2,128)} copy(f32[4096,1,2,1600]{0,3,2,1:T(8,128)} %bitcast.235) | data formatting | bytes 104857600 | tf_op jit(solution)/shard_map/stack | solution.py:189
  1858.1 25.7 broadcast_multiply_fusion
  1883.8 77.8 %copy.126 = f32[4096,1,2,1600]{3,2,1,0:T(2,128)} copy(f32[4096,1,2,1600]{0,3,2,1:T(8,128)} %bitcast.236) | data formatting | bytes 104857600 | tf_op jit(solution)/shard_map/stack | solution.py:189
  1961.6 73.7 %pad_maximum_fusion = f32[4096,2,2,1600]{3,2,1,0:T(2,128)} fusion(f32[4096,1,2,1600]{3,2,1,0:T(2,128)} %copy.127, f32[4096,1,2,1600]{3,2,1,0:T(2,128)} %copy.126), kind=kLoop, calls=%fused_computation.51 | loop fusion | flops 26214400 | bytes 209715200 | tf_op jit(solution)/shard_map/stack | solution.py:189
  2035.4 9.6 convolution_convert_fusion.1
  2045.1 2563.6 %all-reduce.19 = bf16[4096,2,2,1600]{3,2,1,0:T(2,128)(2,1)} all-reduce(f32[4096,2,2,1600]{3,2,1,0:T(2,128)} %pad_maximum_fusion), channel_id=5, replica_groups=mesh['dev'=2,'row'=32,'col'=2] {'row','col'}, use_global_device_ids=true, to_apply=%region_22.23.clone | all-reduce | flops 26214400 | bytes 157286400
  4615.3 8.3 copy.129
  4626.3 5.8 all_to_all.66
  4634.8 8.5 copy.130
  4644.5 7.0 convolution_convert_fusion.2
  4651.5 565.6 %fusion.74 = (bf16[64,2400]{1,0:T(8,128)(2,1)}, bf16[64,800]{1,0:T(8,128)(2,1)}, bf16[64,3200]{1,0:T(8,128)(2,1)}) fusion(bf16[1600,2400]{1,0:T(8,128)(2,1)} %convolution_convert_fusion.2, bf16[1600,800]{1,0:T(8,128)(2,1)} %convolution_convert_fusion.4, bf16[1600,3200]{1,0:T(8,128)(2,1)} %convolution_convert_fusion), kind=kCustom, calls=%all-reduce-scatter.3 | all-reduce-scatter fusion | flops 13107201 | bytes 21299712
  5225.4 4.7 collective-permute-start.10
  5233.7 4.2 collective-permute-start.8
  5237.9 7.8 convolution_convert_fusion.7
  5261.8 10.3 fusion.44
  5282.7 7.9 collective-permute-start.19
  5295.3 8.2 concatenate.2
  5305.3 5.5 collective-permute-start.17
  5315.6 10.6 collective-permute-start.14
  5326.9 25.2 concatenate.1
  5354.1 31.1 concatenate.3
  5392.0 358.6 %all-reduce.8 = (f32[800]{0:T(1024)}, f32[800]{0:T(1024)}, f32[2,800]{1,0:T(2,128)}, f32[800]{0:T(1024)}, f32[800]{0:T(1024)}, /*index=5*/f32[800]{0:T(1024)}, f32[3200]{0:T(1024)}, f32[800]{0:T(1024)}) all-reduce(f32[800]{0:T(1024)S(1)} %get-tuple-element.489, ...), channel_id=1, replica_groups=mesh['dev'=2,'row'=32,'col'=2] {'dev','row'}, use_global_device_ids=true, to_apply=%region_29.30 | all-reduce | flops 9600 | bytes 76800 | tf_op jit(solution)/shard_map/psum | solution.py:204
  (294 shorter events, 159.8 us)
Async XLA Ops:
  7.2 259.0 %all-gather.15.cloned.1.call-start = ((), (), s32[]{:S(2)}) async-start(), calls=%async_computation.12 | async-start | bytes 11827200 | tf_op jit(solution)/shard_map/all_gather | solution.py:93
  7.9 511.6 %all-gather.9.cloned.1.call-start = ((), (), s32[]{:S(2)}) async-start(), calls=%async_computation.9 | async-start | bytes 11827200 | tf_op jit(solution)/shard_map/all_gather | solution.py:90
  9.8 669.7 %all-gather.17.cloned.1.call-start = ((), (), s32[]{:S(2)}) async-start(), calls=%async_computation.16 | async-start | bytes 3311616 | tf_op jit(solution)/shard_map/all_gather | solution.py:91
  10.6 925.5 %all-gather.19.cloned.1.call-start = ((), (), s32[]{:S(2)}) async-start(), calls=%async_computation.17 | async-start | bytes 11827200 | tf_op jit(solution)/shard_map/all_gather | solution.py:92
  11.1 270.5 %copy-start.4 = (bf16[2,128,800]{1,2,0:T(8,128)(2,1)S(1)}, bf16[2,128,800]{1,2,0:T(8,128)(2,1)}, u32[]{:S(2)}) copy-start(bf16[2,128,800]{1,2,0:T(8,128)(2,1)} %param.19) | copy-start | bytes 1228804
  11.1 273.1 %copy-start.33 = (f32[800]{0:T(1024)S(1)}, f32[800]{0:T(1024)}, u32[]{:S(2)}) copy-start(f32[800]{0:T(1024)} %param.21) | copy-start | bytes 9604
  11.2 273.1 %copy-start.44 = (f32[800]{0:T(1024)S(1)}, f32[800]{0:T(1024)}, u32[]{:S(2)}) copy-start(f32[800]{0:T(1024)} %param.22) | copy-start | bytes 9604
  11.2 937.9 %reduce-scatter.23.cloned.1.call-start = ((), (), s32[]{:S(2)}) async-start(), calls=%async_computation.18 | async-start | bytes 4915200
  281.5 966.8 %all-gather.11.cloned.1.call-start = ((), (), s32[]{:S(2)}) async-start(), calls=%async_computation.10 | async-start | bytes 55377920 | tf_op jit(solution)/shard_map/all_gather | solution.py:110
  287.0 260.0 %copy-start.10 = (bf16[256,1600]{0,1:T(8,128)(2,1)}, bf16[256,1600]{0,1:T(8,128)(2,1)S(1)}, u32[]{:S(2)}) copy-start(bf16[256,1600]{0,1:T(8,128)(2,1)S(1)} %all_gather.27) | copy-start | bytes 2457604
  561.2 945.5 %reduce-scatter.17.cloned.1.call-start = ((), (), s32[]{:S(2)}) async-start(), calls=%async_computation.13 | async-start | bytes 1228800 | tf_op jit(solution)/shard_map/reduce_scatter | solution.py:19
  952.8 364.2 %copy-start.19 = (s32[2,4096]{1,0:T(2,128)S(1)}, s32[2,4096]{1,0:T(2,128)}, u32[]{:S(2)}) copy-start(s32[2,4096]{1,0:T(2,128)} %param.20) | copy-start | bytes 98308
  1317.0 143.1 %copy-start.5 = (bf16[2,128,800]{1,2,0:T(8,128)(2,1)S(1)}, bf16[2,128,800]{1,2,0:T(8,128)(2,1)}, u32[]{:S(2)}) copy-start(bf16[2,128,800]{1,2,0:T(8,128)(2,1)} %param.19) | copy-start | bytes 1228804
  1317.1 143.1 %copy-start.48 = (f32[800]{0:T(1024)S(1)}, f32[800]{0:T(1024)}, u32[]{:S(2)}) copy-start(f32[800]{0:T(1024)} %param.26) | copy-start | bytes 9604
  1444.0 24.9 copy-start.47
  1463.6 47.7 copy-start
  1466.4 24.3 slice-start
  1494.7 22.8 copy-start.46
  1494.7 23.4 copy-start.50
  1494.7 37.0 reduce-scatter.19.cloned.1.call-start
  1517.4 517.9 %all-gather.13.cloned.1.call-start = ((), (), s32[]{:S(2)}) async-start(), calls=%async_computation.11 | async-start | bytes 4915200 | tf_op jit(solution)/shard_map/all_gather | solution.py:15
  1529.1 3858.0 %reduce-scatter.25.cloned.1.call-start = ((), (), s32[]{:S(2)}) async-start(), calls=%async_computation.19 | async-start | bytes 11827200
  1540.6 213.5 %copy-start.9 = (bf16[2,64,1,2,800]{1,4,3,0,2:T(8,128)(2,1)S(1)}, bf16[2,64,1,2,800]{1,4,3,0,2:T(8,128)(2,1)}, u32[]{:S(2)}) copy-start(bf16[2,64,1,2,800]{1,4,3,0,2:T(8,128)(2,1)} %copy.125) | copy-start | bytes 1228804
  1754.1 26.1 copy-start.14
  1780.3 77.9 %copy-start.8 = (bf16[2,64,1,1600]{1,3,0,2:T(8,128)(2,1)S(1)}, bf16[2,64,1,1600]{1,3,0,2:T(8,128)(2,1)}, u32[]{:S(2)}) copy-start(bf16[2,64,1,1600]{1,3,0,2:T(8,128)(2,1)} %copy.124) | copy-start | bytes 1228804
  1961.6 73.7 %copy-start.12 = (bf16[2,128,800]{1,2,0:T(8,128)(2,1)S(1)}, bf16[2,128,800]{1,2,0:T(8,128)(2,1)}, u32[]{:S(2)}) copy-start(bf16[2,128,800]{1,2,0:T(8,128)(2,1)} %param.33) | copy-start | bytes 1228804
  2045.0 2563.7 %copy-start.15 = (bf16[2,64,1600]{1,2,0:T(8,128)(2,1)S(1)}, bf16[2,64,1600]{1,2,0:T(8,128)(2,1)}, u32[]{:S(2)}) copy-start(bf16[2,64,1600]{1,2,0:T(8,128)(2,1)} %copy-done.14) | copy-start | bytes 1228804
  2045.0 3342.9 %reduce-scatter.21.cloned.1.call-start = ((), (), s32[]{:S(2)}) async-start(), calls=%async_computation.15 | async-start | bytes 1228800 | tf_op jit(solution)/shard_map/reduce_scatter | solution.py:19
  5217.1 44.7 copy-start.1
  5217.1 44.7 copy-start.49
  5218.1 15.6 collective-permute-start.13
  5220.3 27.3 collective-permute-start.12
  5221.6 28.6 collective-permute-start.11
  5225.4 27.4 collective-permute-start.10
  5230.1 26.9 collective-permute-start.9
  5233.7 24.6 collective-permute-start.8
  5245.7 26.5 copy-start.13
  5247.5 505.2 %all-reduce.18.cloned.1.call-start = ((), (), s32[]{:S(2)}) async-start(), calls=%async_computation.20 | async-start | bytes 2351104 | tf_op jit(solution)/shard_map/psum | solution.py:232
  5247.6 31.5 collective-permute-start.5
  5250.2 32.5 collective-permute-start.4
  5252.9 37.7 collective-permute-start.3
  5257.0 16.0 collective-permute-start.7
  5258.3 16.7 collective-permute-start.6
  5272.1 115.8 %copy-start.6 = (bf16[2,128,800]{1,2,0:T(8,128)(2,1)S(1)}, bf16[2,128,800]{1,2,0:T(8,128)(2,1)}, u32[]{:S(2)}) copy-start(bf16[2,128,800]{1,2,0:T(8,128)(2,1)} %param.19) | copy-start | bytes 1228804
  5272.1 115.8 %copy-start.34 = (f32[800]{0:T(1024)S(1)}, f32[800]{0:T(1024)}, u32[]{:S(2)}) copy-start(f32[800]{0:T(1024)} %param.21) | copy-start | bytes 9604
  5272.1 115.8 %copy-start.36 = (f32[256]{0:T(256)S(1)}, f32[256]{0:T(256)}, u32[]{:S(2)}) copy-start(f32[256]{0:T(256)} %copy-done.35) | copy-start | bytes 3076
  5272.1 115.8 %copy-start.38 = (f32[256]{0:T(256)S(1)}, f32[256]{0:T(256)}, u32[]{:S(2)}) copy-start(f32[256]{0:T(256)} %copy-done.37) | copy-start | bytes 3076
  5272.2 119.8 %copy-start.39 = (f32[800]{0:T(1024)S(1)}, f32[800]{0:T(1024)}, u32[]{:S(2)}) copy-start(f32[800]{0:T(1024)} %get-tuple-element.487) | copy-start | bytes 9604
  5272.2 119.8 %copy-start.40 = (f32[800]{0:T(1024)S(1)}, f32[800]{0:T(1024)}, u32[]{:S(2)}) copy-start(f32[800]{0:T(1024)} %get-tuple-element.495) | copy-start | bytes 9604
  5272.2 119.8 %copy-start.41 = (f32[800]{0:T(1024)S(1)}, f32[800]{0:T(1024)}, u32[]{:S(2)}) copy-start(f32[800]{0:T(1024)} %get-tuple-element.567) | copy-start | bytes 9604
  5272.2 119.8 %copy-start.42 = (f32[3200]{0:T(1024)S(1)}, f32[3200]{0:T(1024)}, u32[]{:S(2)}) copy-start(f32[3200]{0:T(1024)} %get-tuple-element.565) | copy-start | bytes 38404
  5272.2 478.4 %copy-start.3 = (f32[256,800]{0,1:T(8,128)S(1)}, f32[256,800]{0,1:T(8,128)}, u32[]{:S(2)}) copy-start(f32[256,800]{0,1:T(8,128)} %copy-done.2) | copy-start | bytes 2457604
  5273.0 22.2 copy-start.31
  5273.0 30.4 collective-permute-start.2
  5275.1 30.3 collective-permute-start.1
  5279.1 31.8 collective-permute-start
  5282.7 33.0 collective-permute-start.19
  5290.6 22.4 collective-permute-start.20
  5295.3 91.9 %copy-start.21 = (bf16[100,2,8,128]{3,2,1,0:T(8,128)(2,1)S(1)}, bf16[100,2,8,128]{3,2,1,0:T(8,128)(2,1)}, u32[]{:S(2)}) copy-start(bf16[100,2,8,128]{3,2,1,0:T(8,128)(2,1)} %fusion.44) | copy-start | bytes 1228804
  5303.5 50.6 collective-permute-start.18
  5305.3 48.8 collective-permute-start.17
  5310.9 43.2 collective-permute-start.16
  5312.9 41.2 collective-permute-start.15
  5315.6 38.5 collective-permute-start.14
  (24 other events, 326.9 us)
Sparse Core Ops, SparseCore 0:
  9.7 256.4 all-gather.14
  268.4 251.1 all-gather.8
  521.2 158.2 all-gather.16
  681.0 254.9 all-gather.18
  938.2 10.8 reduce-scatter.22
  950.7 297.5 all-gather.10
  1494.9 11.7 reduce-scatter.16
  1517.5 12.2 reduce-scatter.18
  1531.6 16.4 all-gather.12
  2045.2 489.2 reduce-scatter.24
  5247.7 8.2 reduce-scatter.20
  5387.2 65.6 all-reduce.17
where the time goes:
time: 5790 us; the launch traced here: 5770 us
  blocking collectives  3520 us (61%)
  waiting for transfers between devices  1170 us (20%)
  local copies, waits for them, and re-layouts  496 us (9%)
  matrix products  312 us (5%)
  other arithmetic  172 us (3%)
  starting transfers between devices  78.4 us (1%)
    unnamed x2, blocking collectives  3130 us
    psum x1, blocking collectives, per_device(): lax.psum((jnp.sum(grad_one * normed_one, axis=0), jnp.sum(grad_one, axis=...  359 us
    all_gather x1, waiting for transfers between devices, per_device(): lax.all_gather(qkv_heads[:, :, 1:], ('row', 'col'), axis=1, tiled=True)  295 us
    all_gather x1, waiting for transfers between devices, per_device(): lax.all_gather(contract_weight, 'row', axis=0, tiled=True)  255 us
    all_gather x1, waiting for transfers between devices, per_device(): lax.all_gather(expand_weight, 'row', axis=0, tiled=True)  251 us
    all_gather x1, waiting for transfers between devices, per_device(): lax.all_gather(attention_in, 'row', axis=0, tiled=True)  232 us
    another operation x2, local copies, waits for them, and re-layouts, per_device(): jnp.stack((key_grad, value_grad), axis=1)  156 us
    all_gather x1, waiting for transfers between devices, per_device(): lax.all_gather(attention_out, 'row', axis=0, tiled=True)  118 us
  transfers between devices with their start and end apart: 33, of which 7 were waited for; matrix products, arithmetic and copies ran while one was open for 22% of the time, Pallas kernels for 0%

commit v1 on v0

v1 whole, which is shorter than its diff:
```python
import functools

import jax
import jax.numpy as jnp
from jax import lax
from jax.experimental import pallas as pl
from jax.experimental.pallas import tpu as pltpu
from jax.sharding import PartitionSpec as P

MESH = pl.DeviceIdType.MESH


def coords():
    d=lax.axis_index("dev"); r=lax.axis_index("row"); c=lax.axis_index("col")
    return r//8, (r//2)%4, d*2+r%2, c
def place(z,y,x,c):
    return (x//2, (z*4+y)*2+x%2, c)
SPLIT={"q":(4,4,6,5),"o":(2,1,2,2),"e":(7,4,7,7),"c":(1,2,2,2)}
ORD=("yzx","zyx","yxz","zxy")
def cuts(name,W):
    out=[];p=0
    for n in SPLIT[name]:
        out.append((p,min(p+n*128,W))); p+=n*128
    assert out[-1][1]==W,(name,out)
    return out
def gather_kernel(names,widths,*refs):
    n=len(names)
    src=refs[:n]; dst=refs[n:2*n]; ss,rs,ls=refs[2*n:]
    z,y,x,c=coords(); xl=x%2
    def peer(ax,k):
        zz,yy,xx=z,y,x
        if ax=="z": zz=(z+k)%4
        if ax=="y": yy=(y+k)%4
        if ax=="x": xx=(x+k)%4
        return place(zz,yy,xx,c)
    peers=[("z",1),("z",3),("z",2),("y",1),("y",3),("y",2),("x",1),("x",3)]
    bar=pltpu.get_barrier_semaphore()
    for ax,k in peers: pl.semaphore_signal(bar,inc=1,device_id=peer(ax,k),device_id_type=MESH)
    pl.semaphore_wait(bar,len(peers))
    cnt=[0]; allc=[]
    FULL=slice(None)
    LO=pl.ds(0,2); HI=pl.ds(2,2)
    def send(s,d,ax,k):
        i=cnt[0]; cnt[0]+=1
        cp=pltpu.make_async_remote_copy(src_ref=s,dst_ref=d,send_sem=ss.at[i],recv_sem=rs.at[i],device_id=peer(ax,k),device_id_type=MESH)
        cp.start(); allc.append(cp); return cp
    cut=[cuts(nm,w) for nm,w in zip(names,widths)]
    def at(t,p,zi,yi,xi):
        a,b=cut[t][p]
        return dst[t].at[zi,yi,xi,:,pl.ds(a,b-a)]
    def wait(l):
        for cp in l: cp.wait_recv()
    loc=[]
    st1=[[],[],[],[]]
    for t in range(n):
        cp=pltpu.make_async_copy(src[t],dst[t].at[z,y,xl],ls.at[t]); cp.start(); loc.append(cp)
    for t in range(n):
        for p in range(4):
            a,b=cut[t][p]
            for k in (1,3,2):
                st1[p].append(send(src[t].at[:,pl.ds(a,b-a)],at(t,p,z,y,xl),ORD[p][0],k))
    def both(p,f):
        return [cp for t in range(n) for cp in f(t,p)]
    def xsend(zi,yi):
        return lambda t,p:[send(at(t,p,*zi,xl),at(t,p,*zi,xl),"x",1),send(at(t,p,*yi,xl),at(t,p,*yi,xl),"x",3)]
    def ring_a(ax,zi,yi,xi):
        return lambda t,p:[send(at(t,p,zi,yi,xi),at(t,p,zi,yi,xi),ax,k) for k in (1,3)]
    def ring_b(ax,xi):
        def f(t,p):
            if ax=="z":
                u=at(t,p,(z+3)%4,LO,xi); v=at(t,p,(z+1)%4,HI,xi)
            else:
                u=at(t,p,LO,(y+3)%4,xi); v=at(t,p,HI,(y+1)%4,xi)
            return [send(u,u,ax,1),send(v,v,ax,3)]
        return f
    for cp in loc: cp.wait()
    wait(st1[0]); A2=both(0,ring_a("z",z,FULL,xl))
    wait(st1[1]); B2=both(1,ring_a("y",FULL,y,xl))
    wait(st1[2]); C2=both(2,xsend((z,LO),(z,HI)))
    wait(st1[3]); D2=both(3,xsend((LO,y),(HI,y)))
    wait(A2); A2=both(0,ring_b("z",xl))
    wait(B2); B2=both(1,ring_b("y",xl))
    wait(C2); C3=both(2,ring_a("z",z,FULL,FULL))
    wait(D2); D3=both(3,ring_a("y",FULL,y,FULL))
    wait(A2); A3=both(0,xsend((LO,FULL),(HI,FULL)))
    wait(B2); B3=both(1,xsend((LO,FULL),(HI,FULL)))
    wait(C3); C3=both(2,ring_b("z",FULL))
    wait(D3); D3=both(3,ring_b("y",FULL))
    wait(A3);wait(B3);wait(C3);wait(D3)
    for cp in allc: cp.wait_send()
def gather(names,arrs,cid=0):
    n=len(names)
    nd=36*n
    return pl.pallas_call(functools.partial(gather_kernel,names,[a.shape[1] for a in arrs]),
      out_shape=tuple(jax.ShapeDtypeStruct((4,4,2)+a.shape,a.dtype) for a in arrs),
      in_specs=[pl.BlockSpec(memory_space=pl.ANY)]*n,out_specs=tuple([pl.BlockSpec(memory_space=pl.ANY)]*n),
      scratch_shapes=[pltpu.SemaphoreType.DMA((nd,)),pltpu.SemaphoreType.DMA((nd,)),pltpu.SemaphoreType.DMA((n,))],
      compiler_params=pltpu.CompilerParams(collective_id=cid,has_side_effects=True))(*arrs)


RSPLIT={"q":(6,7,6),"o":(2,3,2),"e":(10,7,8),"c":(2,3,2)}
AX=("xzy","yzx","zyx")
def rcuts(name,W):
    out=[];p=0
    for n in RSPLIT[name]:
        out.append((p,min(p+n*128,W))); p+=n*128
    assert out[-1][1]==W,(name,out)
    return out
def rs_kernel(names,widths,hasvec,*refs):
    n=len(names)
    it=iter(refs)
    src=[next(it) for _ in range(n)]
    vec=next(it) if hasvec else None
    out=[next(it) for _ in range(n)]
    vout=next(it) if hasvec else None
    bufs=[[ [next(it) for _ in range(14)] for p in range(3)] for t in range(n)]
    vbuf=[next(it) for _ in range(3)] if hasvec else None
    ss,rs,ls=next(it),next(it),next(it)
    z,y,x,c=coords(); xl=x%2; xh=x//2
    me={"x":x,"y":y,"z":z}
    def peer(ax,k):
        zz,yy,xx=z,y,x
        if ax=="z": zz=(z+k)%4
        if ax=="y": yy=(y+k)%4
        if ax=="x": xx=(x+k)%4
        return place(zz,yy,xx,c)
    peers=[(a,k) for a in "xyz" for k in (1,2,3)]
    bar=pltpu.get_barrier_semaphore()
    for ax,k in peers: pl.semaphore_signal(bar,inc=1,device_id=peer(ax,k),device_id_type=MESH)
    cnt=[0]; lcnt=[0]; allc=[]
    def send(s,d,ax,k):
        i=cnt[0]; cnt[0]+=1
        cp=pltpu.make_async_remote_copy(src_ref=s,dst_ref=d,send_sem=ss.at[i],recv_sem=rs.at[i],device_id=peer(ax,k),device_id_type=MESH)
        cp.start(); allc.append(cp); return cp
    def load(s,d):
        i=lcnt[0]; lcnt[0]+=1
        cp=pltpu.make_async_copy(s,d,ls.at[i]); cp.start(); return cp
    cut=[rcuts(nm,w) for nm,w in zip(names,widths)]
    items=[(t,p) for t in range(n) for p in range(3)]
    def D(t,p,k):
        a,b=cut[t][p]
        if p==0:
            h=(b-a)//2
            return src[t].at[:,:,k%2,:,pl.ds(pl.multiple_of(a+(k//2)*h,128),h)]
        if p==1: return src[t].at[:,k,:,:,pl.ds(a,b-a)]
        return src[t].at[k,:,:,:,pl.ds(a,b-a)]
    def Dh(t,p,k,i):
        a,b=cut[t][p]; s=pl.ds(2*i,2)
        if p==0:
            h=(b-a)//2
            return src[t].at[s,:,k%2,:,pl.ds(pl.multiple_of(a+(k//2)*h,128),h)]
        if p==1: return src[t].at[s,k,:,:,pl.ds(a,b-a)]
        return src[t].at[k,s,:,:,pl.ds(a,b-a)]
    ld={}
    for t,p in items:
        own,bp,bm=bufs[t][p][:3]; k=me[AX[p][0]]
        ld[t,p]=[load(Dh(t,p,(k+1)%4,0),bp),load(Dh(t,p,(k+3)%4,1),bm),load(D(t,p,k),own)]
    pl.semaphore_wait(bar,len(peers))
    R={}
    def vsend(st):
        ax="xyz"[st]; b=vbuf[st]
        for k in (1,2,3): R["v",st,k]=send(b.at[me[ax]],b.at[me[ax]],ax,k)
    def vsum(st):
        for k in (1,2,3): R["v",st,k].wait_recv()
        b=vbuf[st]
        return (b[0]+b[1])+(b[2]+b[3])
    if hasvec:
        vbuf[0][pl.ds(x,1)]=vec[...][None]
        vsend(0)
    for t,p in items:
        own,bp,bm,rlp,rlm,rm,rp=bufs[t][p][:7]; ax=AX[p][0]; k=me[ax]
        R[t,p,"a"]=[send(Dh(t,p,(k+2)%4,0),rlp,ax,1),send(Dh(t,p,(k+2)%4,1),rlm,ax,3)]
    for t,p in items:
        own,bp,bm,rlp,rlm,rm,rp=bufs[t][p][:7]; ax=AX[p][0]; k=me[ax]
        R[t,p,"b"]=[send(Dh(t,p,(k+1)%4,1),rm.at[pl.ds(2,2)],ax,1),send(Dh(t,p,(k+3)%4,0),rp.at[pl.ds(0,2)],ax,3)]
    def addin(dst,other,idx):
        cntn,f,g=idx
        def body(i,_):
            dst[f(i)]=(dst[f(i)].astype(jnp.float32)+other[g(i)].astype(jnp.float32)).astype(jnp.bfloat16)
            return 0
        lax.fori_loop(0,cntn,body,0)
    for t,p in items:
        own,bp,bm,rlp,rlm,rm,rp=bufs[t][p][:7]; ax=AX[p][0]
        m=4 if p==0 else 2
        ix=(2*m,lambda i:(i//m,i%m),lambda i:(i//m,i%m))
        ld[t,p][0].wait(); R[t,p,"a"][0].wait_recv(); addin(bp,rlp,ix)
        R[t,p,"b"].append(send(bp,rm.at[pl.ds(0,2)],ax,1))
        ld[t,p][1].wait(); R[t,p,"a"][1].wait_recv(); addin(bm,rlm,ix)
        R[t,p,"b"].append(send(bm,rp.at[pl.ds(2,2)],ax,3))
    if hasvec:
        v=vsum(0); vbuf[1][pl.ds(y,1)]=v[None]; vsend(1)
    f32=lambda a:a.astype(jnp.float32)
    for t,p in items:
        own,bp,bm,rlp,rlm,rm,rp,rl2p,rl2m,rm2,rp2,out2,r3,_=bufs[t][p]
        m=4 if p==0 else 2; hm=m//2
        ld[t,p][2].wait()
        for cp in R[t,p,"b"]: cp.wait_recv()
        def body(i,_):
            j=(i//m,i%m)
            own[j]=(f32(own[j])+(f32(rm[j])+f32(rp[j]))).astype(jnp.bfloat16)
            return 0
        lax.fori_loop(0,4*m,body,0)
        ax=AX[p][1]; k=me[ax]
        L=pl.ds(0,hm); H=pl.ds(hm,hm)
        R[t,p,"c"]=[send(own.at[(k+2)%4,L],rl2p,ax,1),send(own.at[(k+2)%4,H],rl2m,ax,3)]
        R[t,p,"d"]=[send(own.at[(k+1)%4,H],rm2.at[H],ax,1),send(own.at[(k+3)%4,L],rp2.at[L],ax,3)]
    for t,p in items:
        own,bp,bm,rlp,rlm,rm,rp,rl2p,rl2m,rm2,rp2,out2,r3,_=bufs[t][p]
        m=4 if p==0 else 2; hm=m//2
        ax=AX[p][1]; k=me[ax]
        L=pl.ds(0,hm); H=pl.ds(hm,hm)
        R[t,p,"c"][0].wait_recv()
        addin(own,rl2p,(hm,lambda i:((k+1)%4,i),lambda i:i))
        R[t,p,"d"].append(send(own.at[(k+1)%4,L],rm2.at[L],ax,1))
        R[t,p,"c"][1].wait_recv()
        addin(own,rl2m,(hm,lambda i:((k+3)%4,hm+i),lambda i:i))
        R[t,p,"d"].append(send(own.at[(k+3)%4,H],rp2.at[H],ax,3))
    if hasvec:
        v=vsum(1); vbuf[2][pl.ds(z,1)]=v[None]; vsend(2)
    for t,p in items:
        own,bp,bm,rlp,rlm,rm,rp,rl2p,rl2m,rm2,rp2,out2,r3,_=bufs[t][p]
        m=4 if p==0 else 2
        k=me[AX[p][1]]
        for cp in R[t,p,"d"]: cp.wait_recv()
        def body(i,_):
            out2[i]=(f32(own[k,i])+(f32(rm2[i])+f32(rp2[i]))).astype(jnp.bfloat16)
            return 0
        lax.fori_loop(0,m,body,0)
        ax=AX[p][2]; k=me[ax]
        if p==0:
            R[t,p,"e"]=[send(out2.at[(k+j)%4],r3.at[j-1],ax,j) for j in (1,2,3)]
        else:
            R[t,p,"e"]=[send(out2.at[(k+j)%2],r3.at[j-1],ax,j) for j in (1,2,3)]
    for t,p in sorted(items,key=lambda q:q[1]):
        own,bp,bm,rlp,rlm,rm,rp,rl2p,rl2m,rm2,rp2,out2,r3,r4=bufs[t][p]
        a,b=cut[t][p]
        for cp in R[t,p,"e"]: cp.wait_recv()
        k=me[AX[p][2]] if p==0 else xl
        s=(f32(out2[k])+f32(r3[1]))+(f32(r3[0])+f32(r3[2]))
        if p==0:
            h=(b-a)//2
            s=s.astype(jnp.bfloat16)
            r4[xh]=s
            R[t,p,"f"]=[send(r4.at[xh],r4.at[xh],"x",2)]
        else:
            out[t][:,pl.ds(a,b-a)]=s
    for t in range(n):
        a,b=cut[t][0]; h=(b-a)//2; r4=bufs[t][0][13]
        R[t,0,"f"][0].wait_recv()
        for j in range(2): out[t][:,pl.ds(a+j*h,h)]=f32(r4[j])
    if hasvec: vout[...]=vsum(2)
    for cp in allc: cp.wait_send()
def reduce_scatter(names,parts,vec=None,cid=2):
    n=len(names); widths=[a.shape[4] for a in parts]; rows=[a.shape[3] for a in parts]
    scr=[]
    for nm,w,r in zip(names,widths,rows):
        for p,(a,b) in enumerate(rcuts(nm,w)):
            m=4 if p==0 else 2; v=(b-a)//2 if p==0 else b-a; hm=m//2
            B=lambda *s:pltpu.VMEM(s+(r,v),jnp.bfloat16)
            scr+=[B(4,m),B(2,m),B(2,m),B(2,m),B(2,m),B(4,m),B(4,m),B(hm),B(hm),B(m),B(m),B(m),B(3),B(2) if p==0 else pltpu.VMEM((8,128),jnp.bfloat16)]
    hv=vec is not None
    if hv: scr+=[pltpu.VMEM((4,)+vec.shape,jnp.float32)]*3
    nd=15*3*n+n+9
    scr+=[pltpu.SemaphoreType.DMA((nd,)),pltpu.SemaphoreType.DMA((nd,)),pltpu.SemaphoreType.DMA((9*n,))]
    A=pl.BlockSpec(memory_space=pl.ANY); V=pl.BlockSpec(memory_space=pltpu.VMEM)
    return pl.pallas_call(functools.partial(rs_kernel,names,widths,hv),
      out_shape=tuple(jax.ShapeDtypeStruct((r,w),jnp.float32) for r,w in zip(rows,widths))+((jax.ShapeDtypeStruct(vec.shape,jnp.float32),) if hv else ()),
      in_specs=[A]*n+[V]*hv,out_specs=tuple([V]*(n+hv)),scratch_shapes=scr,
      compiler_params=pltpu.CompilerParams(collective_id=cid,has_side_effects=True,vmem_limit_bytes=58<<20))(*parts,*([vec] if hv else []))


HD=64; LEN=4096; NEG=-1e30; ROWS=32
FQ,FK,BQ,BK=1024,1024,512,512
def dot(a,b): return lax.dot_general(a,b,(((1,),(0,)),((),())),preferred_element_type=jnp.float32)
def dot_nt(a,b): return lax.dot_general(a,b,(((1,),(1,)),((),())),preferred_element_type=jnp.float32)
def group_barrier(d,r,c):
    bar=pltpu.get_barrier_semaphore()
    def body(i,_):
        @pl.when(i!=r*2+c)
        def _():
            pl.semaphore_signal(bar,inc=1,device_id=(d,i//2,i%2),device_id_type=MESH)
        return 0
    lax.fori_loop(0,2*ROWS,body,0)
    pl.semaphore_wait(bar,2*ROWS-1)
def push(src,dst,send_sem,recv_sem,same,target):
    @pl.when(same)
    def _():
        pltpu.make_async_copy(src,dst,recv_sem).start()
    @pl.when(jnp.logical_not(same))
    def _():
        pltpu.make_async_remote_copy(src_ref=src,dst_ref=dst,send_sem=send_sem,recv_sem=recv_sem,device_id=target,device_id_type=MESH).start()
def pushed(src,dst,send_sem,recv_sem,same,target):
    @pl.when(jnp.logical_not(same))
    def _():
        pltpu.make_async_remote_copy(src_ref=src,dst_ref=dst,send_sem=send_sem,recv_sem=recv_sem,device_id=target,device_id_type=MESH).wait_send()
def arrived(ref,sem):
    pltpu.make_async_copy(ref,ref,sem).wait()
def attn_fwd_kernel(qkv_in,start,o_recv,qkv_out,oT,lse,qkv,knt,obf,s_in,s_out,r_in,r_out,l_sem):
    d=lax.axis_index("dev"); r=lax.axis_index("row"); c=lax.axis_index("col")
    group_barrier(d,r,c)
    lanes=pl.ds(pl.multiple_of(r*128,128),128)
    def full(fn):
        def body(i,_):
            fn(qkv_in.at[i%2,:,i//2+c],qkv.at[:,:,lanes],s_in.at[i],r_in,i==r,(d,i,c))
            return 0
        lax.fori_loop(0,24,body,0)
    def halves(fn):
        rows=pl.ds(pl.multiple_of(32*c,32),32)
        for s in range(2):
            fn(qkv_in.at[s,:,12*(1-c),rows],qkv.at[:,rows,lanes],s_in.at[24+s],r_in,(r==24+s)&(c==0),(d,24+s,0))
    full(push); halves(push)
    item=(r<24)|((c==0)&(r<26))
    head=r//2+13*c; seq=r%2
    def outs(qi,fn):
        def body(i,_):
            rr=qi*(FQ//128)+i//2; cc=i%2
            fn(obf.at[:,pl.ds(pl.multiple_of(rr*128,128),128)],o_recv.at[seq,head],s_out.at[rr*2+cc],r_out,(rr==r)&(cc==c),(d,rr,cc))
            return 0
        lax.fori_loop(0,FQ//64,body,0)
    @pl.when(item)
    def _():
        arrived(qkv,r_in)
        save=pltpu.make_async_copy(qkv,qkv_out,l_sem)
        save.start()
        for a in range(LEN//512):
            sl=pl.ds(a*512,512)
            knt[sl,:]=qkv[1,:,sl].T
        iota=lax.broadcasted_iota(jnp.int32,(FK,FQ),0)
        iotl=lax.broadcasted_iota(jnp.int32,(FK,FQ),1)
        def qloop(qi,_):
            qs=pl.ds(pl.multiple_of(qi*FQ,FQ),FQ)
            q=qkv[0,:,qs]*jnp.bfloat16(0.125)
            st=start[:,qs]
            def step(kj,carry,diag):
                m,l,acc=carry
                ks=pl.ds(pl.multiple_of(kj*FK,FK),FK)
                s=dot(knt[ks,:],q)
                ok=iota>=(st-kj*FK)
                if diag: ok=ok&(iota<=iotl)
                s=jnp.where(ok,s,NEG)
                mn=jnp.maximum(m,jnp.max(s,axis=0,keepdims=True))
                p=jnp.exp(s-mn)
                al=jnp.exp(m-mn)
                l=l*al+jnp.sum(p,axis=0,keepdims=True)
                acc=acc*al+dot(qkv[2,:,ks],p.astype(jnp.bfloat16))
                return mn,l,acc
            carry=(jnp.full((1,FQ),NEG,jnp.float32),jnp.zeros((1,FQ),jnp.float32),jnp.zeros((HD,FQ),jnp.float32))
            carry=lax.fori_loop(0,qi,lambda kj,cr:step(kj,cr,False),carry)
            m,l,acc=step(qi,carry,True)
            o=acc/l
            oT[:,qs]=o
            lse[:,qs]=m+jnp.log(l)
            obf[:,qs]=o.astype(jnp.bfloat16)
            outs(qi,push)
            return 0
        lax.fori_loop(0,LEN//FQ,qloop,0)
        save.wait()
        for qi in range(LEN//FQ): outs(qi,pushed)
    full(pushed); halves(pushed)
    arrived(o_recv,r_out)
def attn_bwd_kernel(do_in,qkv,oT,start,lse,d_recv,doT,knt,vnt,dqa,delta,dout,s_in,s_out,r_in,r_out):
    d=lax.axis_index("dev"); r=lax.axis_index("row"); c=lax.axis_index("col")
    group_barrier(d,r,c)
    lanes=pl.ds(pl.multiple_of(r*128,128),128)
    def full(fn):
        def body(i,_):
            fn(do_in.at[i%2,i//2+c],doT.at[:,lanes],s_in.at[i],r_in,i==r,(d,i,c))
            return 0
        lax.fori_loop(0,24,body,0)
    def halves(fn):
        rows=pl.ds(pl.multiple_of(32*c,32),32)
        for s in range(2):
            fn(do_in.at[s,12*(1-c),rows],doT.at[rows,lanes],s_in.at[24+s],r_in,(r==24+s)&(c==0),(d,24+s,0))
    full(push); halves(push)
    item=(r<24)|((c==0)&(r<26))
    def outs(fn):
        @pl.when(r<24)
        def _():
            def body(i,_):
                fn(dout.at[:,:,pl.ds(pl.multiple_of(i*128,128),128)],d_recv.at[:,(r%2)*13+r//2+c],s_out.at[i],r_out,i==r,(d,i,c))
                return 0
            lax.fori_loop(0,ROWS,body,0)
        @pl.when(r>=24)
        def _():
            def body(i,_):
                rr=i//2; cc=i%2
                rows=pl.ds(pl.multiple_of(32*cc,32),32)
                fn(dout.at[:,rows,pl.ds(pl.multiple_of(rr*128,128),128)],d_recv.at[:,(r%2)*13+12*(1-cc),rows],s_out.at[i],r_out,(rr==r)&(cc==c),(d,rr,cc))
                return 0
            lax.fori_loop(0,2*ROWS,body,0)
    @pl.when(item)
    def _():
        for a in range(LEN//512):
            sl=pl.ds(a*512,512)
            knt[sl,:]=qkv[1,:,sl].T
            vnt[sl,:]=qkv[2,:,sl].T
        dqa[...]=jnp.zeros_like(dqa)
        arrived(doT,r_in)
        for a in range(LEN//512):
            sl=pl.ds(a*512,512)
            delta[:,sl]=jnp.sum(oT[:,sl]*doT[:,sl].astype(jnp.float32),axis=0,keepdims=True)
        iota=lax.broadcasted_iota(jnp.int32,(BK,BQ),0)
        iotl=lax.broadcasted_iota(jnp.int32,(BK,BQ),1)
        def kloop(kj,_):
            ks=pl.ds(pl.multiple_of(kj*BK,BK),BK)
            kn=knt[ks,:]; vn=vnt[ks,:]; kT=qkv[1,:,ks]
            def step(qi,carry,diag):
                dk,dv=carry
                qs=pl.ds(pl.multiple_of(qi*BQ,BQ),BQ)
                q=qkv[0,:,qs]*jnp.bfloat16(0.125)
                do=doT[:,qs]
                s=dot(kn,q)
                ok=iota>=(start[:,qs]-kj*BK)
                if diag: ok=ok&(iota<=iotl)
                p=jnp.exp(jnp.where(ok,s,NEG)-lse[:,qs])
                dp=dot(vn,do)
                ds=(p*(dp-delta[:,qs])).astype(jnp.bfloat16)
                dv=dv+dot_nt(do,p.astype(jnp.bfloat16))
                dk=dk+dot_nt(q,ds)
                dqa[:,qs]+=dot(kT,ds)
                return dk,dv
            z=jnp.zeros((HD,BK),jnp.float32)
            carry=step(kj,(z,z),True)
            dk,dv=lax.fori_loop(kj+1,LEN//BQ,lambda qi,cr:step(qi,cr,False),carry)
            dout[1,:,ks]=dk.astype(jnp.bfloat16)
            dout[2,:,ks]=dv.astype(jnp.bfloat16)
            return 0
        lax.fori_loop(0,LEN//BK,kloop,0)
        for a in range(LEN//512):
            sl=pl.ds(a*512,512)
            dout[0,:,sl]=(dqa[:,sl]*0.125).astype(jnp.bfloat16)
        outs(push)
        outs(pushed)
    full(pushed); halves(pushed)
    arrived(d_recv.at[:,pl.ds(0,25)],r_out)
VM=pl.BlockSpec(memory_space=pltpu.VMEM); ANY=pl.BlockSpec(memory_space=pl.ANY)
bf=jnp.bfloat16
def attend(qkv,start,cid=1):
    S=jax.ShapeDtypeStruct
    return pl.pallas_call(attn_fwd_kernel,
      out_shape=(S((2,25,HD,128),bf),S((3,HD,LEN),bf),S((HD,LEN),jnp.float32),S((1,LEN),jnp.float32)),
      in_specs=[VM,VM],out_specs=(ANY,ANY,VM,VM),
      scratch_shapes=[pltpu.VMEM((3,HD,LEN),bf),pltpu.VMEM((LEN,HD),bf),pltpu.VMEM((HD,LEN),bf),
        pltpu.SemaphoreType.DMA((26,)),pltpu.SemaphoreType.DMA((64,)),pltpu.SemaphoreType.DMA,pltpu.SemaphoreType.DMA,pltpu.SemaphoreType.DMA],
      compiler_params=pltpu.CompilerParams(collective_id=cid,has_side_effects=True,vmem_limit_bytes=50<<20))(qkv,start)
def attend_back(do,qkv,oT,start,lse,cid=3):
    S=jax.ShapeDtypeStruct
    return pl.pallas_call(attn_bwd_kernel,
      out_shape=S((3,26,HD,128),bf),
      in_specs=[VM]*5,out_specs=ANY,
      scratch_shapes=[pltpu.VMEM((HD,LEN),bf),pltpu.VMEM((LEN,HD),bf),pltpu.VMEM((LEN,HD),bf),pltpu.VMEM((HD,LEN),jnp.float32),pltpu.VMEM((1,LEN),jnp.float32),pltpu.VMEM((3,HD,LEN),bf),
        pltpu.SemaphoreType.DMA((26,)),pltpu.SemaphoreType.DMA((64,)),pltpu.SemaphoreType.DMA,pltpu.SemaphoreType.DMA],
      compiler_params=pltpu.CompilerParams(collective_id=cid,has_side_effects=True,vmem_limit_bytes=50<<20))(do,qkv,oT,start,lse)


D = 1600
KP = 1792


def width_sums(first_sum, second_sum):
    return lax.psum((first_sum, second_sum), "col")


def full_rows(values):
    return lax.all_gather(values, "col", axis=1, tiled=True)


def norm_forward(values, norm_gain, norm_bias):
    totals = width_sums(jnp.sum(values, axis=1), jnp.sum(values * values, axis=1))
    averages = totals[0] / D
    reciprocal = lax.rsqrt(totals[1] / D - averages * averages + 1e-05)
    normed = (values - averages[:, None]) * reciprocal[:, None]
    return (normed, reciprocal, normed * norm_gain + norm_bias)


def norm_backward(incoming, normed, reciprocal, norm_gain):
    scaled = incoming * norm_gain
    totals = width_sums(jnp.sum(scaled, axis=1), jnp.sum(scaled * normed, axis=1))
    return reciprocal[:, None] * (
        scaled - totals[0][:, None] / D - normed * (totals[1][:, None] / D)
    )


def pad_rows(block):
    return jnp.pad(block, ((0, 6), (0, 0)))


def pad_features(values):
    n = values.shape[0]
    return jnp.pad(values.reshape(n, 32, 50), ((0, 0), (0, 0), (0, 6))).reshape(n, KP)


def feature_sums(values):
    n = values.shape[0]
    values = values.astype(jnp.bfloat16).reshape(n, 32, 56)[:, :, :50].reshape(n, D)
    return lax.psum_scatter(values, "col", scatter_dimension=1, tiled=True).astype(jnp.float32)


def matmul(left, right):
    return jnp.dot(left, right, preferred_element_type=jnp.float32)


def per_device(
    tokens,
    segments,
    first_gain,
    first_bias,
    attention_in,
    attention_bias,
    attention_out,
    output_bias,
    second_gain,
    second_bias,
    expand_weight,
    expand_bias,
    contract_weight,
    contract_bias,
    cotangent,
):
    seqs, block_len, width = tokens.shape
    row_total = seqs * block_len
    row = lax.axis_index("row")
    col = lax.axis_index("col")
    gathered = gather(
        "qoec",
        (
            pad_rows(attention_in.reshape(50, 3 * width)),
            pad_rows(attention_out),
            pad_rows(expand_weight),
            contract_weight,
        ),
        0,
    )
    weight_qkv = gathered[0].reshape(KP, 3 * width)
    weight_out = gathered[1].reshape(KP, width)
    weight_expand = gathered[2].reshape(KP, 4 * width)
    weight_contract = gathered[3].reshape(4 * D, width)

    own_seg = lax.dynamic_index_in_dim(segments, row % 2, 0, keepdims=True)
    positions = jnp.arange(LEN, dtype=jnp.int32)[None]
    before = jnp.concatenate((own_seg[:, :1], own_seg[:, :-1]), axis=1)
    start = lax.cummax(jnp.where(own_seg != before, positions, 0), axis=1)

    float_tokens = tokens.astype(jnp.float32).reshape(row_total, width)
    normed_one, recip_one, hidden_one = norm_forward(float_tokens, first_gain, first_bias)
    rows_one = pad_features(full_rows(hidden_one.astype(jnp.bfloat16)))
    bias_three = jnp.concatenate(
        (attention_bias[0], jnp.zeros_like(attention_bias[0]), attention_bias[1])
    )
    projected = jnp.einsum(
        "dm,snd->smn",
        weight_qkv,
        rows_one.reshape(seqs, block_len, KP),
        preferred_element_type=jnp.float32,
    )
    projected = (projected + bias_three[None, :, None]).astype(jnp.bfloat16)
    projected = projected.reshape(seqs, 3, width, block_len)

    def head_slots(values):
        lead = [(0, 0)] * (values.ndim - 2)
        slots = jnp.where(
            col == 0,
            jnp.pad(values, lead + [(0, 32), (0, 0)]),
            jnp.pad(values, lead + [(32, 0), (0, 0)]),
        )
        return slots.reshape(values.shape[:-2] + (13, HD, block_len))

    attended, qkv_item, out_item, log_totals = attend(head_slots(projected), start, 1)
    rows_attn = jnp.pad(
        attended.reshape(seqs, 32, 50, block_len), ((0, 0), (0, 0), (0, 6), (0, 0))
    ).reshape(seqs, KP, block_len)
    middle = float_tokens + (
        jnp.einsum(
            "sfn,fd->snd", rows_attn, weight_out, preferred_element_type=jnp.float32
        ).reshape(row_total, width)
        + output_bias
    )
    normed_two, recip_two, hidden_two = norm_forward(middle, second_gain, second_bias)
    rows_two = pad_features(full_rows(hidden_two.astype(jnp.bfloat16)))
    pre_gelu = matmul(rows_two, weight_expand) + expand_bias
    gelu_out = jax.nn.gelu(pre_gelu, approximate=True)
    rows_gelu = full_rows(gelu_out.astype(jnp.bfloat16))
    branch_out = matmul(rows_gelu, weight_contract) + contract_bias
    result = (middle + branch_out).astype(jnp.bfloat16).reshape(tokens.shape)

    grad_low = cotangent.reshape(row_total, width)
    grad_float = grad_low.astype(jnp.float32)
    part_contract = matmul(rows_gelu.T, grad_low).astype(jnp.bfloat16)
    grad_gelu = lax.psum_scatter(
        matmul(grad_low, weight_contract.T).astype(jnp.bfloat16),
        "col",
        scatter_dimension=1,
        tiled=True,
    ).astype(jnp.float32)
    gelu_back = jax.vjp(lambda inner: jax.nn.gelu(inner, approximate=True), pre_gelu)[1]
    grad_pre = gelu_back(grad_gelu)[0].astype(jnp.bfloat16)
    part_expand = matmul(rows_two.T, grad_pre).astype(jnp.bfloat16)
    sum_expand, sum_contract = reduce_scatter(
        "ec",
        (part_expand.reshape(4, 4, 2, 56, 4 * width), part_contract.reshape(4, 4, 2, 200, width)),
        None,
        2,
    )
    grad_two = feature_sums(matmul(grad_pre, weight_expand.T))
    grad_middle = grad_float + norm_backward(grad_two, normed_two, recip_two, second_gain)
    grad_attn = grad_middle.astype(jnp.bfloat16)
    part_out = jnp.einsum(
        "sfn,snd->fd",
        rows_attn,
        grad_attn.reshape(seqs, block_len, width),
        preferred_element_type=jnp.float32,
    ).astype(jnp.bfloat16)
    grad_mixed = jnp.einsum(
        "snd,fd->sfn",
        grad_attn.reshape(seqs, block_len, width),
        weight_out,
        preferred_element_type=jnp.float32,
    ).astype(jnp.bfloat16)
    grad_mixed = grad_mixed.reshape(seqs, 32, 56, block_len)[:, :, :50].reshape(seqs, D, block_len)
    grad_mixed = lax.psum_scatter(grad_mixed, "col", scatter_dimension=1, tiled=True)
    grad_slots = attend_back(head_slots(grad_mixed), qkv_item, out_item, start, log_totals, 3)
    grad_qkv = lax.dynamic_slice_in_dim(
        grad_slots.reshape(3, seqs, 13 * HD, block_len), 32 * col, width, 2
    )
    grad_rows = jnp.transpose(grad_qkv, (1, 0, 2, 3)).reshape(seqs, 3 * width, block_len)
    part_qkv = jnp.einsum(
        "snd,smn->dm",
        rows_one.reshape(seqs, block_len, KP),
        grad_rows,
        preferred_element_type=jnp.float32,
    ).astype(jnp.bfloat16)
    grad_one = feature_sums(
        jnp.einsum(
            "smn,dm->snd", grad_rows, weight_qkv, preferred_element_type=jnp.float32
        ).reshape(row_total, KP)
    )
    grad_input = grad_middle + norm_backward(grad_one, normed_one, recip_one, first_gain)
    gradient_tokens = grad_input.astype(jnp.bfloat16).reshape(tokens.shape)
    qkv_sums = jnp.sum(grad_qkv.astype(jnp.float32), axis=(1, 3))
    pieces = (
        jnp.sum(grad_one * normed_one, axis=0),
        jnp.sum(grad_one, axis=0),
        qkv_sums[0],
        qkv_sums[2],
        jnp.sum(grad_attn.astype(jnp.float32), axis=0),
        jnp.sum(grad_two * normed_two, axis=0),
        jnp.sum(grad_two, axis=0),
        jnp.sum(grad_pre.astype(jnp.float32), axis=0),
        jnp.sum(grad_float, axis=0),
    )
    vector = jnp.concatenate(pieces + (jnp.zeros((640,), jnp.float32),)).reshape(80, 128)
    sum_qkv, sum_out, vector = reduce_scatter(
        "qo",
        (part_qkv.reshape(4, 4, 2, 56, 3 * width), part_out.reshape(4, 4, 2, 56, width)),
        vector,
        4,
    )
    vector = vector.reshape(-1)
    sums = []
    at = 0
    for piece in pieces:
        sums.append(vector[at : at + piece.shape[0]])
        at += piece.shape[0]
    return (
        result,
        gradient_tokens,
        sums[0],
        sums[1],
        sum_qkv[:50].reshape(50, 3, width),
        jnp.stack((sums[2], sums[3])),
        sum_out[:50],
        sums[4],
        sums[5],
        sums[6],
        sum_expand[:50],
        sums[7],
        sum_contract,
        sums[8],
    )


def solution(mesh):
    return jax.shard_map(
        per_device,
        mesh=mesh,
        in_specs=(
            P("dev", "row", "col"),
            P("dev", None),
            P("col"),
            P("col"),
            P("row", None, "col"),
            P(None, "col"),
            P("row", "col"),
            P("col"),
            P("col"),
            P("col"),
            P("row", "col"),
            P("col"),
            P("row", "col"),
            P("col"),
            P("dev", "row", "col"),
        ),
        out_specs=(
            P("dev", "row", "col"),
            P("dev", "row", "col"),
            P("col"),
            P("col"),
            P("row", None, "col"),
            P(None, "col"),
            P("row", "col"),
            P("col"),
            P("col"),
            P("col"),
            P("row", "col"),
            P("col"),
            P("row", "col"),
            P("col"),
        ),
        check_vma=False,
    )
```

time: 5790 us -> 701 us (0.12)
  blocking collectives: 3520 us -> 16 us
  waiting for transfers between devices: 1170 us -> 17.1 us
  Pallas kernels: 0 us -> 469 us
  local copies, waits for them, and re-layouts: 496 us -> 79.3 us
  matrix products: 312 us -> 84.5 us
  other arithmetic: 172 us -> 11 us
  starting transfers between devices: 78.4 us -> 0.61 us
    unnamed x2 -> x0, blocking collectives: 3130 us -> none
    all_gather x5 -> x0, waiting for transfers between devices: 1150 us -> none  [the longest x1 295 us: per_device(): lax.all_gather(qkv_heads[:, :, 1:], ('row', 'col'), axis=1, tiled=True)]
    pallas_call x0 -> x5, Pallas kernels: none -> 469 us  [the longest x2 181 us: reduce_scatter(): pl.pallas_call(functools.partial(rs_kernel, names, widths, hv), out_shape...]
    psum x1 -> x0, blocking collectives: 359 us -> none  [per_device(): lax.psum((jnp.sum(grad_one * normed_one, axis=0), jnp.sum(grad_one, axis=...]
    dot_general x24 -> x12, matrix products: 312 us -> 84.5 us  [the longest x6 54.4 us: matmul(): return jnp.dot(left, right, preferred_element_type=jnp.float32)]
    another operation x7 -> x6, local copies, waits for them, and re-layouts: 165 us -> 1.49 us  [the longest x2 1.41 us: per_device(): rows_one.reshape(seqs, block_len, KP)]
    unnamed x127 -> x58, local copies, waits for them, and re-layouts: 110 us -> 13.7 us
    unnamed x23 -> x2, starting transfers between devices: 77.8 us -> 0.08 us
  transfers between devices with their start and end apart: 33 -> 5, of which waited for: 7 -> 2; matrix products, arithmetic and copies ran while one was open for 22% -> 16% of each run, Pallas kernels for 0% -> 35%
where the time goes in v1:
time: 701 us; the launch traced here: 693 us
  Pallas kernels  469 us (67%)
  matrix products  84.5 us (12%)
  local copies, waits for them, and re-layouts  79.3 us (11%)
  waiting for transfers between devices  17.1 us (2%)
  blocking collectives  16 us (2%)
  between operations  15.2 us (2%)
  other arithmetic  11 us (2%)
    pallas_call x2, Pallas kernels, reduce_scatter(): pl.pallas_call(functools.partial(rs_kernel, names, widths, hv), out_shape...  181 us
    pallas_call x1, Pallas kernels, gather(): pl.pallas_call(functools.partial(gather_kernel, names, [a.shape[1] for a...  160 us
    pallas_call x1, Pallas kernels, attend_back(): pl.pallas_call(attn_bwd_kernel, out_shape=S((3, 26, HD, 128), bf), in_spe...  72.5 us
    pallas_call x1, Pallas kernels, attend(): pl.pallas_call(attn_fwd_kernel, out_shape=(S((2, 25, HD, 128), bf), S((3,...  55.6 us
    dot_general x6, matrix products, matmul(): return jnp.dot(left, right, preferred_element_type=jnp.float32)  54.4 us
    convert_element_type x1, local copies, waits for them, and re-layouts, per_device(): part_contract = matmul(rows_gelu.T, grad_low).astype(jnp.bfloat16)  15.7 us
  transfers between devices with their start and end apart: 5, of which 2 were waited for; matrix products, arithmetic and copies ran while one was open for 16% of the time, Pallas kernels for 35%

profile of v1, /device:TPU:0, one launch (start us, length us, event | category | flops | bytes accessed | tf_op | source)
XLA Modules:
  0.0 692.8 jit_solution(16108763049613032360)
XLA Ops:
  7.2 1.1 copy.73
  8.7 1.5 pad.41.refs_1_
  10.3 0.7 pad.40.refs_0_
  11.0 1.7 pad.42.refs_2_
  12.8 160.0 %shard_map.254 = (bf16[4,4,2,56,2400]{4,3,2,1,0:T(8,128)(2,1)}, bf16[4,4,2,56,800]{4,3,2,1,0:T(8,128)(2,1)}, bf16[4,4,2,56,3200]{4,3,2,1,0:T(8,128)(2,1)}, bf16[4,4,2,200,800]{4,3,2,1,0:T(8,128)(2,1)}) custom-call(bf16[56,2400]{1,0:T(8,128)(2,1)} %pad.40.refs_0_, bf16[56,800]{1,0:T(8,128)(2,1)} %pad.41.refs_1_, bf16[56,3200]{1,0:T(8,128)(2,1)} %pad.42.refs_2_, ...), custom_call_target="tpu_custom_call" | custom-call | tf_op jit(solution)/shard_map/pallas_call | solution.py:94
  172.8 9.6 %convolution_convert_fusion.2 = bf16[6400,256]{1,0:T(8,128)(2,1)} fusion(bf16[6400,800]{1,0:T(8,128)(2,1)} %bitcast.185, bf16[2,128,800]{1,2,0:T(8,128)(2,1)S(1)} %copy-done.4), kind=kOutput, calls=%fused_computation.3 | convolution fusion | flops 2623078400 | bytes 13926400 | tf_op jit(solution)/shard_map/dot_general | solution.py:500
  182.5 0.7 copy-done.16
  183.7 0.7 compare_select_fusion
  185.3 2.5 all-reduce.14
  188.0 3.1 all_gather.9
  191.7 1.2 copy.74
  193.2 7.4 %fusion = bf16[2,128,2400]{1,2,0:T(8,128)(2,1)S(1)} fusion(bf16[2,128,1792]{2,1,0:T(8,128)(2,1)S(1)} %copy.74, bf16[1792,2400,1]{1,0,2:T(8,128)(2,1)} %bitcast.189, f32[2400]{0:T(1024)S(1)} %concatenate.9), kind=kOutput, calls=%fused_computation.11 | convolution fusion | flops 2203238400 | bytes 10757504 | tf_op jit(solution)/shard_map/dm,snd->smn/dot_general | solution.py:550
  200.8 55.6 %shard_map.255 = (bf16[2,25,64,128]{3,2,1,0:T(8,128)(2,1)S(1)}, bf16[3,64,4096]{2,1,0:T(8,128)(2,1)}, f32[64,4096]{1,0:T(8,128)S(1)}, f32[1,4096]{1,0:T(1,128)S(1)}) custom-call(bf16[2,3,13,64,128]{4,3,2,1,0:T(8,128)(2,1)S(1)} %bitcast.151, s32[1,4096]{1,0:T(1,128)S(1)} %reduce_window_max.19.start), custom_call_target="tpu_custom_call" | custom-call | tf_op jit(solution)/shard_map/pallas_call | solution.py:440
  256.4 0.8 copy.76
  257.5 1.3 copy.78
  258.8 3.6 fusion.43
  262.3 2.5 all-reduce.13
  265.1 2.7 all_gather.10
  267.9 2.1 reshape.208
  270.0 2.2 pad.46
  272.2 3.7 copy.102
  276.0 12.0 %convert_reduce_fusion = (f32[3200]{0:T(1024)S(1)}, bf16[256,3200]{1,0:T(8,128)(2,1)S(1)}, bf16[256,3200]{1,0:T(8,128)(2,1)}) fusion(bf16[256,3200]{1,0:T(8,128)(2,1)} %copy.102, f32[3200]{0:T(1024)S(1)} %copy-done.20, bf16[256,1792]{0,1:T(8,128)(2,1)} %bitcast.161, bf16[1792,3200]{1,0:T(8,128)(2,1)} %bitcast.187), kind=kOutput, calls=%fused_computation.22 | convolution fusion | flops 2957308928 | bytes 17327104 | tf_op jit(solution)/shard_map/dot_general | solution.py:500
  288.0 1.1 copy-done.10
  289.1 8.5 %convolution_convert_fusion.3 = bf16[256,1792]{1,0:T(8,128)(2,1)} fusion(bf16[256,3200]{1,0:T(8,128)(2,1)S(1)} %get-tuple-element.107, bf16[1792,3200]{1,0:T(8,128)(2,1)} %bitcast.188), kind=kOutput, calls=%fused_computation.24 | convolution fusion | flops 2936471552 | bytes 14024704 | tf_op jit(solution)/shard_map/dot_general | solution.py:500
  297.7 2.2 copy.81
  299.9 2.2 reshape.215
  302.1 10.8 %reduce-scatter.6.cloned.1.call-done = bf16[256,800]{0,1:T(8,128)(2,1)} async-done(((bf16[256,1600]{0,1:T(8,128)(2,1)}), bf16[256,800]{0,1:T(8,128)(2,1)}) %reduce-scatter.6.cloned.1.call-update) | async-done | bytes 409616 | tf_op jit(solution)/shard_map/reduce_scatter | solution.py:496
  313.0 1.5 fusion.31
  314.5 2.6 all-reduce.12
  317.1 1.8 convert_reduce_fusion.6
  318.9 3.0 convolution_convert_fusion.5
  321.9 1.7 copy.103
  325.5 1.2 convert_reduce_fusion.5
  326.7 9.2 %convolution_convert_fusion = bf16[1792,3200]{1,0:T(8,128)(2,1)} fusion(bf16[256,1792]{0,1:T(8,128)(2,1)} %bitcast.162, bf16[256,3200]{1,0:T(8,128)(2,1)} %copy-done.10), kind=kOutput, calls=%fused_computation.1 | convolution fusion | flops 2941747200 | bytes 14024704 | tf_op jit(solution)/shard_map/dot_general | solution.py:500
  335.9 2.5 bitcast_convert_fusion.1
  338.4 5.5 copy.92
  343.9 6.2 all-reduce.17.cloned.1.call-done
  350.1 1.3 constant_dynamic-slice_fusion.2
  352.0 72.5 %shard_map.256 = bf16[3,26,64,128]{3,2,1,0:T(8,128)(2,1)S(1)} custom-call(bf16[2,13,64,128]{3,2,1,0:T(8,128)(2,1)S(1)} %bitcast.152, bf16[3,64,4096]{2,1,0:T(8,128)(2,1)} %get-tuple-element.32.qkv, f32[64,4096]{1,0:T(8,128)S(1)} %get-tuple-element.33.oT, s32[1,4096]{1,0:T(1,128)S(1)} %reduce_window_max.19.start, f32[1,4096]{1,0:T(1,128)S(1)} %get-tuple-element.34.lse), custom_call_target="tpu_custom_call" | custom-call | tf_op jit(solution)/shard_map/pallas_call | solution.py:448
  424.6 1.1 copy.86
  425.7 2.4 copy.87
  428.1 7.4 %convolution_convert_fusion.4 = bf16[256,1792]{1,0:T(8,128)(2,1)} fusion(bf16[256,2400]{1,0:T(8,128)(2,1)} %bitcast.168, bf16[1792,2400]{1,0:T(8,128)(2,1)} %bitcast.190), kind=kOutput, calls=%fused_computation.25 | convolution fusion | flops 2202468352 | bytes 10747904 | tf_op jit(solution)/shard_map/smn,dm->snd/dot_general | solution.py:633
  435.5 2.3 copy.88
  437.8 2.1 reshape.223
  439.9 6.3 bitcast_convert_fusion
  446.2 12.5 %copy.90 = bf16[1792,2400]{1,0:T(8,128)(2,1)} copy(bf16[1792,2400]{0,1:T(8,128)(2,1)} %bitcast_convert_fusion) | data formatting | bytes 17203200 | tf_op jit(solution)/shard_map/convert_element_type | solution.py:631
  459.4 9.7 %fusion.14 = bf16[100,2,8,128]{3,2,1,0:T(8,128)(2,1)S(1)} fusion(f32[256,800]{0,1:T(8,128)S(1)} %copy-done.1, bf16[256,6400]{1,0:T(8,128)(2,1)} %all-gather.2.cloned.1.call-done, bf16[6400,800]{1,0:T(8,128)(2,1)} %bitcast.186, f32[800]{0:T(1024)S(1)} %copy-done.22), kind=kOutput, calls=%fused_computation.43 | convolution fusion | flops 2622054400 | bytes 14748800 | tf_op jit(solution)/shard_map/dot_general | solution.py:500
  469.1 0.8 copy.141
  469.9 5.3 convolution_convert_fusion.1
  475.2 15.7 %copy.93 = bf16[6400,800]{1,0:T(8,128)(2,1)} copy(bf16[6400,800]{0,1:T(8,128)(2,1)} %convolution_convert_fusion.1) | data formatting | bytes 20480000 | tf_op jit(solution)/shard_map/convert_element_type | solution.py:588
  490.9 117.3 %shard_map.258 = (f32[56,3200]{1,0:T(8,128)}, f32[200,800]{1,0:T(8,128)}) custom-call(bf16[4,4,2,56,3200]{4,3,2,1,0:T(8,128)(2,1)} %bitcast.153, bf16[4,4,2,200,800]{4,3,2,1,0:T(8,128)(2,1)} %bitcast.154), custom_call_target="tpu_custom_call" | custom-call | tf_op jit(solution)/shard_map/pallas_call | solution.py:266
  608.3 1.6 fusion.32
  609.8 0.7 concatenate.11
  610.5 63.5 %shard_map.257 = (f32[56,2400]{1,0:T(8,128)}, f32[56,800]{1,0:T(8,128)}, f32[80,128]{1,0:T(8,128)}) custom-call(bf16[4,4,2,56,2400]{4,3,2,1,0:T(8,128)(2,1)} %bitcast.155, bf16[4,4,2,56,800]{4,3,2,1,0:T(8,128)(2,1)} %bitcast.158, f32[80,128]{1,0:T(8,128)} %bitcast.176), custom_call_target="tpu_custom_call" | custom-call | tf_op jit(solution)/shard_map/pallas_call | solution.py:266
  674.1 1.4 slice.105
  675.5 1.5 fusion.46
  677.0 2.6 all-reduce.11
  679.6 1.4 reshape.229
  681.1 0.9 copy.96
  681.9 0.6 pad_maximum_fusion
  682.6 1.1 copy_bitcast_fusion
  683.6 0.7 copy.146
  684.3 0.9 copy.147
  685.2 0.9 copy.148
  (94 shorter events, 6.0 us)
Async XLA Ops:
  7.2 165.6 %copy-start.4 = (bf16[2,128,800]{1,2,0:T(8,128)(2,1)S(1)}, bf16[2,128,800]{1,2,0:T(8,128)(2,1)}, u32[]{:S(2)}) copy-start(bf16[2,128,800]{1,2,0:T(8,128)(2,1)} %param.29) | copy-start | bytes 1228804
  7.2 265.0 %reduce-scatter.10.cloned.1.call-start = ((), (), s32[]{:S(2)}) async-start(), calls=%async_computation.6 | async-start | bytes 4915200
  182.4 0.8 copy-start.16
  182.4 2.7 copy-start.2
  182.4 5.3 copy-start.15
  182.4 5.3 copy-start.18
  182.4 130.6 %reduce-scatter.6.cloned.1.call-start = ((), (), s32[]{:S(2)}) async-start(), calls=%async_computation.4 | async-start | bytes 1228800 | tf_op jit(solution)/shard_map/reduce_scatter | solution.py:496
  191.2 1.8 copy-start.17
  192.9 7.6 %copy-start.6 = (bf16[2,128,1792]{2,1,0:T(8,128)(2,1)}, bf16[2,128,1792]{2,1,0:T(8,128)(2,1)S(1)}, u32[]{:S(2)}) copy-start(bf16[2,128,1792]{2,1,0:T(8,128)(2,1)S(1)} %copy.74) | copy-start | bytes 2752516
  256.4 2.4 copy-start.21
  258.8 6.1 copy-start.14
  258.8 6.1 copy-start.19
  262.3 50.7 %copy-start = (f32[256,800]{0,1:T(8,128)}, f32[256,800]{0,1:T(8,128)S(1)}, u32[]{:S(2)}) copy-start(f32[256,800]{0,1:T(8,128)S(1)} %get-tuple-element.123) | copy-start | bytes 2457604
  267.9 8.1 %copy-start.20 = (f32[3200]{0:T(1024)S(1)}, f32[3200]{0:T(1024)}, u32[]{:S(2)}) copy-start(f32[3200]{0:T(1024)} %param.26) | copy-start | bytes 38404
  288.0 1.1 copy-start.10
  302.1 48.0 %all-reduce.17.cloned.1.call-start = ((), (), s32[]{:S(2)}) async-start(), calls=%async_computation.7 | async-start | bytes 1638400
  318.9 5.3 copy-start.23
  323.7 135.6 %all-gather.2.cloned.1.call-start = ((), (), s32[]{:S(2)}) async-start(), calls=%async_computation.3 | async-start | bytes 4915200 | tf_op jit(solution)/shard_map/all_gather | solution.py:465
  325.4 282.8 %reduce-scatter.8.cloned.1.call-start = ((), (), s32[]{:S(2)}) async-start(), calls=%async_computation.5 | async-start | bytes 1228800 | tf_op jit(solution)/shard_map/reduce_scatter | solution.py:496
  435.5 4.4 copy-start.7
  446.2 13.1 %copy-start.1 = (f32[256,800]{0,1:T(8,128)S(1)}, f32[256,800]{0,1:T(8,128)}, u32[]{:S(2)}) copy-start(f32[256,800]{0,1:T(8,128)} %copy-done) | copy-start | bytes 2457604
  446.2 13.1 %copy-start.22 = (f32[800]{0:T(1024)S(1)}, f32[800]{0:T(1024)}, u32[]{:S(2)}) copy-start(f32[800]{0:T(1024)} %param.28) | copy-start | bytes 9604
  459.3 10.6 %copy-start.5 = (bf16[2,128,800]{1,2,0:T(8,128)(2,1)S(1)}, bf16[2,128,800]{1,2,0:T(8,128)(2,1)}, u32[]{:S(2)}) copy-start(bf16[2,128,800]{1,2,0:T(8,128)(2,1)} %param.29) | copy-start | bytes 1228804
  459.4 10.5 %copy-start.8 = (bf16[256,6400]{1,0:T(8,128)(2,1)S(1)}, bf16[256,6400]{1,0:T(8,128)(2,1)}, u32[]{:S(2)}) copy-start(bf16[256,6400]{1,0:T(8,128)(2,1)} %all-gather.2.cloned.1.call-done) | copy-start | bytes 9830404
  490.8 117.4 %copy-start.3 = (bf16[2,128,800]{1,2,0:T(8,128)(2,1)S(1)}, bf16[2,128,800]{1,2,0:T(8,128)(2,1)}, u32[]{:S(2)}) copy-start(bf16[2,128,800]{1,2,0:T(8,128)(2,1)} %param.15) | copy-start | bytes 1228804
  610.5 72.0 %copy-start.9 = (bf16[256,800]{0,1:T(8,128)(2,1)S(1)}, bf16[256,800]{0,1:T(8,128)(2,1)}, u32[]{:S(2)}) copy-start(bf16[256,800]{0,1:T(8,128)(2,1)} %reduce-scatter.8.cloned.1.call-done) | copy-start | bytes 1228804
  674.1 9.6 %copy-start.13 = (f32[56,800]{1,0:T(8,128)S(1)}, f32[56,800]{1,0:T(8,128)}, u32[]{:S(2)}) copy-start(f32[56,800]{1,0:T(8,128)} %get-tuple-element.37) | copy-start | bytes 537604
  677.0 8.2 %copy-start.11 = (f32[200,800]{1,0:T(8,128)S(1)}, f32[200,800]{1,0:T(8,128)}, u32[]{:S(2)}) copy-start(f32[200,800]{1,0:T(8,128)} %get-tuple-element.152) | copy-start | bytes 1920004
  681.1 3.2 copy-start.12
Sparse Core Ops, SparseCore 0:
  182.6 11.9 reduce-scatter.9
  302.2 10.7 reduce-scatter.5
  323.8 26.2 all-reduce.16
  351.7 16.3 all-gather.1
  459.4 11.8 reduce-scatter.7

commit v2 on v1

v2 whole, which is shorter than its diff:
```python
import functools

import jax
import jax.numpy as jnp
from jax import lax
from jax.experimental import pallas as pl
from jax.experimental.pallas import tpu as pltpu
from jax.sharding import PartitionSpec as P

MESH = pl.DeviceIdType.MESH
D = 1600
KP = 1792


def coords():
    d=lax.axis_index("dev"); r=lax.axis_index("row"); c=lax.axis_index("col")
    return r//8, (r//2)%4, d*2+r%2, c
def place(z,y,x,c):
    return (x//2, (z*4+y)*2+x%2, c)
def peer_of(ax,k):
    z,y,x,c=coords()
    if ax=="z": z=(z+k)%4
    if ax=="y": y=(y+k)%4
    if ax=="x": x=(x+k)%4
    return place(z,y,x,c)
def greet(peers):
    bar=pltpu.get_barrier_semaphore()
    for ax,k in peers: pl.semaphore_signal(bar,inc=1,device_id=peer_of(ax,k),device_id_type=MESH)
    pl.semaphore_wait(bar,len(peers))
SPLIT={"q":(4,4,6,5),"o":(2,1,2,2),"e":(7,4,7,7),"c":(1,2,2,2)}
ORD=("yzx","zyx","yxz","zxy")
GPEERS=[("z",1),("z",3),("z",2),("y",1),("y",3),("y",2),("x",1),("x",3)]
def cuts(name,W):
    out=[];p=0
    for n in SPLIT[name]:
        out.append((p,min(p+n*128,W))); p+=n*128
    assert out[-1][1]==W,(name,out)
    return out
def gather_steps(names,widths,src,dst,ss,rs,ls):
    n=len(names)
    z,y,x,c=coords(); xl=x%2
    cnt=[0]; allc=[]
    FULL=slice(None)
    LO=pl.ds(0,2); HI=pl.ds(2,2)
    def mk(s,d,ax,k):
        i=cnt[0]; cnt[0]+=1
        cp=pltpu.make_async_remote_copy(src_ref=s,dst_ref=d,send_sem=ss.at[i],recv_sem=rs.at[i],device_id=peer_of(ax,k),device_id_type=MESH)
        allc.append(cp); return cp
    cut=[cuts(nm,w) for nm,w in zip(names,widths)]
    def at(t,p,zi,yi,xi):
        a,b=cut[t][p]
        return dst[t].at[zi,yi,xi,:,pl.ds(a,b-a)]
    def wait(l):
        for cp in l: cp.wait_recv()
    def go(l):
        for cp in l: cp.start()
    loc=[pltpu.make_async_copy(src[t],dst[t].at[z,y,xl],ls.at[t]) for t in range(n)]
    st1=[[],[],[],[]]
    for t in range(n):
        for p in range(4):
            a,b=cut[t][p]
            for k in (1,3,2):
                st1[p].append(mk(src[t].at[:,pl.ds(a,b-a)],at(t,p,z,y,xl),ORD[p][0],k))
    def both(p,f):
        return [cp for t in range(n) for cp in f(t,p)]
    def xsend(zi,yi):
        return lambda t,p:[mk(at(t,p,*zi,xl),at(t,p,*zi,xl),"x",1),mk(at(t,p,*yi,xl),at(t,p,*yi,xl),"x",3)]
    def ring_a(ax,zi,yi,xi):
        return lambda t,p:[mk(at(t,p,zi,yi,xi),at(t,p,zi,yi,xi),ax,k) for k in (1,3)]
    def ring_b(ax,xi):
        def f(t,p):
            if ax=="z":
                u=at(t,p,(z+3)%4,LO,xi); v=at(t,p,(z+1)%4,HI,xi)
            else:
                u=at(t,p,LO,(y+3)%4,xi); v=at(t,p,HI,(y+1)%4,xi)
            return [mk(u,u,ax,1),mk(v,v,ax,3)]
        return f
    A2=both(0,ring_a("z",z,FULL,xl)); B2=both(1,ring_a("y",FULL,y,xl))
    C2=both(2,xsend((z,LO),(z,HI))); D2=both(3,xsend((LO,y),(HI,y)))
    A2b=both(0,ring_b("z",xl)); B2b=both(1,ring_b("y",xl))
    C3=both(2,ring_a("z",z,FULL,FULL)); D3=both(3,ring_a("y",FULL,y,FULL))
    A3=both(0,xsend((LO,FULL),(HI,FULL))); B3=both(1,xsend((LO,FULL),(HI,FULL)))
    C3b=both(2,ring_b("z",FULL)); D3b=both(3,ring_b("y",FULL))
    def f0():
        go(loc)
        for p in range(4): go(st1[p])
    def f1():
        wait_loc=[cp.wait() for cp in loc]
        wait(st1[0]); go(A2)
        wait(st1[1]); go(B2)
        wait(st1[2]); go(C2)
        wait(st1[3]); go(D2)
    def f2():
        wait(A2); go(A2b); wait(B2); go(B2b)
        wait(C2); go(C3); wait(D2); go(D3)
    def f3():
        wait(A2b); go(A3); wait(B2b); go(B3)
    def f4():
        wait(C3); go(C3b); wait(D3); go(D3b)
    def f5():
        wait(A3);wait(B3);wait(C3b);wait(D3b)
        for cp in allc: cp.wait_send()
    return [f0,f1,f2,f3,f4,f5]
def gather_sems(n):
    return [pltpu.SemaphoreType.DMA((36,)),pltpu.SemaphoreType.DMA((36,)),pltpu.SemaphoreType.DMA((1,))]*n
def gather_chains(names,widths,src,dst,sems):
    chains=[gather_steps(names[t],[widths[t]],[src[t]],[dst[t]],*sems[3*t:3*t+3]) for t in range(len(names))]
    def both(k):
        def f():
            for ch in chains: ch[k]()
        return f
    return [both(k) for k in range(6)]
def gather_kernel(names,widths,*refs):
    n=len(names)
    steps=gather_chains(names,widths,refs[:n],refs[n:2*n],refs[2*n:])
    greet(GPEERS)
    for f in steps: f()
def gather_shapes(arrs):
    return tuple(jax.ShapeDtypeStruct((4,4,2)+a.shape,a.dtype) for a in arrs)
def gather(names,arrs,cid=0):
    n=len(names)
    return pl.pallas_call(functools.partial(gather_kernel,names,[a.shape[1] for a in arrs]),
      out_shape=gather_shapes(arrs),
      in_specs=[pl.BlockSpec(memory_space=pl.ANY)]*n,out_specs=tuple([pl.BlockSpec(memory_space=pl.ANY)]*n),
      scratch_shapes=gather_sems(n),
      compiler_params=pltpu.CompilerParams(collective_id=cid,has_side_effects=True))(*arrs)


RSPLIT={"q":(6,7,6),"o":(2,3,2),"e":(10,7,8),"c":(2,3,2)}
AX=("xzy","yzx","zyx")
RPEERS=[(a,k) for a in "xyz" for k in (1,2,3)]
def rcuts(name,W):
    out=[];p=0
    for n in RSPLIT[name]:
        out.append((p,min(p+n*128,W))); p+=n*128
    assert out[-1][1]==W,(name,out)
    return out
def scatter_steps(names,widths,src,vec,out,vout,scr):
    n=len(names); hasvec=vec is not None
    it=iter(scr)
    bufs=[[ [next(it) for _ in range(14)] for p in range(3)] for t in range(n)]
    vbuf=[next(it) for _ in range(3)] if hasvec else None
    ss,rs,ls=next(it),next(it),next(it)
    z,y,x,c=coords(); xl=x%2; xh=x//2
    me={"x":x,"y":y,"z":z}
    cnt=[0]; lcnt=[0]; allc=[]
    def mk(s,d,ax,k):
        i=cnt[0]; cnt[0]+=1
        cp=pltpu.make_async_remote_copy(src_ref=s,dst_ref=d,send_sem=ss.at[i],recv_sem=rs.at[i],device_id=peer_of(ax,k),device_id_type=MESH)
        allc.append(cp); return cp
    def mkload(s,d):
        i=lcnt[0]; lcnt[0]+=1
        return pltpu.make_async_copy(s,d,ls.at[i])
    cut=[rcuts(nm,w) for nm,w in zip(names,widths)]
    items=[(t,p) for t in range(n) for p in range(3)]
    f32=lambda a:a.astype(jnp.float32)
    def Dh(t,p,k,i=None):
        a,b=cut[t][p]; s=slice(None) if i is None else pl.ds(2*i,2)
        if p==0:
            h=(b-a)//2
            return src[t].at[s,:,k%2,:,pl.ds(pl.multiple_of(a+(k//2)*h,128),h)]
        if p==1: return src[t].at[s,k,:,:,pl.ds(a,b-a)]
        return src[t].at[k,s,:,:,pl.ds(a,b-a)]
    ld={}; R={}
    for t,p in items:
        own,bp,bm,rlp,rlm,rm,rp,rl2p,rl2m,rm2,rp2,out2,r3,r4=bufs[t][p]
        k=me[AX[p][0]]; ax=AX[p][0]
        ld[t,p]=[mkload(Dh(t,p,(k+1)%4,0),bp),mkload(Dh(t,p,(k+3)%4,1),bm),mkload(Dh(t,p,k),own)]
        R[t,p,"a"]=[mk(Dh(t,p,(k+2)%4,0),rlp,ax,1),mk(Dh(t,p,(k+2)%4,1),rlm,ax,3)]
        R[t,p,"b"]=[mk(Dh(t,p,(k+1)%4,1),rm.at[pl.ds(2,2)],ax,1),mk(Dh(t,p,(k+3)%4,0),rp.at[pl.ds(0,2)],ax,3),
                    mk(bp,rm.at[pl.ds(0,2)],ax,1),mk(bm,rp.at[pl.ds(2,2)],ax,3)]
        m=4 if p==0 else 2; hm=m//2
        ax=AX[p][1]; k=me[ax]
        L=pl.ds(0,hm); H=pl.ds(hm,hm)
        R[t,p,"c"]=[mk(own.at[(k+2)%4,L],rl2p,ax,1),mk(own.at[(k+2)%4,H],rl2m,ax,3)]
        R[t,p,"d"]=[mk(own.at[(k+1)%4,H],rm2.at[H],ax,1),mk(own.at[(k+3)%4,L],rp2.at[L],ax,3),
                    mk(own.at[(k+1)%4,L],rm2.at[L],ax,1),mk(own.at[(k+3)%4,H],rp2.at[H],ax,3)]
        ax=AX[p][2]; k=me[ax]; q=4 if p==0 else 2
        R[t,p,"e"]=[mk(out2.at[(k+j)%q],r3.at[j-1],ax,j) for j in (1,2,3)]
        if p==0: R[t,p,"f"]=[mk(r4.at[xh],r4.at[xh],"x",2)]
    if hasvec:
        for st in range(3):
            ax="xyz"[st]; b=vbuf[st]
            R["v",st]=[mk(b.at[me[ax]],b.at[me[ax]],ax,k) for k in (1,2,3)]
    def vgo(st,v):
        vbuf[st][pl.ds(me["xyz"[st]],1)]=v[None]
        for cp in R["v",st]: cp.start()
    def vsum(st):
        for cp in R["v",st]: cp.wait_recv()
        b=vbuf[st]
        return (b[0]+b[1])+(b[2]+b[3])
    def addin(dst,other,cntn,f,g):
        def body(i,_):
            dst[f(i)]=(f32(dst[f(i)])+f32(other[g(i)])).astype(jnp.bfloat16)
            return 0
        lax.fori_loop(0,cntn,body,0)
    def first():
        for t,p in items:
            for cp in ld[t,p]: cp.start()
        if hasvec: vgo(0,vec[...])
        for t,p in items:
            for cp in R[t,p,"a"]: cp.start()
        for t,p in items:
            for cp in R[t,p,"b"][:2]: cp.start()
    def relay(t,p):
        def f():
            own,bp,bm,rlp,rlm=bufs[t][p][:5]
            m=4 if p==0 else 2
            ix=lambda i:(i//m,i%m)
            ld[t,p][0].wait(); R[t,p,"a"][0].wait_recv(); addin(bp,rlp,2*m,ix,ix); R[t,p,"b"][2].start()
            ld[t,p][1].wait(); R[t,p,"a"][1].wait_recv(); addin(bm,rlm,2*m,ix,ix); R[t,p,"b"][3].start()
        return f
    def sum1(t,p):
        def f():
            own,bp,bm,rlp,rlm,rm,rp=bufs[t][p][:7]
            m=4 if p==0 else 2
            ld[t,p][2].wait()
            for cp in R[t,p,"b"]: cp.wait_recv()
            def body(i,_):
                j=(i//m,i%m)
                own[j]=(f32(own[j])+(f32(rm[j])+f32(rp[j]))).astype(jnp.bfloat16)
                return 0
            lax.fori_loop(0,4*m,body,0)
            for cp in R[t,p,"c"]: cp.start()
            for cp in R[t,p,"d"][:2]: cp.start()
        return f
    def relay2(t,p):
        def f():
            own,rl2p,rl2m=bufs[t][p][0],bufs[t][p][7],bufs[t][p][8]
            m=4 if p==0 else 2; hm=m//2; k=me[AX[p][1]]
            R[t,p,"c"][0].wait_recv()
            addin(own,rl2p,hm,lambda i:((k+1)%4,i),lambda i:i)
            R[t,p,"d"][2].start()
            R[t,p,"c"][1].wait_recv()
            addin(own,rl2m,hm,lambda i:((k+3)%4,hm+i),lambda i:i)
            R[t,p,"d"][3].start()
        return f
    def sum2(t,p):
        def f():
            own,rm2,rp2,out2=bufs[t][p][0],bufs[t][p][9],bufs[t][p][10],bufs[t][p][11]
            m=4 if p==0 else 2
            k=me[AX[p][1]]
            for cp in R[t,p,"d"]: cp.wait_recv()
            def body(i,_):
                out2[i]=(f32(own[k,i])+(f32(rm2[i])+f32(rp2[i]))).astype(jnp.bfloat16)
                return 0
            lax.fori_loop(0,m,body,0)
            for cp in R[t,p,"e"]: cp.start()
        return f
    def last(t,p):
        def f():
            out2,r3,r4=bufs[t][p][11:14]
            a,b=cut[t][p]
            for cp in R[t,p,"e"]: cp.wait_recv()
            k=me[AX[p][2]] if p==0 else xl
            s=(f32(out2[k])+f32(r3[1]))+(f32(r3[0])+f32(r3[2]))
            if p==0:
                r4[xh]=s.astype(jnp.bfloat16)
                R[t,p,"f"][0].start()
            else:
                out[t][:,pl.ds(a,b-a)]=s
        return f
    def end():
        for t in range(n):
            a,b=cut[t][0]; h=(b-a)//2; r4=bufs[t][0][13]
            R[t,0,"f"][0].wait_recv()
            for j in range(2): out[t][:,pl.ds(a+j*h,h)]=f32(r4[j])
        if hasvec: vout[...]=vsum(2)
        for cp in allc: cp.wait_send()
    stages=[[first]]+[[f(t,p) for t,p in items] for f in (relay,sum1,relay2,sum2)]+[[last(t,p) for t,p in sorted(items,key=lambda q:q[1])],[end]]
    if hasvec:
        stages[2].insert(0,lambda:vgo(1,vsum(0)))
        stages[4].insert(0,lambda:vgo(2,vsum(1)))
    return stages
def staggered(chains,by=2):
    order=[]
    for tick in range(7+by*(len(chains)-1)):
        for i,ch in enumerate(chains):
            if 0<=tick-by*i<7: order.append(ch[tick-by*i])
    return order
def scatter_chains(names,widths,src,vec,out,vout,scr):
    hv=vec is not None; chains=[]; at=0
    for t in range(len(names)):
        size=42+3*(hv and t==0)+3
        chains.append(scatter_steps(names[t],[widths[t]],[src[t]],vec if t==0 else None,[out[t]],vout if t==0 else None,scr[at:at+size]))
        at+=size
    return chains
def scatter_scratch(names,parts,vec=None):
    scr=[]
    for t,nm in enumerate(names):
        r,w=parts[t].shape[3:]; hv=vec is not None and t==0
        for p,(a,b) in enumerate(rcuts(nm,w)):
            m=4 if p==0 else 2; v=(b-a)//2 if p==0 else b-a; hm=m//2
            B=lambda *s:pltpu.VMEM(s+(r,v),jnp.bfloat16)
            scr+=[B(4,m),B(2,m),B(2,m),B(2,m),B(2,m),B(4,m),B(4,m),B(hm),B(hm),B(m),B(m),B(m),B(3),B(2) if p==0 else pltpu.VMEM((8,128),jnp.bfloat16)]
        if hv: scr+=[pltpu.VMEM((4,)+vec.shape,jnp.float32)]*3
        nd=46+9*hv
        scr+=[pltpu.SemaphoreType.DMA((nd,)),pltpu.SemaphoreType.DMA((nd,)),pltpu.SemaphoreType.DMA((9,))]
    return scr
def scatter_kernel(names,widths,hasvec,*refs):
    n=len(names); h=int(hasvec)
    chains=scatter_chains(names,widths,refs[:n],refs[n] if h else None,refs[n+h:2*n+h],refs[2*n+h] if h else None,refs[2*(n+h):])
    greet(RPEERS)
    for stage in staggered(chains):
        for f in stage: f()
def scatter_shapes(parts,vec=None):
    return tuple(jax.ShapeDtypeStruct(a.shape[3:],jnp.float32) for a in parts)+((jax.ShapeDtypeStruct(vec.shape,jnp.float32),) if vec is not None else ())
def reduce_scatter(names,parts,vec=None,cid=2):
    n=len(names); hv=vec is not None
    A=pl.BlockSpec(memory_space=pl.ANY); V=pl.BlockSpec(memory_space=pltpu.VMEM)
    return pl.pallas_call(functools.partial(scatter_kernel,names,[a.shape[4] for a in parts],hv),
      out_shape=scatter_shapes(parts,vec),
      in_specs=[A]*n+[V]*hv,out_specs=tuple([V]*(n+hv)),scratch_shapes=scatter_scratch(names,parts,vec),
      compiler_params=pltpu.CompilerParams(collective_id=cid,has_side_effects=True,vmem_limit_bytes=58<<20))(*parts,*([vec] if hv else []))


HD=64; LEN=4096; NEG=-1e30; ROWS=32
FQ,FK,BQ,BK=1024,1024,512,512
def dot(a,b): return lax.dot_general(a,b,(((1,),(0,)),((),())),preferred_element_type=jnp.float32)
def dot_nt(a,b): return lax.dot_general(a,b,(((1,),(1,)),((),())),preferred_element_type=jnp.float32)
def group_barrier(d,r,c,across):
    bar=pltpu.get_barrier_semaphore()
    for rr in across: pl.semaphore_signal(bar,inc=1,device_id=(1-d,rr,c),device_id_type=MESH)
    def body(i,_):
        @pl.when(i!=r*2+c)
        def _():
            pl.semaphore_signal(bar,inc=1,device_id=(d,i//2,i%2),device_id_type=MESH)
        return 0
    lax.fori_loop(0,2*ROWS,body,0)
    pl.semaphore_wait(bar,2*ROWS-1+len(across))
def push(src,dst,send_sem,recv_sem,same,target):
    @pl.when(same)
    def _():
        pltpu.make_async_copy(src,dst,recv_sem).start()
    @pl.when(jnp.logical_not(same))
    def _():
        pltpu.make_async_remote_copy(src_ref=src,dst_ref=dst,send_sem=send_sem,recv_sem=recv_sem,device_id=target,device_id_type=MESH).start()
def pushed(src,dst,send_sem,recv_sem,same,target):
    @pl.when(jnp.logical_not(same))
    def _():
        pltpu.make_async_remote_copy(src_ref=src,dst_ref=dst,send_sem=send_sem,recv_sem=recv_sem,device_id=target,device_id_type=MESH).wait_send()
def arrived(ref,sem):
    pltpu.make_async_copy(ref,ref,sem).wait()
FWD_AT=((1,2),(2,3))
BWD_AT=((0,3),(1,4),(2,5),(3,7),(4,8),(5,9))
def attn_fwd_kernel(names,widths,*refs):
    n=len(names)
    qkv_in,start=refs[:2]
    o_recv,qkv_out,oT,lse=refs[2+n:6+n]
    qkv,knt,obf,s_in,s_out,r_in,r_out,l_sem=refs[6+2*n:14+2*n]
    steps=gather_chains(names,widths,refs[2:2+n],refs[6+n:6+2*n],refs[14+2*n:])
    d=lax.axis_index("dev"); r=lax.axis_index("row"); c=lax.axis_index("col")
    group_barrier(d,r,c,[r+1-2*(r%2)])
    lanes=pl.ds(pl.multiple_of(r*128,128),128)
    def full(fn):
        def body(i,_):
            fn(qkv_in.at[i%2,:,i//2+c],qkv.at[:,:,lanes],s_in.at[i],r_in,i==r,(d,i,c))
            return 0
        lax.fori_loop(0,24,body,0)
    def halves(fn):
        rows=pl.ds(pl.multiple_of(32*c,32),32)
        for s in range(2):
            fn(qkv_in.at[s,:,12*(1-c),rows],qkv.at[:,rows,lanes],s_in.at[24+s],r_in,(r==24+s)&(c==0),(d,24+s,0))
    full(push); halves(push)
    steps[0]()
    item=(r<24)|((c==0)&(r<26))
    head=r//2+13*c; seq=r%2
    def outs(qi,fn):
        def body(i,_):
            rr=qi*(FQ//128)+i//2; cc=i%2
            fn(obf.at[:,pl.ds(pl.multiple_of(rr*128,128),128)],o_recv.at[seq,head],s_out.at[rr*2+cc],r_out,(rr==r)&(cc==c),(d,rr,cc))
            return 0
        lax.fori_loop(0,FQ//64,body,0)
    save=pltpu.make_async_copy(qkv,qkv_out,l_sem)
    @pl.when(item)
    def _():
        arrived(qkv,r_in)
        save.start()
        for a in range(LEN//512):
            sl=pl.ds(a*512,512)
            knt[sl,:]=qkv[1,:,sl].T
    steps[1]()
    def qloop(qi,_):
        @pl.when(item)
        def _():
            iota=lax.broadcasted_iota(jnp.int32,(FK,FQ),0)
            iotl=lax.broadcasted_iota(jnp.int32,(FK,FQ),1)
            qs=pl.ds(pl.multiple_of(qi*FQ,FQ),FQ)
            q=qkv[0,:,qs]*jnp.bfloat16(0.125)
            st=start[:,qs]
            def step(kj,carry,diag):
                m,l,acc=carry
                ks=pl.ds(pl.multiple_of(kj*FK,FK),FK)
                s=dot(knt[ks,:],q)
                ok=iota>=(st-kj*FK)
                if diag: ok=ok&(iota<=iotl)
                s=jnp.where(ok,s,NEG)
                mn=jnp.maximum(m,jnp.max(s,axis=0,keepdims=True))
                p=jnp.exp(s-mn)
                al=jnp.exp(m-mn)
                l=l*al+jnp.sum(p,axis=0,keepdims=True)
                acc=acc*al+dot(qkv[2,:,ks],p.astype(jnp.bfloat16))
                return mn,l,acc
            carry=(jnp.full((1,FQ),NEG,jnp.float32),jnp.zeros((1,FQ),jnp.float32),jnp.zeros((HD,FQ),jnp.float32))
            carry=lax.fori_loop(0,qi,lambda kj,cr:step(kj,cr,False),carry)
            m,l,acc=step(qi,carry,True)
            o=acc/l
            oT[:,qs]=o
            lse[:,qs]=m+jnp.log(l)
            obf[:,qs]=o.astype(jnp.bfloat16)
            outs(qi,push)
        for at,f in FWD_AT:
            pl.when(qi==at)(steps[f])
        return 0
    lax.fori_loop(0,LEN//FQ,qloop,0)
    for f in range(FWD_AT[-1][1]+1,6): steps[f]()
    @pl.when(item)
    def _():
        save.wait()
        for qi in range(LEN//FQ): outs(qi,pushed)
    full(pushed); halves(pushed)
    arrived(o_recv,r_out)
def attn_bwd_kernel(names,widths,*refs):
    n=len(names)
    do_in,qkv,oT,start,lse=refs[:5]
    d_recv=refs[5+n]
    doT,knt,vnt,dqa,delta,dout,s_in,s_out,r_in,r_out=refs[6+2*n:16+2*n]
    order=staggered(scatter_chains(names,widths,refs[5:5+n],None,refs[6+n:6+2*n],None,refs[16+2*n:]))
    d=lax.axis_index("dev"); r=lax.axis_index("row"); c=lax.axis_index("col")
    group_barrier(d,r,c,[r+1-2*(r%2),r])
    lanes=pl.ds(pl.multiple_of(r*128,128),128)
    def full(fn):
        def body(i,_):
            fn(do_in.at[i%2,i//2+c],doT.at[:,lanes],s_in.at[i],r_in,i==r,(d,i,c))
            return 0
        lax.fori_loop(0,24,body,0)
    def halves(fn):
        rows=pl.ds(pl.multiple_of(32*c,32),32)
        for s in range(2):
            fn(do_in.at[s,12*(1-c),rows],doT.at[rows,lanes],s_in.at[24+s],r_in,(r==24+s)&(c==0),(d,24+s,0))
    full(push); halves(push)
    order[0][0]()
    item=(r<24)|((c==0)&(r<26))
    def outs(fn):
        @pl.when(r<24)
        def _():
            def body(i,_):
                fn(dout.at[:,:,pl.ds(pl.multiple_of(i*128,128),128)],d_recv.at[:,(r%2)*13+r//2+c],s_out.at[i],r_out,i==r,(d,i,c))
                return 0
            lax.fori_loop(0,ROWS,body,0)
        @pl.when(r>=24)
        def _():
            def body(i,_):
                rr=i//2; cc=i%2
                rows=pl.ds(pl.multiple_of(32*cc,32),32)
                fn(dout.at[:,rows,pl.ds(pl.multiple_of(rr*128,128),128)],d_recv.at[:,(r%2)*13+12*(1-cc),rows],s_out.at[i],r_out,(rr==r)&(cc==c),(d,rr,cc))
                return 0
            lax.fori_loop(0,2*ROWS,body,0)
    @pl.when(item)
    def _():
        for a in range(LEN//512):
            sl=pl.ds(a*512,512)
            knt[sl,:]=qkv[1,:,sl].T
            vnt[sl,:]=qkv[2,:,sl].T
        dqa[...]=jnp.zeros_like(dqa)
        arrived(doT,r_in)
        for a in range(LEN//512):
            sl=pl.ds(a*512,512)
            delta[:,sl]=jnp.sum(oT[:,sl]*doT[:,sl].astype(jnp.float32),axis=0,keepdims=True)
    def kloop(kj,_):
        @pl.when(item)
        def _():
            iota=lax.broadcasted_iota(jnp.int32,(BK,BQ),0)
            iotl=lax.broadcasted_iota(jnp.int32,(BK,BQ),1)
            ks=pl.ds(pl.multiple_of(kj*BK,BK),BK)
            kn=knt[ks,:]; vn=vnt[ks,:]; kT=qkv[1,:,ks]
            def step(qi,carry,diag):
                dk,dv=carry
                qs=pl.ds(pl.multiple_of(qi*BQ,BQ),BQ)
                q=qkv[0,:,qs]*jnp.bfloat16(0.125)
                do=doT[:,qs]
                s=dot(kn,q)
                ok=iota>=(start[:,qs]-kj*BK)
                if diag: ok=ok&(iota<=iotl)
                p=jnp.exp(jnp.where(ok,s,NEG)-lse[:,qs])
                dp=dot(vn,do)
                ds=(p*(dp-delta[:,qs])).astype(jnp.bfloat16)
                dv=dv+dot_nt(do,p.astype(jnp.bfloat16))
                dk=dk+dot_nt(q,ds)
                dqa[:,qs]+=dot(kT,ds)
                return dk,dv
            z=jnp.zeros((HD,BK),jnp.float32)
            carry=step(kj,(z,z),True)
            dk,dv=lax.fori_loop(kj+1,LEN//BQ,lambda qi,cr:step(qi,cr,False),carry)
            dout[1,:,ks]=dk.astype(jnp.bfloat16)
            dout[2,:,ks]=dv.astype(jnp.bfloat16)
        at=1
        for step,to in BWD_AT:
            for stage in order[at:to]:
                for f in stage: pl.when(kj==step)(f)
            at=to
        return 0
    lax.fori_loop(0,LEN//BK,kloop,0)
    @pl.when(item)
    def _():
        for a in range(LEN//512):
            sl=pl.ds(a*512,512)
            dout[0,:,sl]=(dqa[:,sl]*0.125).astype(jnp.bfloat16)
        outs(push)
    for stage in order[BWD_AT[-1][1]:]:
        for f in stage: f()
    pl.when(item)(lambda:outs(pushed))
    full(pushed); halves(pushed)
    arrived(d_recv.at[:,pl.ds(0,25)],r_out)
VM=pl.BlockSpec(memory_space=pltpu.VMEM); ANY=pl.BlockSpec(memory_space=pl.ANY)
bf=jnp.bfloat16
def attend(qkv,start,names,arrs,cid=1):
    S=jax.ShapeDtypeStruct; n=len(names)
    out=pl.pallas_call(functools.partial(attn_fwd_kernel,names,[a.shape[1] for a in arrs]),
      out_shape=(S((2,25,HD,128),bf),S((3,HD,LEN),bf),S((HD,LEN),jnp.float32),S((1,LEN),jnp.float32))+gather_shapes(arrs),
      in_specs=[VM,VM]+[ANY]*n,out_specs=(ANY,ANY,VM,VM)+(ANY,)*n,
      scratch_shapes=[pltpu.VMEM((3,HD,LEN),bf),pltpu.VMEM((LEN,HD),bf),pltpu.VMEM((HD,LEN),bf),
        pltpu.SemaphoreType.DMA((26,)),pltpu.SemaphoreType.DMA((64,)),pltpu.SemaphoreType.DMA,pltpu.SemaphoreType.DMA,pltpu.SemaphoreType.DMA]+gather_sems(n),
      compiler_params=pltpu.CompilerParams(collective_id=cid,has_side_effects=True,vmem_limit_bytes=50<<20))(qkv,start,*arrs)
    return out[0],out[1:4],out[4:]
def attend_back(do,kept,start,names,parts,cid=3):
    S=jax.ShapeDtypeStruct; n=len(names)
    qkv,oT,lse=kept
    out=pl.pallas_call(functools.partial(attn_bwd_kernel,names,[a.shape[4] for a in parts]),
      out_shape=(S((3,26,HD,128),bf),)+scatter_shapes(parts),
      in_specs=[VM]*5+[ANY]*n,out_specs=(ANY,)+(VM,)*n,
      scratch_shapes=[pltpu.VMEM((HD,LEN),bf),pltpu.VMEM((LEN,HD),bf),pltpu.VMEM((LEN,HD),bf),pltpu.VMEM((HD,LEN),jnp.float32),pltpu.VMEM((1,LEN),jnp.float32),pltpu.VMEM((3,HD,LEN),bf),
        pltpu.SemaphoreType.DMA((26,)),pltpu.SemaphoreType.DMA((64,)),pltpu.SemaphoreType.DMA,pltpu.SemaphoreType.DMA]+scatter_scratch(names,parts),
      compiler_params=pltpu.CompilerParams(collective_id=cid,has_side_effects=True,vmem_limit_bytes=60<<20))(do,qkv,oT,start,lse,*parts)
    return out[0],out[1:]


TT=256; WC=800; FH=3200; TF=640; KH=896
GC=0.7978845608028654
def dot_tn(a,b): return lax.dot_general(a,b,(((0,),(0,)),((),())),preferred_element_type=jnp.float32)
def mlp_kernel(h2,we,eb,wc,mid,cb,g,result,part_c,part_e,dh2,dsum,
        wev,wcv,pre,a_own,a_recv,da_send,da_recv,dpre,dh_send,dh_recv,stage_e,stage_c,w_sem,s_sem,r_sem,e_sem,c_sem):
    c=lax.axis_index("col"); other=1-c
    partner=(lax.axis_index("dev"),lax.axis_index("row"),other)
    loads=[pltpu.make_async_copy(wc,wcv,w_sem.at[0]),pltpu.make_async_copy(we,wev,w_sem.at[1])]
    for cp in loads: cp.start()
    bar=pltpu.get_barrier_semaphore()
    pl.semaphore_signal(bar,inc=1,device_id=partner,device_id_type=MESH)
    pl.semaphore_wait(bar,1)
    def swap(i,s,d):
        return pltpu.make_async_remote_copy(src_ref=s,dst_ref=d,send_sem=s_sem.at[i],recv_sem=r_sem.at[i],device_id=partner,device_id_type=MESH)
    x_da,x_a,x_dh=swap(0,da_send,da_recv),swap(1,a_own,a_recv),swap(2,dh_send,dh_recv)
    lanes=lambda k,n:pl.ds(pl.multiple_of(k*n,128),n)
    rows=lambda base,k,n:pl.ds(pl.multiple_of(base+k*n,128),n)
    f32=lambda v:v.astype(jnp.float32)
    NT=FH//TF
    def loop(n,f):
        def body(k,_):
            f(k)
            return 0
        lax.fori_loop(0,n,body,0)
    loads[0].wait()
    def f(k): da_send[:,lanes(k,TF)]=dot_nt(g[...],wcv[rows(other*FH,k,TF),:]).astype(bf)
    loop(NT,f)
    x_da.start()
    loads[1].wait()
    def f(k):
        p=dot(h2[...],wev[:,lanes(k,TF)])+eb[:,lanes(k,TF)]
        pre[:,lanes(k,TF)]=p
        a_own[:,lanes(k,TF)]=(p*(0.5*(1.0+jnp.tanh(GC*(p+0.044715*(p*p*p)))))).astype(bf)
    loop(NT,f)
    x_a.start()
    x_da.wait_recv()
    def f(k):
        sl=lanes(k,TF)
        d=dot_nt(g[...],wcv[rows(c*FH,k,TF),:])+f32(da_recv[:,sl])
        p=pre[:,sl]
        t=jnp.tanh(GC*(p+0.044715*(p*p*p)))
        slope=0.5*(1.0+t)+p*(0.5*(1.0-t*t)*(GC*(1.0+(3*0.044715)*(p*p))))
        dp=(d*slope).astype(bf)
        dpre[:,sl]=dp
        dsum[:,sl]=jnp.sum(f32(dp),axis=0,keepdims=True)
    loop(NT,f)
    def f(k): dh_send[:,lanes(k,128)]=dot_nt(dpre[...],wev[rows(other*KH,k,128),:]).astype(bf)
    loop(KH//128,f)
    x_dh.start()
    def f(k): dh2[:,lanes(k,128)]=dot_nt(dpre[...],wev[rows(c*KH,k,128),:])
    loop(KH//128,f)
    def emit(i,stage,sem,dst,value):
        slot=i%2
        cp=pltpu.make_async_copy(stage.at[slot],dst,sem.at[slot])
        if i>=2: prev[slot].wait()
        stage[slot]=value
        cp.start(); prev[slot]=cp
    prev={}
    for j in range(KP//256):
        emit(j,stage_e,e_sem,part_e.at[pl.ds(256*j,256)],dot_tn(h2[:,256*j:256*j+256],dpre[...]).astype(bf))
    for cp in prev.values(): cp.wait()
    x_a.wait_recv()
    br=dot(a_own[...],wcv[rows(c*FH,0,FH),:])+dot(a_recv[...],wcv[rows(other*FH,0,FH),:])
    result[...]=(mid[...]+(br+cb[...])).astype(bf)
    prev={}
    for i in range(2*NT):
        a,b,k=(a_own,c,i) if i<NT else (a_recv,other,i-NT)
        emit(i,stage_c,c_sem,part_c.at[rows(b*FH,k,TF)],dot_tn(a[:,k*TF:k*TF+TF],g[...]).astype(bf))
    x_dh.wait_recv()
    dh2[...]=dh2[...]+f32(dh_recv[...])
    for cp in prev.values(): cp.wait()
    for cp in (x_da,x_a,x_dh): cp.wait_send()
def mlp(h2,we,eb,wc,mid,cb,g,cid=4):
    S=jax.ShapeDtypeStruct; f=jnp.float32; V=pltpu.VMEM
    return pl.pallas_call(mlp_kernel,
      out_shape=(S((TT,WC),bf),S((6400,WC),bf),S((KP,FH),bf),S((TT,KH),f),S((1,FH),f)),
      in_specs=[VM,ANY,VM,ANY,VM,VM,VM],out_specs=(VM,ANY,ANY,VM,VM),
      scratch_shapes=[V((KP,FH),bf),V((6400,WC),bf),V((TT,FH),f)]+[V((TT,FH),bf)]*5+[V((TT,KH),bf)]*2+[V((2,256,FH),bf),V((2,TF,WC),bf)]+[pltpu.SemaphoreType.DMA((n,)) for n in (2,3,3,2,2)],
      compiler_params=pltpu.CompilerParams(collective_id=cid,has_side_effects=True,vmem_limit_bytes=58<<20))(h2,we,eb,wc,mid,cb,g)
def pair_dot_kernel(v,w,out,send,recv,s_sem,r_sem):
    c=lax.axis_index("col"); other=1-c
    partner=(lax.axis_index("dev"),lax.axis_index("row"),other)
    bar=pltpu.get_barrier_semaphore()
    pl.semaphore_signal(bar,inc=1,device_id=partner,device_id_type=MESH)
    for k in range(KH//128):
        send[:,128*k:128*k+128]=dot_nt(v[...],w[pl.ds(pl.multiple_of(other*KH+128*k,128),128),:]).astype(bf)
    pl.semaphore_wait(bar,1)
    cp=pltpu.make_async_remote_copy(src_ref=send,dst_ref=recv,send_sem=s_sem,recv_sem=r_sem,device_id=partner,device_id_type=MESH)
    cp.start()
    for k in range(KH//128):
        out[:,128*k:128*k+128]=dot_nt(v[...],w[pl.ds(pl.multiple_of(c*KH+128*k,128),128),:])
    cp.wait()
    out[...]=out[...]+recv[...].astype(jnp.float32)
def pair_dot(v,w,cid):
    return pl.pallas_call(pair_dot_kernel,out_shape=jax.ShapeDtypeStruct((TT,KH),jnp.float32),in_specs=[VM,VM],out_specs=VM,
      scratch_shapes=[pltpu.VMEM((TT,KH),bf)]*2+[pltpu.SemaphoreType.DMA]*2,
      compiler_params=pltpu.CompilerParams(collective_id=cid,has_side_effects=True,vmem_limit_bytes=40<<20))(v,w)
def outer_kernel(a,b,o):
    o[...]=dot_tn(a[...],b[...]).astype(bf)
def outer(a,b):
    m=a.shape[1]; n=b.shape[1]
    return pl.pallas_call(outer_kernel,out_shape=jax.ShapeDtypeStruct((m,n),bf),grid=(m//256,),
      in_specs=[pl.BlockSpec((TT,256),lambda i:(0,i)),pl.BlockSpec((TT,n),lambda i:(0,0))],out_specs=pl.BlockSpec((256,n),lambda i:(i,0)),
      compiler_params=pltpu.CompilerParams(vmem_limit_bytes=32<<20))(a,b)


def width_sums(first_sum, second_sum):
    return lax.psum((first_sum, second_sum), "col")


def full_rows(values):
    return lax.all_gather(values, "col", axis=1, tiled=True)


def norm_forward(values, norm_gain, norm_bias):
    totals = width_sums(jnp.sum(values, axis=1), jnp.sum(values * values, axis=1))
    averages = totals[0] / D
    reciprocal = lax.rsqrt(totals[1] / D - averages * averages + 1e-05)
    normed = (values - averages[:, None]) * reciprocal[:, None]
    return (normed, reciprocal, normed * norm_gain + norm_bias)


def norm_backward(incoming, normed, reciprocal, norm_gain):
    scaled = incoming * norm_gain
    totals = width_sums(jnp.sum(scaled, axis=1), jnp.sum(scaled * normed, axis=1))
    return reciprocal[:, None] * (
        scaled - totals[0][:, None] / D - normed * (totals[1][:, None] / D)
    )


def pad_rows(block):
    return jnp.pad(block, ((0, 6), (0, 0)))


def pad_features(values):
    n = values.shape[0]
    return jnp.pad(values.reshape(n, 32, 50), ((0, 0), (0, 0), (0, 6))).reshape(n, KP)


def unpad_features(values):
    n = values.shape[0]
    return values.reshape(n, 16, 56)[:, :, :50].reshape(n, 800)


def per_device(
    tokens,
    segments,
    first_gain,
    first_bias,
    attention_in,
    attention_bias,
    attention_out,
    output_bias,
    second_gain,
    second_bias,
    expand_weight,
    expand_bias,
    contract_weight,
    contract_bias,
    cotangent,
):
    seqs, block_len, width = tokens.shape
    row_total = seqs * block_len
    row = lax.axis_index("row")
    col = lax.axis_index("col")
    weight_qkv, weight_expand = gather(
        "qe", (pad_rows(attention_in.reshape(50, 3 * width)), pad_rows(expand_weight)), 0
    )
    weight_qkv = weight_qkv.reshape(KP, 3 * width)

    own_seg = lax.dynamic_index_in_dim(segments, row % 2, 0, keepdims=True)
    positions = jnp.arange(LEN, dtype=jnp.int32)[None]
    before = jnp.concatenate((own_seg[:, :1], own_seg[:, :-1]), axis=1)
    start = lax.cummax(jnp.where(own_seg != before, positions, 0), axis=1)

    float_tokens = tokens.astype(jnp.float32).reshape(row_total, width)
    normed_one, recip_one, hidden_one = norm_forward(float_tokens, first_gain, first_bias)
    rows_one = pad_features(full_rows(hidden_one.astype(jnp.bfloat16)))
    bias_three = jnp.concatenate(
        (attention_bias[0], jnp.zeros_like(attention_bias[0]), attention_bias[1])
    )
    projected = jnp.einsum(
        "dm,snd->smn",
        weight_qkv,
        rows_one.reshape(seqs, block_len, KP),
        preferred_element_type=jnp.float32,
    )
    projected = (projected + bias_three[None, :, None]).astype(jnp.bfloat16)
    projected = projected.reshape(seqs, 3, width, block_len)

    def head_slots(values):
        lead = [(0, 0)] * (values.ndim - 2)
        slots = jnp.where(
            col == 0,
            jnp.pad(values, lead + [(0, 32), (0, 0)]),
            jnp.pad(values, lead + [(32, 0), (0, 0)]),
        )
        return slots.reshape(values.shape[:-2] + (13, HD, block_len))

    attended, kept, gathered = attend(
        head_slots(projected),
        start,
        "co",
        (contract_weight, pad_rows(attention_out)),
        1,
    )
    weight_out = gathered[1].reshape(KP, width)
    weight_expand = weight_expand.reshape(KP, 4 * width)
    weight_contract = gathered[0].reshape(4 * D, width)
    rows_attn = jnp.pad(
        attended.reshape(seqs, 32, 50, block_len), ((0, 0), (0, 0), (0, 6), (0, 0))
    ).reshape(seqs, KP, block_len)
    middle = float_tokens + (
        jnp.einsum(
            "sfn,fd->snd", rows_attn, weight_out, preferred_element_type=jnp.float32
        ).reshape(row_total, width)
        + output_bias
    )
    normed_two, recip_two, hidden_two = norm_forward(middle, second_gain, second_bias)
    rows_two = pad_features(full_rows(hidden_two.astype(jnp.bfloat16)))
    grad_low = cotangent.reshape(row_total, width)
    grad_float = grad_low.astype(jnp.float32)
    result, part_contract, part_expand, grad_two, expand_sums = mlp(
        rows_two, weight_expand, expand_bias[None], weight_contract, middle, contract_bias[None], grad_low, 4
    )
    result = result.reshape(tokens.shape)
    grad_two = unpad_features(grad_two)
    grad_middle = grad_float + norm_backward(grad_two, normed_two, recip_two, second_gain)
    grad_attn = grad_middle.astype(jnp.bfloat16)
    part_out = outer(jnp.transpose(rows_attn, (0, 2, 1)).reshape(row_total, KP), grad_attn)
    grad_mixed = unpad_features(pair_dot(grad_attn, weight_out, 5).astype(jnp.bfloat16))
    grad_mixed = jnp.transpose(grad_mixed.reshape(seqs, block_len, width), (0, 2, 1))
    grad_slots, (sum_contract, sum_expand) = attend_back(
        head_slots(grad_mixed),
        kept,
        start,
        "ce",
        (part_contract.reshape(4, 4, 2, 200, width), part_expand.reshape(4, 4, 2, 56, 4 * width)),
        2,
    )
    grad_qkv = lax.dynamic_slice_in_dim(
        grad_slots.reshape(3, seqs, 13 * HD, block_len), 32 * col, width, 2
    )
    grad_rows = jnp.transpose(grad_qkv, (1, 3, 0, 2)).reshape(row_total, 3 * width)
    part_qkv = outer(rows_one, grad_rows)
    grad_one = unpad_features(pair_dot(grad_rows, weight_qkv, 6))
    grad_input = grad_middle + norm_backward(grad_one, normed_one, recip_one, first_gain)
    gradient_tokens = grad_input.astype(jnp.bfloat16).reshape(tokens.shape)
    qkv_sums = jnp.sum(grad_qkv.astype(jnp.float32), axis=(1, 3))
    pieces = (
        jnp.sum(grad_one * normed_one, axis=0),
        jnp.sum(grad_one, axis=0),
        qkv_sums[0],
        qkv_sums[2],
        jnp.sum(grad_attn.astype(jnp.float32), axis=0),
        jnp.sum(grad_two * normed_two, axis=0),
        jnp.sum(grad_two, axis=0),
        expand_sums[0],
        jnp.sum(grad_float, axis=0),
    )
    vector = jnp.concatenate(pieces + (jnp.zeros((640,), jnp.float32),)).reshape(80, 128)
    sum_qkv, sum_out, vector = reduce_scatter(
        "qo",
        (part_qkv.reshape(4, 4, 2, 56, 3 * width), part_out.reshape(4, 4, 2, 56, width)),
        vector,
        3,
    )
    vector = vector.reshape(-1)
    sums = []
    at = 0
    for piece in pieces:
        sums.append(vector[at : at + piece.shape[0]])
        at += piece.shape[0]
    return (
        result,
        gradient_tokens,
        sums[0],
        sums[1],
        sum_qkv[:50].reshape(50, 3, width),
        jnp.stack((sums[2], sums[3])),
        sum_out[:50],
        sums[4],
        sums[5],
        sums[6],
        sum_expand[:50],
        sums[7],
        sum_contract,
        sums[8],
    )


def solution(mesh):
    return jax.shard_map(
        per_device,
        mesh=mesh,
        in_specs=(
            P("dev", "row", "col"),
            P("dev", None),
            P("col"),
            P("col"),
            P("row", None, "col"),
            P(None, "col"),
            P("row", "col"),
            P("col"),
            P("col"),
            P("col"),
            P("row", "col"),
            P("col"),
            P("row", "col"),
            P("col"),
            P("dev", "row", "col"),
        ),
        out_specs=(
            P("dev", "row", "col"),
            P("dev", "row", "col"),
            P("col"),
            P("col"),
            P("row", None, "col"),
            P(None, "col"),
            P("row", "col"),
            P("col"),
            P("col"),
            P("col"),
            P("row", "col"),
            P("col"),
            P("row", "col"),
            P("col"),
        ),
        check_vma=False,
    )
```

time: 701 us -> 612 us (0.87)
  matrix products: 84.5 us -> 10.5 us
  Pallas kernels: 469 us -> 489 us
  waiting for transfers between devices: 17.1 us -> 0 us
  local copies, waits for them, and re-layouts: 79.3 us -> 65 us
  between operations: 15.2 us -> 1.63 us
  other arithmetic: 11 us -> 23 us
    pallas_call x4 -> x8, Pallas kernels: 309 us -> 395 us  [the longest x1 152 us: attend_back(): pl.pallas_call(functools.partial(attn_bwd_kernel, names, [a.shape[4] for...]
    dot_general x10 -> x0, matrix products: 73.6 us -> none  [the longest x6 54.4 us: matmul(): return jnp.dot(left, right, preferred_element_type=jnp.float32)]
    pallas_call x1, Pallas kernels: 160 us -> 93.2 us  [gather(): pl.pallas_call(functools.partial(gather_kernel, names, [a.shape[1] for a...]
    convert_element_type x5, local copies, waits for them, and re-layouts: 38.3 us -> 4.09 us  [the longest x2 3.51 us: per_device(): float_tokens = tokens.astype(jnp.float32).reshape(row_total, width)]
    reduce_scatter x2 -> x0, waiting for transfers between devices: 10.9 us -> none  [feature_sums(): lax.psum_scatter(values, 'col', scatter_dimension=1, tiled=True)]
    reshape x3 -> x8, local copies, waits for them, and re-layouts: 5.04 us -> 12.7 us  [the longest x4 6.03 us: unpad_features(): return values.reshape(n, 16, 56)[:, :, :50].reshape(n, 800)]
    unnamed x58 -> x89, local copies, waits for them, and re-layouts: 13.7 us -> 19 us
  transfers between devices with their start and end apart: 5 -> 0, of which waited for: 2 -> 0; matrix products, arithmetic and copies ran while one was open for 16% -> 0% of each run, Pallas kernels for 35% -> 0%
where the time goes in v2:
time: 612 us; the launch traced here: 603 us
  Pallas kernels  489 us (80%)
  local copies, waits for them, and re-layouts  65 us (11%)
  other arithmetic  23 us (4%)
  blocking collectives  14.6 us (2%)
  matrix products  10.5 us (2%)
    pallas_call x1, Pallas kernels, attend_back(): pl.pallas_call(functools.partial(attn_bwd_kernel, names, [a.shape[4] for...  152 us
    pallas_call x1, Pallas kernels, attend(): pl.pallas_call(functools.partial(attn_fwd_kernel, names, [a.shape[1] for...  108 us
    pallas_call x1, Pallas kernels, gather(): pl.pallas_call(functools.partial(gather_kernel, names, [a.shape[1] for a...  93.2 us
    pallas_call x1, Pallas kernels, reduce_scatter(): pl.pallas_call(functools.partial(scatter_kernel, names, [a.shape[4] for a...  74 us
    pallas_call x1, Pallas kernels, mlp(): pl.pallas_call(mlp_kernel, out_shape=(S((TT, WC), bf), S((6400, WC), bf),...  46.7 us
    unnamed x89, local copies, waits for them, and re-layouts  19 us

profile of v2, /device:TPU:0, one launch (start us, length us, event | category | flops | bytes accessed | tf_op | source)
XLA Modules:
  0.0 603.3 jit_solution(14859295804076082676)
XLA Ops:
  1.4 1.2 constant_dynamic-slice_fusion.2
  2.6 1.5 compare_select_fusion
  5.0 1.1 convert_reduce_fusion.3
  6.1 2.5 all-reduce.13
  8.6 1.2 copy.64
  9.8 1.0 add_convert_fusion.2
  11.0 2.4 all_gather.6
  13.4 1.1 reshape.223
  14.5 1.3 pad.39
  15.8 1.2 reshape_reshape.6
  19.0 93.2 %shard_map.254 = (bf16[4,4,2,56,2400]{4,3,2,1,0:T(8,128)(2,1)}, bf16[4,4,2,56,3200]{4,3,2,1,0:T(8,128)(2,1)}) custom-call(bf16[56,2400]{1,0:T(8,128)(2,1)} %pad.40.refs_0_, bf16[56,3200]{1,0:T(8,128)(2,1)} %pad.41.refs_1_), custom_call_target="tpu_custom_call" | custom-call | tf_op jit(solution)/shard_map/pallas_call | solution.py:122
  112.4 7.3 %fusion = bf16[2,128,2400]{1,2,0:T(8,128)(2,1)S(1)} fusion(bf16[1792,2400,1]{1,0,2:T(8,128)(2,1)} %bitcast.81, f32[2400]{0:T(1024)S(1)} %concatenate.9, bf16[2,128,1792]{1,0,2:T(2,128)(2,1)} %reshape_reshape.6), kind=kOutput, calls=%fused_computation.1 | convolution fusion | flops 2203238400 | bytes 10757504 | tf_op jit(solution)/shard_map/dm,snd->smn/dot_general | solution.py:719
  120.8 107.9 %shard_map.255 = (bf16[2,25,64,128]{3,2,1,0:T(8,128)(2,1)S(1)}, bf16[3,64,4096]{2,1,0:T(8,128)(2,1)}, f32[64,4096]{1,0:T(8,128)S(1)}, f32[1,4096]{1,0:T(1,128)S(...) custom-call(bf16[2,3,13,64,128]{4,3,2,1,0:T(8,128)(2,1)S(1)} %bitcast.83, ...), custom_call_target="tpu_custom_call" | custom-call | tf_op jit(solution)/shard_map/pallas_call | solution.py:519
  228.7 0.8 copy.68
  230.4 3.2 fusion.4
  233.6 2.5 all-reduce.12
  236.5 2.4 all_gather.7
  238.9 1.1 reshape.236
  240.0 1.3 pad.46
  241.3 1.4 copy.74.h2
  242.7 1.0 copy.73
  244.9 46.7 %shard_map.256 = (bf16[256,800]{1,0:T(8,128)(2,1)}, bf16[6400,800]{1,0:T(8,128)(2,1)}, bf16[1792,3200]{1,0:T(8,128)(2,1)}, f32[256,896]{1,0:T(8,128)}, f32[1,3200]{1,0:T(1,128)}) custom-call(bf16[256,1792]{1,0:T(8,128)(2,1)} %copy.74.h2, bf16[1792,3200]{1,0:T(8,128)(2,1)} %bitcast.88, f32[1,3200]{1,0:T(1,128)} %broadcast_in_dim.14.eb, ...), custom_call_target="tpu_custom_call" | custom-call | tf_op jit(solution)/shard_map/pallas_call | solution.py:612
  291.6 1.5 copy.75
  293.2 1.1 slice_reduce_fusion.5
  294.2 2.2 reshape.243
  296.4 1.4 copy.76
  297.8 0.9 multiply_reduce_fusion
  298.8 2.4 all-reduce.11
  301.2 3.1 convert_reduce_fusion.1
  304.3 2.8 shard_map.257
  308.1 0.8 copy.78
  308.9 152.2 %shard_map.258 = (bf16[3,26,64,128]{3,2,1,0:T(8,128)(2,1)}, f32[200,800]{1,0:T(8,128)}, f32[56,3200]{1,0:T(8,128)}) custom-call(bf16[2,13,64,128]{3,2,1,0:T(8,128)(2,1)} %bitcast.104, bf16[3,64,4096]{2,1,0:T(8,128)(2,1)} %get-tuple-element.40.refs_1_, f32[64,4096]{1,0:T(8,128)} %copy-done.4, s32[1,4096]{1,0:T(1,128)} %copy-done.6, f32[1,4096]{1,0:T(1,128)} %copy-done.7, ...), custom_call_target="tpu_custom_call" | custom-call | tf_op jit(solution)/shard_map/pallas_call | solution.py:529
  461.1 1.4 constant_dynamic-slice_fusion.1
  462.5 0.9 copy.91
  463.5 1.2 copy.98
  464.7 1.7 copy.80.v.b
  466.4 3.5 copy-done.2
  469.9 5.5 shard_map.259
  475.4 1.3 copy.81
  476.7 2.3 copy.83
  479.0 2.7 reshape.252
  482.4 3.0 multiply_reduce_fusion.1
  485.4 1.4 reduce_sum.156
  486.7 1.4 reduce_sum.158
  488.1 6.2 %convert_reduce_fusion = f32[3,800]{1,0:T(4,128)S(1)} fusion(bf16[3,2,800,128]{3,2,1,0:T(8,128)(2,1)} %copy-done.10), kind=kLoop, calls=%fused_computation.2 | loop fusion | flops 1226400 | bytes 1238400 | tf_op jit(solution)/shard_map/reduce_sum | solution.py:786
  496.3 1.9 convert_reduce_fusion.2
  498.8 1.5 concatenate.11
  500.3 2.4 shard_map.261
  502.7 1.7 copy-done.1
  504.4 0.8 copy.84.a
  505.3 3.8 shard_map.260
  509.1 3.3 copy-done
  512.4 74.0 %shard_map.262 = (f32[56,2400]{1,0:T(8,128)}, f32[56,800]{1,0:T(8,128)}, f32[80,128]{1,0:T(8,128)}) custom-call(bf16[4,4,2,56,2400]{4,3,2,1,0:T(8,128)(2,1)} %bitcast.79, bf16[4,4,2,56,800]{4,3,2,1,0:T(8,128)(2,1)} %bitcast.80, f32[80,128]{1,0:T(8,128)} %bitcast.112), custom_call_target="tpu_custom_call" | custom-call | tf_op jit(solution)/shard_map/pallas_call | solution.py:311
  586.5 1.5 fusion.5
  588.7 1.4 reshape.259
  590.2 0.9 copy.89
  591.0 1.4 slice.105
  592.5 2.4 all-reduce.10
  594.9 1.0 reshape.251
  595.9 1.4 copy.82
  597.8 1.0 copy.88
  598.7 2.0 copy.87
  601.4 0.9 copy.103
  602.3 0.9 copy.104
  (119 shorter events, 13.3 us)
Async XLA Ops:
  4.9 115.7 %copy-start.6 = (s32[1,4096]{1,0:T(1,128)}, s32[1,4096]{1,0:T(1,128)S(1)}, u32[]{:S(2)}) copy-start(s32[1,4096]{1,0:T(1,128)S(1)} %reduce_window_max.19.refs_1_.refs_3_) | copy-start | bytes 49156
  8.6 2.2 copy-start.30
  8.6 473.8 %copy-start.28 = (f32[256]{0:T(256)}, f32[256]{0:T(256)S(1)}, u32[]{:S(2)}) copy-start(f32[256]{0:T(256)S(1)} %get-tuple-element.133) | copy-start | bytes 3076
  9.8 220.6 %copy-start.13 = (f32[2,128,800]{2,1,0:T(8,128)}, f32[2,128,800]{2,1,0:T(8,128)S(1)}, u32[]{:S(2)}) copy-start(f32[2,128,800]{2,1,0:T(8,128)S(1)} %copy.64) | copy-start | bytes 2457604
  13.4 3.7 copy-start.22
  14.5 3.7 copy-start.21
  15.8 96.4 %copy-start.11 = (bf16[256,32,56]{0,2,1:T(8,128)(2,1)}, bf16[256,32,56]{0,2,1:T(8,128)(2,1)S(1)}, u32[]{:S(2)}) copy-start(bf16[256,32,56]{0,2,1:T(8,128)(2,1)S(1)} %pad.39) | copy-start | bytes 2752516
  15.8 96.4 %copy-start.33 = (f32[2,800]{1,0:T(2,128)S(1)}, f32[2,800]{1,0:T(2,128)}, u32[]{:S(2)}) copy-start(f32[2,800]{1,0:T(2,128)} %param.20) | copy-start | bytes 19204
  119.7 0.9 copy-start.24
  119.7 1.0 copy-start.5
  228.7 1.1 copy-start.4
  228.7 1.1 copy-start.7
  229.6 0.8 copy-start.38
  230.4 5.7 copy-start.25
  230.4 5.7 copy-start.34
  233.6 6.5 %copy-start.8 = (f32[256,800]{1,0:T(8,128)}, f32[256,800]{1,0:T(8,128)S(1)}, u32[]{:S(2)}) copy-start(f32[256,800]{1,0:T(8,128)S(1)} %get-tuple-element.135.mid) | copy-start | bytes 2457604
  238.9 3.8 copy-start.18
  240.0 3.7 copy-start.32
  240.0 4.3 copy-start.37
  293.2 4.7 copy-start.9
  301.2 3.1 copy-start.3
  462.5 2.2 copy-start.10
  466.4 3.5 copy-start.2
  475.4 6.3 %copy-start.26 = (f32[800]{0:T(1024)S(1)}, f32[800]{0:T(1024)}, u32[]{:S(2)}) copy-start(f32[800]{0:T(1024)} %param.17) | copy-start | bytes 9604
  476.7 5.7 copy-start.16
  496.3 8.1 %copy-start.12 = (bf16[256,32,56]{0,2,1:T(8,128)(2,1)S(1)}, bf16[256,32,56]{0,2,1:T(8,128)(2,1)}, u32[]{:S(2)}) copy-start(bf16[256,32,56]{0,2,1:T(8,128)(2,1)} %copy-done.11) | copy-start | bytes 2752516
  502.7 1.7 copy-start.1
  509.1 3.3 copy-start
  586.5 6.0 copy-start.35
  586.5 6.0 copy-start.36
  586.5 8.4 %copy-start.17 = (f32[256,16,50]{0,2,1:T(8,128)S(1)}, f32[256,16,50]{0,2,1:T(8,128)}, u32[]{:S(2)}) copy-start(f32[256,16,50]{0,2,1:T(8,128)} %get-tuple-element.121) | copy-start | bytes 2457604
  590.1 7.2 %copy-start.14 = (f32[2,128,800]{2,1,0:T(8,128)S(1)}, f32[2,128,800]{2,1,0:T(8,128)}, u32[]{:S(2)}) copy-start(f32[2,128,800]{2,1,0:T(8,128)} %copy-done.13) | copy-start | bytes 2457604
  590.1 7.2 %copy-start.15 = (f32[256,800]{1,0:T(8,128)S(1)}, f32[256,800]{1,0:T(8,128)}, u32[]{:S(2)}) copy-start(f32[256,800]{1,0:T(8,128)} %get-tuple-element.120) | copy-start | bytes 2457604
  590.1 7.2 %copy-start.27 = (f32[800]{0:T(1024)S(1)}, f32[800]{0:T(1024)}, u32[]{:S(2)}) copy-start(f32[800]{0:T(1024)} %param.17) | copy-start | bytes 9604
  590.2 7.2 %copy-start.29 = (f32[256]{0:T(256)S(1)}, f32[256]{0:T(256)}, u32[]{:S(2)}) copy-start(f32[256]{0:T(256)} %copy-done.28) | copy-start | bytes 3076
  590.2 7.2 %copy-start.31 = (f32[256]{0:T(256)S(1)}, f32[256]{0:T(256)}, u32[]{:S(2)}) copy-start(f32[256]{0:T(256)} %copy-done.30) | copy-start | bytes 3076
  597.4 3.3 copy-start.23
  597.7 3.6 copy-start.20
  597.8 4.5 copy-start.19

commit v3 on v2

--- a/solution.py
+++ b/solution.py
@@ -135,190 +135,168 @@
         out.append((p,min(p+n*128,W))); p+=n*128
     assert out[-1][1]==W,(name,out)
     return out
-def scatter_steps(names,widths,src,vec,out,vout,scr):
-    n=len(names); hasvec=vec is not None
-    it=iter(scr)
-    bufs=[[ [next(it) for _ in range(14)] for p in range(3)] for t in range(n)]
-    vbuf=[next(it) for _ in range(3)] if hasvec else None
-    ss,rs,ls=next(it),next(it),next(it)
+def scatter_steps(nm,width,src,out,bufs,sems):
+    ss,rs,ls=sems
     z,y,x,c=coords(); xl=x%2; xh=x//2
     me={"x":x,"y":y,"z":z}
     cnt=[0]; lcnt=[0]; allc=[]
-    def mk(s,d,ax,k):
+    def mk(s,d,ax,k,keep=True):
         i=cnt[0]; cnt[0]+=1
         cp=pltpu.make_async_remote_copy(src_ref=s,dst_ref=d,send_sem=ss.at[i],recv_sem=rs.at[i],device_id=peer_of(ax,k),device_id_type=MESH)
-        allc.append(cp); return cp
+        if keep: allc.append(cp)
+        return cp
     def mkload(s,d):
         i=lcnt[0]; lcnt[0]+=1
         return pltpu.make_async_copy(s,d,ls.at[i])
-    cut=[rcuts(nm,w) for nm,w in zip(names,widths)]
-    items=[(t,p) for t in range(n) for p in range(3)]
+    cut=rcuts(nm,width)
     f32=lambda a:a.astype(jnp.float32)
-    def Dh(t,p,k,i=None):
-        a,b=cut[t][p]; s=slice(None) if i is None else pl.ds(2*i,2)
+    def D(p,k,i=None):
+        a,b=cut[p]; s=slice(None) if i is None else pl.ds(2*i,2)
         if p==0:
             h=(b-a)//2
-            return src[t].at[s,:,k%2,:,pl.ds(pl.multiple_of(a+(k//2)*h,128),h)]
-        if p==1: return src[t].at[s,k,:,:,pl.ds(a,b-a)]
-        return src[t].at[k,s,:,:,pl.ds(a,b-a)]
+            return src.at[s,:,k%2,:,pl.ds(pl.multiple_of(a+(k//2)*h,128),h)]
+        if p==1: return src.at[s,k,:,:,pl.ds(a,b-a)]
+        return src.at[k,s,:,:,pl.ds(a,b-a)]
+    M=(4,2,2); P3=(0,1,2)
     ld={}; R={}
-    for t,p in items:
-        own,bp,bm,rlp,rlm,rm,rp,rl2p,rl2m,rm2,rp2,out2,r3,r4=bufs[t][p]
+    for p in P3:
+        own,rlp,rlm,rm,rp,rl2p,rl2m,rm2,rp2,out2,r3,r4=bufs[p]
         k=me[AX[p][0]]; ax=AX[p][0]
-        ld[t,p]=[mkload(Dh(t,p,(k+1)%4,0),bp),mkload(Dh(t,p,(k+3)%4,1),bm),mkload(Dh(t,p,k),own)]
-        R[t,p,"a"]=[mk(Dh(t,p,(k+2)%4,0),rlp,ax,1),mk(Dh(t,p,(k+2)%4,1),rlm,ax,3)]
-        R[t,p,"b"]=[mk(Dh(t,p,(k+1)%4,1),rm.at[pl.ds(2,2)],ax,1),mk(Dh(t,p,(k+3)%4,0),rp.at[pl.ds(0,2)],ax,3),
-                    mk(bp,rm.at[pl.ds(0,2)],ax,1),mk(bm,rp.at[pl.ds(2,2)],ax,3)]
-        m=4 if p==0 else 2; hm=m//2
+        bp=own.at[pl.ds(0,2)]; bm=own.at[pl.ds(2,2)]
+        ld[p]=[mkload(D(p,(k+1)%4,0),bp),mkload(D(p,(k+3)%4,1),bm),mkload(D(p,k),own)]
+        R[p,"a"]=[mk(D(p,(k+2)%4,0),rlp,ax,1),mk(D(p,(k+2)%4,1),rlm,ax,3)]
+        R[p,"b"]=[mk(D(p,(k+1)%4,1),rm.at[pl.ds(2,2)],ax,1),mk(D(p,(k+3)%4,0),rp.at[pl.ds(0,2)],ax,3),
+                  mk(bp,rm.at[pl.ds(0,2)],ax,1,False),mk(bm,rp.at[pl.ds(2,2)],ax,3,False)]
+        m=M[p]; hm=m//2
         ax=AX[p][1]; k=me[ax]
         L=pl.ds(0,hm); H=pl.ds(hm,hm)
-        R[t,p,"c"]=[mk(own.at[(k+2)%4,L],rl2p,ax,1),mk(own.at[(k+2)%4,H],rl2m,ax,3)]
-        R[t,p,"d"]=[mk(own.at[(k+1)%4,H],rm2.at[H],ax,1),mk(own.at[(k+3)%4,L],rp2.at[L],ax,3),
-                    mk(own.at[(k+1)%4,L],rm2.at[L],ax,1),mk(own.at[(k+3)%4,H],rp2.at[H],ax,3)]
+        R[p,"c"]=[mk(own.at[(k+2)%4,L],rl2p,ax,1),mk(own.at[(k+2)%4,H],rl2m,ax,3)]
+        R[p,"d"]=[mk(own.at[(k+1)%4,H],rm2.at[H],ax,1),mk(own.at[(k+3)%4,L],rp2.at[L],ax,3),
+                  mk(own.at[(k+1)%4,L],rm2.at[L],ax,1),mk(own.at[(k+3)%4,H],rp2.at[H],ax,3)]
         ax=AX[p][2]; k=me[ax]; q=4 if p==0 else 2
-        R[t,p,"e"]=[mk(out2.at[(k+j)%q],r3.at[j-1],ax,j) for j in (1,2,3)]
-        if p==0: R[t,p,"f"]=[mk(r4.at[xh],r4.at[xh],"x",2)]
-    if hasvec:
-        for st in range(3):
-            ax="xyz"[st]; b=vbuf[st]
-            R["v",st]=[mk(b.at[me[ax]],b.at[me[ax]],ax,k) for k in (1,2,3)]
-    def vgo(st,v):
-        vbuf[st][pl.ds(me["xyz"[st]],1)]=v[None]
-        for cp in R["v",st]: cp.start()
-    def vsum(st):
-        for cp in R["v",st]: cp.wait_recv()
-        b=vbuf[st]
-        return (b[0]+b[1])+(b[2]+b[3])
+        R[p,"e"]=[mk(out2.at[(k+j)%q],r3.at[j-1],ax,j) for j in (1,2,3)]
+        if p==0: R[p,"f"]=[mk(r4.at[xh],r4.at[xh],"x",2)]
     def addin(dst,other,cntn,f,g):
         def body(i,_):
             dst[f(i)]=(f32(dst[f(i)])+f32(other[g(i)])).astype(jnp.bfloat16)
             return 0
         lax.fori_loop(0,cntn,body,0)
     def first():
-        for t,p in items:
-            for cp in ld[t,p]: cp.start()
-        if hasvec: vgo(0,vec[...])
-        for t,p in items:
-            for cp in R[t,p,"a"]: cp.start()
-        for t,p in items:
-            for cp in R[t,p,"b"][:2]: cp.start()
-    def relay(t,p):
+        for p in P3:
+            for cp in ld[p][:2]: cp.start()
+        for p in P3:
+            for cp in R[p,"a"]: cp.start()
+        for p in P3:
+            for cp in R[p,"b"][:2]: cp.start()
+    def relay(p):
         def f():
-            own,bp,bm,rlp,rlm=bufs[t][p][:5]
-            m=4 if p==0 else 2
-            ix=lambda i:(i//m,i%m)
-            ld[t,p][0].wait(); R[t,p,"a"][0].wait_recv(); addin(bp,rlp,2*m,ix,ix); R[t,p,"b"][2].start()
-            ld[t,p][1].wait(); R[t,p,"a"][1].wait_recv(); addin(bm,rlm,2*m,ix,ix); R[t,p,"b"][3].start()
+            own,rlp,rlm=bufs[p][:3]
+            m=M[p]
+            ld[p][0].wait(); R[p,"a"][0].wait_recv(); addin(own,rlp,2*m,lambda i:(i//m,i%m),lambda i:(i//m,i%m)); R[p,"b"][2].start()
+            ld[p][1].wait(); R[p,"a"][1].wait_recv(); addin(own,rlm,2*m,lambda i:(2+i//m,i%m),lambda i:(i//m,i%m)); R[p,"b"][3].start()
         return f
-    def sum1(t,p):
+    def reload(p):
         def f():
-            own,bp,bm,rlp,rlm,rm,rp=bufs[t][p][:7]
-            m=4 if p==0 else 2
-            ld[t,p][2].wait()
-            for cp in R[t,p,"b"]: cp.wait_recv()
+            for cp in R[p,"b"][2:]: cp.wait_send()
+            ld[p][2].start()
+        return f
+    def sum1(p):
+        def f():
+            own,rm,rp=bufs[p][0],bufs[p][3],bufs[p][4]
+            m=M[p]
+            ld[p][2].wait()
+            for cp in R[p,"b"]: cp.wait_recv()
             def body(i,_):
                 j=(i//m,i%m)
                 own[j]=(f32(own[j])+(f32(rm[j])+f32(rp[j]))).astype(jnp.bfloat16)
                 return 0
             lax.fori_loop(0,4*m,body,0)
-            for cp in R[t,p,"c"]: cp.start()
-            for cp in R[t,p,"d"][:2]: cp.start()
+            for cp in R[p,"c"]: cp.start()
+            for cp in R[p,"d"][:2]: cp.start()
         return f
-    def relay2(t,p):
+    def relay2(p):
         def f():
-            own,rl2p,rl2m=bufs[t][p][0],bufs[t][p][7],bufs[t][p][8]
-            m=4 if p==0 else 2; hm=m//2; k=me[AX[p][1]]
-            R[t,p,"c"][0].wait_recv()
+            own,rl2p,rl2m=bufs[p][0],bufs[p][5],bufs[p][6]
+            hm=M[p]//2; k=me[AX[p][1]]
+            R[p,"c"][0].wait_recv()
             addin(own,rl2p,hm,lambda i:((k+1)%4,i),lambda i:i)
-            R[t,p,"d"][2].start()
-            R[t,p,"c"][1].wait_recv()
+            R[p,"d"][2].start()
+            R[p,"c"][1].wait_recv()
             addin(own,rl2m,hm,lambda i:((k+3)%4,hm+i),lambda i:i)
-            R[t,p,"d"][3].start()
+            R[p,"d"][3].start()
         return f
-    def sum2(t,p):
+    def sum2(p):
         def f():
-            own,rm2,rp2,out2=bufs[t][p][0],bufs[t][p][9],bufs[t][p][10],bufs[t][p][11]
-            m=4 if p==0 else 2
+            own,rm2,rp2,out2=bufs[p][0],bufs[p][7],bufs[p][8],bufs[p][9]
             k=me[AX[p][1]]
-            for cp in R[t,p,"d"]: cp.wait_recv()
+            for cp in R[p,"d"]: cp.wait_recv()
             def body(i,_):
                 out2[i]=(f32(own[k,i])+(f32(rm2[i])+f32(rp2[i]))).astype(jnp.bfloat16)
                 return 0
-            lax.fori_loop(0,m,body,0)
-            for cp in R[t,p,"e"]: cp.start()
+            lax.fori_loop(0,M[p],body,0)
+            for cp in R[p,"e"]: cp.start()
         return f
-    def last(t,p):
+    def last(p):
         def f():
-            out2,r3,r4=bufs[t][p][11:14]
-            a,b=cut[t][p]
-            for cp in R[t,p,"e"]: cp.wait_recv()
+            out2,r3,r4=bufs[p][9:12]
+            a,b=cut[p]
+            for cp in R[p,"e"]: cp.wait_recv()
             k=me[AX[p][2]] if p==0 else xl
             s=(f32(out2[k])+f32(r3[1]))+(f32(r3[0])+f32(r3[2]))
             if p==0:
                 r4[xh]=s.astype(jnp.bfloat16)
-                R[t,p,"f"][0].start()
+                R[p,"f"][0].start()
             else:
-                out[t][:,pl.ds(a,b-a)]=s
+                out[:,pl.ds(a,b-a)]=s
         return f
     def end():
-        for t in range(n):
-            a,b=cut[t][0]; h=(b-a)//2; r4=bufs[t][0][13]
-            R[t,0,"f"][0].wait_recv()
-            for j in range(2): out[t][:,pl.ds(a+j*h,h)]=f32(r4[j])
-        if hasvec: vout[...]=vsum(2)
+        a,b=cut[0]; h=(b-a)//2; r4=bufs[0][11]
+        R[0,"f"][0].wait_recv()
+        for j in range(2): out[:,pl.ds(a+j*h,h)]=f32(r4[j])
         for cp in allc: cp.wait_send()
-    stages=[[first]]+[[f(t,p) for t,p in items] for f in (relay,sum1,relay2,sum2)]+[[last(t,p) for t,p in sorted(items,key=lambda q:q[1])],[end]]
-    if hasvec:
-        stages[2].insert(0,lambda:vgo(1,vsum(0)))
-        stages[4].insert(0,lambda:vgo(2,vsum(1)))
-    return stages
-def staggered(chains,by=2):
-    order=[]
-    for tick in range(7+by*(len(chains)-1)):
-        for i,ch in enumerate(chains):
-            if 0<=tick-by*i<7: order.append(ch[tick-by*i])
-    return order
-def scatter_chains(names,widths,src,vec,out,vout,scr):
-    hv=vec is not None; chains=[]; at=0
-    for t in range(len(names)):
-        size=42+3*(hv and t==0)+3
-        chains.append(scatter_steps(names[t],[widths[t]],[src[t]],vec if t==0 else None,[out[t]],vout if t==0 else None,scr[at:at+size]))
-        at+=size
-    return chains
-def scatter_scratch(names,parts,vec=None):
+    return [[first]]+[[f(p) for p in P3] for f in (relay,reload,sum1,relay2,sum2,last)]+[[end]]
+STAGES=8
+def staggered(chains,by):
+    return [[f for i,ch in enumerate(chains) if 0<=tick-by*i<STAGES for f in ch[tick-by*i]] for tick in range(STAGES+by*(len(chains)-1))]
+def scatter_bufs(nm,r,w):
     scr=[]
-    for t,nm in enumerate(names):
-        r,w=parts[t].shape[3:]; hv=vec is not None and t==0
-        for p,(a,b) in enumerate(rcuts(nm,w)):
-            m=4 if p==0 else 2; v=(b-a)//2 if p==0 else b-a; hm=m//2
-            B=lambda *s:pltpu.VMEM(s+(r,v),jnp.bfloat16)
-            scr+=[B(4,m),B(2,m),B(2,m),B(2,m),B(2,m),B(4,m),B(4,m),B(hm),B(hm),B(m),B(m),B(m),B(3),B(2) if p==0 else pltpu.VMEM((8,128),jnp.bfloat16)]
-        if hv: scr+=[pltpu.VMEM((4,)+vec.shape,jnp.float32)]*3
-        nd=46+9*hv
-        scr+=[pltpu.SemaphoreType.DMA((nd,)),pltpu.SemaphoreType.DMA((nd,)),pltpu.SemaphoreType.DMA((9,))]
+    for p,(a,b) in enumerate(rcuts(nm,w)):
+        m=4 if p==0 else 2; v=(b-a)//2 if p==0 else b-a; hm=m//2
+        B=lambda *s:pltpu.VMEM(s+(r,v),jnp.bfloat16)
+        scr+=[B(4,m),B(2,m),B(2,m),B(4,m),B(4,m),B(hm),B(hm),B(m),B(m),B(m),B(3),B(2) if p==0 else pltpu.VMEM((8,128),jnp.bfloat16)]
     return scr
-def scatter_kernel(names,widths,hasvec,*refs):
-    n=len(names); h=int(hasvec)
-    chains=scatter_chains(names,widths,refs[:n],refs[n] if h else None,refs[n+h:2*n+h],refs[2*n+h] if h else None,refs[2*(n+h):])
-    greet(RPEERS)
-    for stage in staggered(chains):
-        for f in stage: f()
-def scatter_shapes(parts,vec=None):
-    return tuple(jax.ShapeDtypeStruct(a.shape[3:],jnp.float32) for a in parts)+((jax.ShapeDtypeStruct(vec.shape,jnp.float32),) if vec is not None else ())
-def reduce_scatter(names,parts,vec=None,cid=2):
-    n=len(names); hv=vec is not None
-    A=pl.BlockSpec(memory_space=pl.ANY); V=pl.BlockSpec(memory_space=pltpu.VMEM)
-    return pl.pallas_call(functools.partial(scatter_kernel,names,[a.shape[4] for a in parts],hv),
-      out_shape=scatter_shapes(parts,vec),
-      in_specs=[A]*n+[V]*hv,out_specs=tuple([V]*(n+hv)),scratch_shapes=scatter_scratch(names,parts,vec),
-      compiler_params=pltpu.CompilerParams(collective_id=cid,has_side_effects=True,vmem_limit_bytes=58<<20))(*parts,*([vec] if hv else []))
-
-
-HD=64; LEN=4096; NEG=-1e30; ROWS=32
+def scatter_sems():
+    return [pltpu.SemaphoreType.DMA((46,)),pltpu.SemaphoreType.DMA((46,)),pltpu.SemaphoreType.DMA((9,))]
+def by_part(refs):
+    return [refs[12*p:12*p+12] for p in range(3)]
+def narrowed(bufs,nm,w):
+    out=[]
+    for p,(a,b) in enumerate(rcuts(nm,w)):
+        v=(b-a)//2 if p==0 else b-a
+        out.append([ref if ref.shape[-1]==v or ref.shape==(8,128) else ref.at[(slice(None),)*(len(ref.shape)-1)+(pl.ds(0,v),)] for ref in bufs[p]])
+    return out
+def vector_steps(vbuf,sems):
+    z,y,x,c=coords(); me=(x,y,z)
+    ss,rs=sems
+    R=[[pltpu.make_async_remote_copy(src_ref=vbuf[st].at[me[st]],dst_ref=vbuf[st].at[me[st]],send_sem=ss.at[3*st+k-1],recv_sem=rs.at[3*st+k-1],device_id=peer_of("xyz"[st],k),device_id_type=MESH) for k in (1,2,3)] for st in range(3)]
+    def go(st,v):
+        vbuf[st][pl.ds(me[st],1)]=v[None]
+        for cp in R[st]: cp.start()
+    def total(st):
+        for cp in R[st]: cp.wait_recv()
+        b=vbuf[st]
+        return (b[0]+b[1])+(b[2]+b[3])
+    def end():
+        for l in R:
+            for cp in l: cp.wait_send()
+    return go,total,end
+
+
+TT=256; KH=896; HD=64; LEN=4096; NEG=-1e30; ROWS=32
 FQ,FK,BQ,BK=1024,1024,512,512
 def dot(a,b): return lax.dot_general(a,b,(((1,),(0,)),((),())),preferred_element_type=jnp.float32)
 def dot_nt(a,b): return lax.dot_general(a,b,(((1,),(1,)),((),())),preferred_element_type=jnp.float32)
-def group_barrier(d,r,c,across):
+def group_greet(d,r,c,across):
     bar=pltpu.get_barrier_semaphore()
     for rr in across: pl.semaphore_signal(bar,inc=1,device_id=(1-d,rr,c),device_id_type=MESH)
     def body(i,_):
@@ -327,7 +305,8 @@
             pl.semaphore_signal(bar,inc=1,device_id=(d,i//2,i%2),device_id_type=MESH)
         return 0
     lax.fori_loop(0,2*ROWS,body,0)
-    pl.semaphore_wait(bar,2*ROWS-1+len(across))
+def group_wait(across):
+    pl.semaphore_wait(pltpu.get_barrier_semaphore(),2*ROWS-1+across)
 def push(src,dst,send_sem,recv_sem,same,target):
     @pl.when(same)
     def _():
@@ -350,10 +329,12 @@
     qkv,knt,obf,s_in,s_out,r_in,r_out,l_sem=refs[6+2*n:14+2*n]
     steps=gather_chains(names,widths,refs[2:2+n],refs[6+n:6+2*n],refs[14+2*n:])
     d=lax.axis_index("dev"); r=lax.axis_index("row"); c=lax.axis_index("col")
-    group_barrier(d,r,c,[r+1-2*(r%2)])
+    group_greet(d,r,c,[r+1-2*(r%2)])
+    group_wait(1)
     lanes=pl.ds(pl.multiple_of(r*128,128),128)
     def full(fn):
-        def body(i,_):
+        def body(k,_):
+            i=(r+k)%24
             fn(qkv_in.at[i%2,:,i//2+c],qkv.at[:,:,lanes],s_in.at[i],r_in,i==r,(d,i,c))
             return 0
         lax.fori_loop(0,24,body,0)
@@ -367,7 +348,7 @@
     head=r//2+13*c; seq=r%2
     def outs(qi,fn):
         def body(i,_):
-            rr=qi*(FQ//128)+i//2; cc=i%2
+            rr=qi*(FQ//128)+(r+i//2)%(FQ//128); cc=i%2
             fn(obf.at[:,pl.ds(pl.multiple_of(rr*128,128),128)],o_recv.at[seq,head],s_out.at[rr*2+cc],r_out,(rr==r)&(cc==c),(d,rr,cc))
             return 0
         lax.fori_loop(0,FQ//64,body,0)
@@ -420,17 +401,41 @@
         for qi in range(LEN//FQ): outs(qi,pushed)
     full(pushed); halves(pushed)
     arrived(o_recv,r_out)
-def attn_bwd_kernel(names,widths,*refs):
+BWD_AT=((0,1),(1,2),(3,3),(5,4),(7,5))
+KQ=2432
+def back_kernel(names,widths,*refs):
+    it=iter(refs)
+    take=lambda n:[next(it) for _ in range(n)]
     n=len(names)
-    do_in,qkv,oT,start,lse=refs[:5]
-    d_recv=refs[5+n]
-    doT,knt,vnt,dqa,delta,dout,s_in,s_out,r_in,r_out=refs[6+2*n:16+2*n]
-    order=staggered(scatter_chains(names,widths,refs[5:5+n],None,refs[6+n:6+2*n],None,refs[16+2*n:]))
+    do_in,qkv,oT,start,lse,h1t,normt,vec_in,wq=take(9)
+    parts=take(n)
+    part_q,dh1t,sum_q,vec_out=take(4)
+    sums=take(n)
+    doT,knt,vnt,dqa,delta,dout,dq,stage,wblk,dh_send,dh_recv=take(11)
+    vbuf=take(3); vtmp=next(it)
+    s_in,s_out,r_in,r_out,q_sem,w_sem,x_sem,free=take(8)
+    v_sems=take(2)
+    bufs=[by_part(take(36)) for _ in range(n)]
+    chains=[scatter_steps(names[t],widths[t],parts[t],sums[t],bufs[t],take(3)) for t in range(n)]
+    chain_q=scatter_steps("q",KQ,part_q,sum_q,narrowed(bufs[0],"q",KQ),take(3))
+    ticks=staggered(chains,1)
+    v_go,v_total,v_end=vector_steps(vbuf,v_sems)
     d=lax.axis_index("dev"); r=lax.axis_index("row"); c=lax.axis_index("col")
-    group_barrier(d,r,c,[r+1-2*(r%2),r])
+    item=(r<24)|((c==0)&(r<26))
+    group_greet(d,r,c,[r+1-2*(r%2),r])
+    @pl.when(item)
+    def _():
+        for a in range(LEN//512):
+            sl=pl.ds(a*512,512)
+            knt[sl,:]=qkv[1,:,sl].T
+            vnt[sl,:]=qkv[2,:,sl].T
+        dqa[...]=jnp.zeros_like(dqa)
+    stage[...]=jnp.zeros_like(stage)
+    group_wait(2)
     lanes=pl.ds(pl.multiple_of(r*128,128),128)
     def full(fn):
-        def body(i,_):
+        def body(k,_):
+            i=(r+k)%24
             fn(do_in.at[i%2,i//2+c],doT.at[:,lanes],s_in.at[i],r_in,i==r,(d,i,c))
             return 0
         lax.fori_loop(0,24,body,0)
@@ -439,30 +444,27 @@
         for s in range(2):
             fn(do_in.at[s,12*(1-c),rows],doT.at[rows,lanes],s_in.at[24+s],r_in,(r==24+s)&(c==0),(d,24+s,0))
     full(push); halves(push)
-    order[0][0]()
-    item=(r<24)|((c==0)&(r<26))
+    def tick(k):
+        for f in ticks[k]: f()
+    tick(0)
     def outs(fn):
+        seq=pl.ds(pl.multiple_of((r%2)*128,128),128)
         @pl.when(r<24)
         def _():
-            def body(i,_):
-                fn(dout.at[:,:,pl.ds(pl.multiple_of(i*128,128),128)],d_recv.at[:,(r%2)*13+r//2+c],s_out.at[i],r_out,i==r,(d,i,c))
+            def body(k,_):
+                i=(r+k)%ROWS
+                fn(dout.at[:,:,pl.ds(pl.multiple_of(i*128,128),128)],dq.at[:,pl.ds(pl.multiple_of(64*(r//2)+32*c,32),64),seq],s_out.at[i],r_out,i==r,(d,i,c))
                 return 0
             lax.fori_loop(0,ROWS,body,0)
         @pl.when(r>=24)
         def _():
-            def body(i,_):
-                rr=i//2; cc=i%2
-                rows=pl.ds(pl.multiple_of(32*cc,32),32)
-                fn(dout.at[:,rows,pl.ds(pl.multiple_of(rr*128,128),128)],d_recv.at[:,(r%2)*13+12*(1-cc),rows],s_out.at[i],r_out,(rr==r)&(cc==c),(d,rr,cc))
+            def body(k,_):
+                rr=(r+k//2)%ROWS; cc=k%2
+                fn(dout.at[:,pl.ds(pl.multiple_of(32*cc,32),32),pl.ds(pl.multiple_of(rr*128,128),128)],dq.at[:,pl.ds(pl.multiple_of(768*(1-cc),32),32),seq],s_out.at[2*rr+cc],r_out,(rr==r)&(cc==c),(d,rr,cc))
                 return 0
             lax.fori_loop(0,2*ROWS,body,0)
     @pl.when(item)
     def _():
-        for a in range(LEN//512):
-            sl=pl.ds(a*512,512)
-            knt[sl,:]=qkv[1,:,sl].T
-            vnt[sl,:]=qkv[2,:,sl].T
-        dqa[...]=jnp.zeros_like(dqa)
         arrived(doT,r_in)
         for a in range(LEN//512):
             sl=pl.ds(a*512,512)
@@ -494,11 +496,8 @@
             dk,dv=lax.fori_loop(kj+1,LEN//BQ,lambda qi,cr:step(qi,cr,False),carry)
             dout[1,:,ks]=dk.astype(jnp.bfloat16)
             dout[2,:,ks]=dv.astype(jnp.bfloat16)
-        at=1
-        for step,to in BWD_AT:
-            for stage in order[at:to]:
-                for f in stage: pl.when(kj==step)(f)
-            at=to
+        for step,k in BWD_AT:
+            pl.when(kj==step)(functools.partial(tick,k))
         return 0
     lax.fori_loop(0,LEN//BK,kloop,0)
     @pl.when(item)
@@ -507,11 +506,60 @@
             sl=pl.ds(a*512,512)
             dout[0,:,sl]=(dqa[:,sl]*0.125).astype(jnp.bfloat16)
         outs(push)
-    for stage in order[BWD_AT[-1][1]:]:
-        for f in stage: f()
+    for k in range(BWD_AT[-1][1]+1,STAGES): tick(k)
+    for ax,k in RPEERS: pl.semaphore_signal(free,inc=1,device_id=peer_of(ax,k),device_id_type=MESH)
+    arrived(dq,r_out)
+    grads=dq[...].reshape(2400,TT)
+    prev={}
+    for b in range(8):
+        slot=b%2
+        if b>=2: prev[slot].wait()
+        stage[slot,:,:,:,pl.ds(0,2400)]=dot_nt(h1t[pl.ds(224*b,224),:],grads).reshape(2,2,56,2400).astype(bf)
+        prev[slot]=pltpu.make_async_copy(stage.at[slot],part_q.at[b//2,pl.ds(2*(b%2),2)],q_sem.at[slot])
+        prev[slot].start()
+    partner=(d,r,1-c)
+    half=lambda base,k:wq.at[pl.ds(pl.multiple_of(base*KH+128*k,128),128)]
+    blocks=[half(1-c,k) for k in range(7)]+[half(c,k) for k in range(7)]
+    loads=[pltpu.make_async_copy(blocks[k],wblk.at[k%2],w_sem.at[k%2]) for k in range(14)]
+    loads[0].start(); loads[1].start()
+    for cp in prev.values(): cp.wait()
+    pl.semaphore_wait(free,len(RPEERS))
+    def go_q(k):
+        for f in chain_q[k]: f()
+    go_q(0)
+    swap=pltpu.make_async_remote_copy(src_ref=dh_send,dst_ref=dh_recv,send_sem=x_sem.at[0],recv_sem=x_sem.at[1],device_id=partner,device_id_type=MESH)
+    for k in range(14):
+        loads[k].wait()
+        v=dot(wblk[k%2],grads)
+        if k<7: dh_send[pl.ds(128*k,128),:]=v.astype(bf)
+        else: dh1t[pl.ds(128*(k-7),128),:]=v
+        if k<12: loads[k+2].start()
+        if k==6: swap.start()
+    go_q(1)
+    for k in range(STAGES,len(ticks)): tick(k)
+    swap.wait()
+    dh1t[...]=dh1t[...]+dh_recv[...].astype(jnp.float32)
+    def token_sums(v,precision=None):
+        return lax.dot_general(jnp.ones((8,TT),v.dtype),v,(((1,),(1,)),((),())),precision=precision,preferred_element_type=jnp.float32)[:1]
+    gain=token_sums(dh1t[...]*normt[...],lax.Precision.HIGHEST)
+    bias=token_sums(dh1t[...],lax.Precision.HIGHEST)
+    both=token_sums(grads)
+    both=jnp.concatenate((both,jnp.zeros((1,32),jnp.float32)),axis=1)
+    vtmp[pl.ds(0,40),:]=jnp.zeros((40,128),jnp.float32)
+    vtmp[pl.ds(40,vec_in.shape[0]),:]=vec_in[...]
+    for at,row,cnt in ((0,gain,7),(7,bias,7),(14,both,19)):
+        for k in range(cnt): vtmp[pl.ds(at+k,1),:]=row[:,128*k:128*k+128]
+    v_go(0,vtmp[...])
+    go_q(2); go_q(3)
+    v_go(1,v_total(0))
+    go_q(4)
+    v_go(2,v_total(1))
+    go_q(5); go_q(6)
+    vec_out[...]=v_total(2)
+    go_q(7)
+    v_end()
     pl.when(item)(lambda:outs(pushed))
     full(pushed); halves(pushed)
-    arrived(d_recv.at[:,pl.ds(0,25)],r_out)
 VM=pl.BlockSpec(memory_space=pltpu.VMEM); ANY=pl.BlockSpec(memory_space=pl.ANY)
 bf=jnp.bfloat16
 def attend(qkv,start,names,arrs,cid=1):
@@ -523,19 +571,23 @@
         pltpu.SemaphoreType.DMA((26,)),pltpu.SemaphoreType.DMA((64,)),pltpu.SemaphoreType.DMA,pltpu.SemaphoreType.DMA,pltpu.SemaphoreType.DMA]+gather_sems(n),
       compiler_params=pltpu.CompilerParams(collective_id=cid,has_side_effects=True,vmem_limit_bytes=50<<20))(qkv,start,*arrs)
     return out[0],out[1:4],out[4:]
-def attend_back(do,kept,start,names,parts,cid=3):
-    S=jax.ShapeDtypeStruct; n=len(names)
+def attend_back(do,kept,start,h1t,normt,vec,wq,names,parts,cid=2):
+    S=jax.ShapeDtypeStruct; n=len(names); f=jnp.float32; V=pltpu.VMEM; DM=pltpu.SemaphoreType.DMA
     qkv,oT,lse=kept
-    out=pl.pallas_call(functools.partial(attn_bwd_kernel,names,[a.shape[4] for a in parts]),
-      out_shape=(S((3,26,HD,128),bf),)+scatter_shapes(parts),
-      in_specs=[VM]*5+[ANY]*n,out_specs=(ANY,)+(VM,)*n,
-      scratch_shapes=[pltpu.VMEM((HD,LEN),bf),pltpu.VMEM((LEN,HD),bf),pltpu.VMEM((LEN,HD),bf),pltpu.VMEM((HD,LEN),jnp.float32),pltpu.VMEM((1,LEN),jnp.float32),pltpu.VMEM((3,HD,LEN),bf),
-        pltpu.SemaphoreType.DMA((26,)),pltpu.SemaphoreType.DMA((64,)),pltpu.SemaphoreType.DMA,pltpu.SemaphoreType.DMA]+scatter_scratch(names,parts),
-      compiler_params=pltpu.CompilerParams(collective_id=cid,has_side_effects=True,vmem_limit_bytes=60<<20))(do,qkv,oT,start,lse,*parts)
-    return out[0],out[1:]
-
-
-TT=256; WC=800; FH=3200; TF=640; KH=896
+    rows=40+vec.shape[0]
+    out=pl.pallas_call(functools.partial(back_kernel,names,[a.shape[4] for a in parts]),
+      out_shape=(S((4,4,2,56,KQ),bf),S((KH,TT),f),S((56,KQ),f),S((rows,128),f))+tuple(S(a.shape[3:],f) for a in parts),
+      in_specs=[VM]*8+[ANY]*(1+n),out_specs=(ANY,VM,VM,VM)+(VM,)*n,
+      scratch_shapes=[V((HD,LEN),bf),V((LEN,HD),bf),V((LEN,HD),bf),V((HD,LEN),f),V((1,LEN),f),V((3,HD,LEN),bf),
+        V((3,800,TT),bf),V((2,2,2,56,KQ),bf),V((2,128,2400),bf),V((KH,TT),bf),V((KH,TT),bf)]+[V((4,rows,128),f)]*3+[V((rows,128),f)]+
+        [DM((26,)),DM((64,)),DM,DM,DM((2,)),DM((2,)),DM((2,)),pltpu.SemaphoreType.REGULAR,DM((9,)),DM((9,))]+
+        sum([scatter_bufs(nm,*a.shape[3:]) for nm,a in zip(names,parts)],[])+scatter_sems()*(n+1),
+      compiler_params=pltpu.CompilerParams(collective_id=cid,has_side_effects=True,vmem_limit_bytes=VMEM_BACK))(do,qkv,oT,start,lse,h1t,normt,vec,wq,*parts)
+    return out[1],out[2],out[3],out[4:]
+VMEM_BACK=62<<20
+
+
+WC=800; FH=3200; TF=640
 GC=0.7978845608028654
 def dot_tn(a,b): return lax.dot_general(a,b,(((0,),(0,)),((),())),preferred_element_type=jnp.float32)
 def mlp_kernel(h2,we,eb,wc,mid,cb,g,result,part_c,part_e,dh2,dsum,
@@ -767,62 +819,51 @@
     part_out = outer(jnp.transpose(rows_attn, (0, 2, 1)).reshape(row_total, KP), grad_attn)
     grad_mixed = unpad_features(pair_dot(grad_attn, weight_out, 5).astype(jnp.bfloat16))
     grad_mixed = jnp.transpose(grad_mixed.reshape(seqs, block_len, width), (0, 2, 1))
-    grad_slots, (sum_contract, sum_expand) = attend_back(
+    sums_rest = (
+        jnp.sum(grad_attn.astype(jnp.float32), axis=0),
+        jnp.sum(grad_two * normed_two, axis=0),
+        jnp.sum(grad_two, axis=0),
+        jnp.sum(grad_float, axis=0),
+        expand_sums[0],
+    )
+    grad_one, sum_qkv, vector, (sum_expand, sum_contract, sum_out) = attend_back(
         head_slots(grad_mixed),
         kept,
         start,
-        "ce",
-        (part_contract.reshape(4, 4, 2, 200, width), part_expand.reshape(4, 4, 2, 56, 4 * width)),
+        rows_one.T,
+        jnp.pad(normed_one.reshape(row_total, 16, 50), ((0, 0), (0, 0), (0, 6))).reshape(row_total, KH).T,
+        jnp.concatenate(sums_rest).reshape(50, 128),
+        weight_qkv,
+        "eco",
+        (
+            part_expand.reshape(4, 4, 2, 56, 4 * width),
+            part_contract.reshape(4, 4, 2, 200, width),
+            part_out.reshape(4, 4, 2, 56, width),
+        ),
         2,
     )
-    grad_qkv = lax.dynamic_slice_in_dim(
-        grad_slots.reshape(3, seqs, 13 * HD, block_len), 32 * col, width, 2
-    )
-    grad_rows = jnp.transpose(grad_qkv, (1, 3, 0, 2)).reshape(row_total, 3 * width)
-    part_qkv = outer(rows_one, grad_rows)
-    grad_one = unpad_features(pair_dot(grad_rows, weight_qkv, 6))
+    grad_one = unpad_features(grad_one.T)
     grad_input = grad_middle + norm_backward(grad_one, normed_one, recip_one, first_gain)
     gradient_tokens = grad_input.astype(jnp.bfloat16).reshape(tokens.shape)
-    qkv_sums = jnp.sum(grad_qkv.astype(jnp.float32), axis=(1, 3))
-    pieces = (
-        jnp.sum(grad_one * normed_one, axis=0),
-        jnp.sum(grad_one, axis=0),
-        qkv_sums[0],
-        qkv_sums[2],
-        jnp.sum(grad_attn.astype(jnp.float32), axis=0),
-        jnp.sum(grad_two * normed_two, axis=0),
-        jnp.sum(grad_two, axis=0),
-        expand_sums[0],
-        jnp.sum(grad_float, axis=0),
-    )
-    vector = jnp.concatenate(pieces + (jnp.zeros((640,), jnp.float32),)).reshape(80, 128)
-    sum_qkv, sum_out, vector = reduce_scatter(
-        "qo",
-        (part_qkv.reshape(4, 4, 2, 56, 3 * width), part_out.reshape(4, 4, 2, 56, width)),
-        vector,
-        3,
-    )
-    vector = vector.reshape(-1)
-    sums = []
-    at = 0
-    for piece in pieces:
-        sums.append(vector[at : at + piece.shape[0]])
-        at += piece.shape[0]
+    first = unpad_features(vector[:14].reshape(2, KH))
+    qkv_sums = vector[14:33].reshape(-1)[: 3 * width].reshape(3, width)
+    rest = vector[40:].reshape(-1)
+    sums = [rest[width * k : width * (k + 1)] for k in range(4)] + [rest[4 * width :]]
     return (
         result,
         gradient_tokens,
+        first[0],
+        first[1],
+        sum_qkv[:50, : 3 * width].reshape(50, 3, width),
+        jnp.stack((qkv_sums[0], qkv_sums[2])),
+        sum_out[:50],
         sums[0],
         sums[1],
-        sum_qkv[:50].reshape(50, 3, width),
-        jnp.stack((sums[2], sums[3])),
-        sum_out[:50],
+        sums[2],
+        sum_expand[:50],
         sums[4],
-        sums[5],
-        sums[6],
-        sum_expand[:50],
-        sums[7],
         sum_contract,
-        sums[8],
+        sums[3],
     )
 
 

time: 612 us -> 556 us (0.908)
  Pallas kernels: 489 us -> 454 us
  local copies, waits for them, and re-layouts: 65 us -> 49.7 us
  other arithmetic: 23 us -> 15.2 us
    pallas_call x2 -> x1, Pallas kernels: 226 us -> 203 us  [attend_back(): pl.pallas_call(functools.partial(back_kernel, names, [a.shape[4] for a in...]
    unnamed x89 -> x61, local copies, waits for them, and re-layouts: 19 us -> 12.2 us
    reduce_sum x2 -> x1, other arithmetic: 9.11 us -> 2.28 us  [norm_backward(): jnp.sum(scaled, axis=1)]
where the time goes in v3:
time: 556 us; the launch traced here: 547 us
  Pallas kernels  454 us (82%)
  local copies, waits for them, and re-layouts  49.7 us (9%)
  blocking collectives  16.7 us (3%)
  other arithmetic  15.2 us (3%)
  matrix products  10.2 us (2%)
    pallas_call x1, Pallas kernels, attend_back(): pl.pallas_call(functools.partial(back_kernel, names, [a.shape[4] for a in...  203 us
    pallas_call x1, Pallas kernels, attend(): pl.pallas_call(functools.partial(attn_fwd_kernel, names, [a.shape[1] for...  106 us
    pallas_call x1, Pallas kernels, gather(): pl.pallas_call(functools.partial(gather_kernel, names, [a.shape[1] for a...  93.2 us
    pallas_call x1, Pallas kernels, mlp(): pl.pallas_call(mlp_kernel, out_shape=(S((TT, WC), bf), S((6400, WC), bf),...  46.7 us
    unnamed x61, local copies, waits for them, and re-layouts  12.2 us

profile of v3, /device:TPU:0, one launch (start us, length us, event | category | flops | bytes accessed | tf_op | source)
XLA Modules:
  0.0 547.3 jit_solution(7085305538548247350)
XLA Ops:
  0.7 0.8 constant_dynamic-slice_fusion
  1.4 1.2 constant_dynamic-slice_fusion.1
  2.6 1.5 compare_select_fusion
  5.0 1.1 convert_reduce_fusion.2
  6.1 2.5 all-reduce.14
  8.6 1.2 copy.61
  9.8 0.9 add_convert_fusion.2
  10.9 2.4 all_gather.6
  13.8 1.2 copy.63
  15.0 0.3 reshape.229
  15.4 0.7 pad.44.refs_0_
  16.1 1.7 pad.45.refs_1_
  17.8 93.2 %shard_map.254 = (bf16[4,4,2,56,2400]{4,3,2,1,0:T(8,128)(2,1)}, bf16[4,4,2,56,3200]{4,3,2,1,0:T(8,128)(2,1)}) custom-call(bf16[56,2400]{1,0:T(8,128)(2,1)} %pad.44.refs_0_, bf16[56,3200]{1,0:T(8,128)(2,1)} %pad.45.refs_1_), custom_call_target="tpu_custom_call" | custom-call | tf_op jit(solution)/shard_map/pallas_call | solution.py:122
  111.1 0.7 concatenate.9
  111.8 7.1 %fusion = bf16[2,128,2400]{1,2,0:T(8,128)(2,1)S(1)} fusion(bf16[1792,2400,1]{1,0,2:T(8,128)(2,1)} %bitcast.91, f32[2400]{0:T(1024)} %concatenate.9, bf16[2,128,1792]{1,0,2:T(2,128)(2,1)S(1)} %reshape_reshape.9), kind=kOutput, calls=%fused_computation.1 | convolution fusion | flops 2203238400 | bytes 10757504 | tf_op jit(solution)/shard_map/dm,snd->smn/dot_general | solution.py:771
  119.2 106.3 %shard_map.255 = (bf16[2,25,64,128]{3,2,1,0:T(8,128)(2,1)S(1)}, bf16[3,64,4096]{2,1,0:T(8,128)(2,1)}, f32[64,4096]{1,0:T(8,128)S(1)}, f32[1,4096]{1,0:T(1,128)S(...) custom-call(bf16[2,3,13,64,128]{4,3,2,1,0:T(8,128)(2,1)S(1)} %bitcast.82, ...), custom_call_target="tpu_custom_call" | custom-call | tf_op jit(solution)/shard_map/pallas_call | solution.py:567
  225.6 0.8 copy.65
  226.7 0.5 copy.67
  227.2 3.2 fusion.4
  230.4 2.5 all-reduce.13
  233.1 0.9 copy.69
  234.1 4.2 all_gather.7
  238.3 2.1 reshape.241
  240.4 2.2 pad.50
  242.7 2.2 copy.71.h2
  244.9 1.0 copy.70
  245.9 0.6 broadcast_in_dim.12.eb
  246.5 0.6 broadcast_in_dim.13.cb
  247.0 46.7 %shard_map.256 = (bf16[256,800]{1,0:T(8,128)(2,1)}, bf16[6400,800]{1,0:T(8,128)(2,1)}, bf16[1792,3200]{1,0:T(8,128)(2,1)}, f32[256,896]{1,0:T(8,128)}, f32[1,3200]{1,0:T(1,128)}) custom-call(bf16[256,1792]{1,0:T(8,128)(2,1)} %copy.71.h2, bf16[1792,3200]{1,0:T(8,128)(2,1)} %bitcast.87, f32[1,3200]{1,0:T(1,128)} %broadcast_in_dim.12.eb, ...), custom_call_target="tpu_custom_call" | custom-call | tf_op jit(solution)/shard_map/pallas_call | solution.py:664
  293.7 2.5 copy.72
  296.3 2.2 slice_reduce_fusion.3
  298.5 2.2 reshape.248
  300.7 2.4 copy.73
  303.1 1.6 multiply_reduce_fusion.1
  304.7 2.6 all-reduce.12
  307.3 2.7 convert_reduce_fusion
  310.0 2.4 shard_map.258
  312.4 1.6 copy-done
  314.4 0.7 concatenate.11
  315.1 1.9 copy-done.1
  317.0 2.8 shard_map.257
  320.3 0.5 broadcast_select_fusion
  320.8 0.8 copy.75
  322.0 0.7 reshape.252
  322.7 1.0 pad.53
  323.7 202.8 %shard_map.259 = (bf16[4,4,2,56,2432]{4,3,2,1,0:T(8,128)(2,1)}, f32[896,256]{1,0:T(8,128)}, f32[56,2432]{1,0:T(8,128)}, f32[90,128]{1,0:T(8,128)}, f32[56,3200]{...) custom-call(bf16[2,13,64,128]{3,2,1,0:T(8,128)(2,1)} %bitcast.103, bf16[3,64,4096]{2,1,0:T(8,128)(2,1)} %get-tuple-element.40.refs_1_, ...), custom_call_target="tpu_custom_call" | custom-call | tf_op jit(solution)/shard_map/pallas_call | solution.py:578
  526.5 0.8 slice_bitcast_fusion.2
  527.3 0.6 pad_maximum_fusion
  528.0 2.3 multiply_reduce_fusion.5
  530.3 2.4 all-reduce.11
  532.8 2.2 reshape.259
  534.9 1.4 copy.78
  536.4 0.3 add_convert_fusion
  536.8 1.0 copy.80
  537.7 1.4 reshape.261
  539.2 0.9 copy.81
  540.0 0.7 fusion.5
  540.8 0.7 squeeze.18
  541.5 0.7 squeeze.19
  542.2 0.6 slice_bitcast_fusion.1
  542.8 2.0 copy.79
  544.8 0.7 copy.89
  545.4 0.9 copy.90
  546.3 0.9 copy.91
  (89 shorter events, 3.8 us)
Async XLA Ops:
  4.9 114.3 %copy-start.4 = (s32[1,4096]{1,0:T(1,128)}, s32[1,4096]{1,0:T(1,128)S(1)}, u32[]{:S(2)}) copy-start(s32[1,4096]{1,0:T(1,128)S(1)} %reduce_window_max.19.refs_1_.refs_3_) | copy-start | bytes 49156
  13.5 97.6 %copy-start.22 = (f32[2,800]{1,0:T(2,128)S(1)}, f32[2,800]{1,0:T(2,128)}, u32[]{:S(2)}) copy-start(f32[2,800]{1,0:T(2,128)} %param.20) | copy-start | bytes 19204
  13.6 97.6 %copy-start.8 = (bf16[256,32,56]{0,2,1:T(8,128)(2,1)}, bf16[256,32,56]{0,2,1:T(8,128)(2,1)S(1)}, u32[]{:S(2)}) copy-start(bf16[256,32,56]{0,2,1:T(8,128)(2,1)S(1)} %pad.43) | copy-start | bytes 2752516
  111.8 7.3 %copy-start.16 = (bf16[50,800]{1,0:T(8,128)(2,1)S(1)}, bf16[50,800]{1,0:T(8,128)(2,1)}, u32[]{:S(2)}) copy-start(bf16[50,800]{1,0:T(8,128)(2,1)} %param.21) | copy-start | bytes 240004
  111.8 7.4 %copy-start.3 = (bf16[200,800]{1,0:T(8,128)(2,1)S(1)}, bf16[200,800]{1,0:T(8,128)(2,1)}, u32[]{:S(2)}) copy-start(bf16[200,800]{1,0:T(8,128)(2,1)} %refs_2_.1) | copy-start | bytes 960004
  225.5 1.1 copy-start.2
  225.5 1.1 copy-start.5
  225.6 1.6 copy-start.25
  227.2 5.7 %copy-start.18 = (f32[800]{0:T(1024)S(1)}, f32[800]{0:T(1024)}, u32[]{:S(2)}) copy-start(f32[800]{0:T(1024)} %param.23) | copy-start | bytes 9604
  227.2 5.7 %copy-start.23 = (f32[800]{0:T(1024)S(1)}, f32[800]{0:T(1024)}, u32[]{:S(2)}) copy-start(f32[800]{0:T(1024)} %param.24) | copy-start | bytes 9604
  230.4 12.3 %copy-start.6 = (f32[256,800]{1,0:T(8,128)}, f32[256,800]{1,0:T(8,128)S(1)}, u32[]{:S(2)}) copy-start(f32[256,800]{1,0:T(8,128)S(1)} %get-tuple-element.131.mid) | copy-start | bytes 2457604
  234.1 10.8 %copy-start.11 = (bf16[2,128,800]{1,2,0:T(8,128)(2,1)S(1)}, bf16[2,128,800]{1,2,0:T(8,128)(2,1)}, u32[]{:S(2)}) copy-start(bf16[2,128,800]{1,2,0:T(8,128)(2,1)} %param.29) | copy-start | bytes 1228804
  238.3 7.6 %copy-start.20 = (f32[3200]{0:T(1024)S(1)}, f32[3200]{0:T(1024)}, u32[]{:S(2)}) copy-start(f32[3200]{0:T(1024)} %param.26) | copy-start | bytes 38404
  238.3 8.2 %copy-start.24 = (f32[800]{0:T(1024)S(1)}, f32[800]{0:T(1024)}, u32[]{:S(2)}) copy-start(f32[800]{0:T(1024)} %param.28) | copy-start | bytes 9604
  293.7 9.4 %copy-start.7 = (f32[256,800]{1,0:T(8,128)S(1)}, f32[256,800]{1,0:T(8,128)}, u32[]{:S(2)}) copy-start(f32[256,800]{1,0:T(8,128)} %copy-done.6) | copy-start | bytes 2457604
  310.0 4.1 copy-start.21
  310.0 4.2 copy-start.12
  312.4 1.6 copy-start
  315.1 1.9 copy-start.1
  319.8 1.8 copy-start.9
  323.7 204.3 %copy-start.19 = (f32[800]{0:T(1024)S(1)}, f32[800]{0:T(1024)}, u32[]{:S(2)}) copy-start(f32[800]{0:T(1024)} %param.17) | copy-start | bytes 9604
  526.4 9.9 %copy-start.10 = (f32[256,800]{1,0:T(8,128)S(1)}, f32[256,800]{1,0:T(8,128)}, u32[]{:S(2)}) copy-start(f32[256,800]{1,0:T(8,128)} %get-tuple-element.116) | copy-start | bytes 2457604
  536.4 3.6 copy-start.17
  536.4 8.4 %copy-start.15 = (f32[56,800]{1,0:T(8,128)S(1)}, f32[56,800]{1,0:T(8,128)}, u32[]{:S(2)}) copy-start(f32[56,800]{1,0:T(8,128)} %get-tuple-element.49) | copy-start | bytes 537604
  536.7 8.7 %copy-start.14 = (f32[56,3200]{1,0:T(8,128)S(1)}, f32[56,3200]{1,0:T(8,128)}, u32[]{:S(2)}) copy-start(f32[56,3200]{1,0:T(8,128)} %get-tuple-element.50) | copy-start | bytes 2150404
  536.8 9.5 %copy-start.13 = (f32[200,800]{1,0:T(8,128)S(1)}, f32[200,800]{1,0:T(8,128)}, u32[]{:S(2)}) copy-start(f32[200,800]{1,0:T(8,128)} %get-tuple-element.160) | copy-start | bytes 1920004

commit v4 on v3

--- a/solution.py
+++ b/solution.py
@@ -34,7 +34,7 @@
     out=[];p=0
     for n in SPLIT[name]:
         out.append((p,min(p+n*128,W))); p+=n*128
-    assert out[-1][1]==W,(name,out)
+    assert out[-1][1]==W
     return out
 def gather_steps(names,widths,src,dst,ss,rs,ls):
     n=len(names)
@@ -133,7 +133,7 @@
     out=[];p=0
     for n in RSPLIT[name]:
         out.append((p,min(p+n*128,W))); p+=n*128
-    assert out[-1][1]==W,(name,out)
+    assert out[-1][1]==W
     return out
 def scatter_steps(nm,width,src,out,bufs,sems):
     ss,rs,ls=sems
@@ -247,12 +247,12 @@
                 r4[xh]=s.astype(jnp.bfloat16)
                 R[p,"f"][0].start()
             else:
-                out[:,pl.ds(a,b-a)]=s
+                out[:,pl.ds(a,b-a)]=s[0:out.shape[0],:]
         return f
     def end():
         a,b=cut[0]; h=(b-a)//2; r4=bufs[0][11]
         R[0,"f"][0].wait_recv()
-        for j in range(2): out[:,pl.ds(a+j*h,h)]=f32(r4[j])
+        for j in range(2): out[:,pl.ds(a+j*h,h)]=f32(r4[j])[0:out.shape[0],:]
         for cp in allc: cp.wait_send()
     return [[first]]+[[f(p) for p in P3] for f in (relay,reload,sum1,relay2,sum2,last)]+[[end]]
 STAGES=8
@@ -320,30 +320,100 @@
         pltpu.make_async_remote_copy(src_ref=src,dst_ref=dst,send_sem=send_sem,recv_sem=recv_sem,device_id=target,device_id_type=MESH).wait_send()
 def arrived(ref,sem):
     pltpu.make_async_copy(ref,ref,sem).wait()
-FWD_AT=((1,2),(2,3))
-BWD_AT=((0,3),(1,4),(2,5),(3,7),(4,8),(5,9))
+def steps(text):
+    return [text[k:k+2] for k in range(0,len(text),2)]
+FWD_BEFORE=steps("q1o0q2e1q3o1q4e2q5")
+FWD_LOAD=steps("c0e3o2")
+FWD_PROJ=steps("c1o3")
+FWD_SENT=steps("e4c2o4")
+FWD_AT=((1,"c3"),)
+FWD_THEN=steps("o5e5")
+FWD_LATE=steps("c4")
+FWD_END=steps("c5")
+QW=2432
+GC=0.7978845608028654
+def dot_tn(a,b): return lax.dot_general(a,b,(((0,),(0,)),((),())),preferred_element_type=jnp.float32)
 def attn_fwd_kernel(names,widths,*refs):
+    it=iter(refs)
+    take=lambda n:[next(it) for _ in range(n)]
     n=len(names)
-    qkv_in,start=refs[:2]
-    o_recv,qkv_out,oT,lse=refs[2+n:6+n]
-    qkv,knt,obf,s_in,s_out,r_in,r_out,l_sem=refs[6+2*n:14+2*n]
-    steps=gather_chains(names,widths,refs[2:2+n],refs[6+n:6+2*n],refs[14+2*n:])
+    xt,cols,bias,eb,segs=take(5)
+    src=take(n)
+    qkv_out,oT,lse,start,op,h1t,norm1t,norm2t,recips,h2t,mid,pre,a_own,a_other=take(14)
+    dst=take(n)
+    o_recv,qkv,knt,obf,wv,wov,acc,pt,of,mt,stat_s,stat_r,s_in,s_out,r_in,r_out,l_sem,w_sem,x_sem=take(19)
+    chains={nm:gather_steps(nm,[widths[t]],[src[t]],[dst[t]],*take(3)) for t,nm in enumerate(names)}
+    def run(which):
+        for k in which: chains[k[0]][int(k[1])]()
     d=lax.axis_index("dev"); r=lax.axis_index("row"); c=lax.axis_index("col")
+    partner=(d,r,1-c)
+    def swap(k,s,t):
+        cp=pltpu.make_async_remote_copy(src_ref=s,dst_ref=t,send_sem=x_sem.at[2*k],recv_sem=x_sem.at[2*k+1],device_id=partner,device_id_type=MESH)
+        cp.start()
+        return cp
+    def norm(k,v,gain,shift,normed,hidden):
+        stat_s[k,0:1,:]=jnp.sum(v,axis=0,keepdims=True)
+        stat_s[k,1:2,:]=jnp.sum(v*v,axis=0,keepdims=True)
+        swap(2*k,stat_s.at[k],stat_r.at[k]).wait()
+        m=(stat_s[k,0:1,:]+stat_r[k,0:1,:])*(1.0/D)
+        recip=lax.rsqrt((stat_s[k,1:2,:]+stat_r[k,1:2,:])*(1.0/D)-m*m+1e-5)
+        xhat=(v-m)*recip
+        normed[...]=xhat
+        recips[k:k+1,:]=recip
+        own=pl.ds(pl.multiple_of(16*c,16),16)
+        hidden[own]=(xhat*gain+shift).reshape(16,56,TT).astype(bf)
+        return swap(2*k+1,hidden.at[own],hidden.at[own])
     group_greet(d,r,c,[r+1-2*(r%2)])
+    acc[...]=jnp.broadcast_to(bias[...],acc.shape)
+    pre[...]=jnp.broadcast_to(eb[...],pre.shape)
+    seg=jnp.broadcast_to(jnp.where(r%2==0,segs[0:1,:],segs[1:2,:]),(8,LEN))
+    pos=lax.broadcasted_iota(jnp.int32,(8,LEN),1)
+    first=jnp.where((seg!=pltpu.roll(seg,1,1))&(pos>0),pos,0)
+    for k in range(12):
+        first=jnp.maximum(first,jnp.where(pos>=2**k,pltpu.roll(first,2**k,1),0))
+    start[...]=first[0:1,:]
     group_wait(1)
+    run(["q0","e0"])
+    sent=norm(0,xt[...].astype(jnp.float32),cols[:,1:2],cols[:,3:4],norm1t,h1t)
+    run(FWD_BEFORE)
+    wq=wv.at[:,:,:,:,pl.ds(0,QW)]
+    load=pltpu.make_async_copy(dst[0],wq,w_sem.at[0])
+    load.start()
+    run(FWD_LOAD)
+    sent.wait()
+    load.wait()
+    def over_blocks(total,tile,hidden,weight):
+        n=total.shape[1]
+        def body(k,_):
+            hk=jnp.concatenate([hidden[4*k+b] for b in range(4)],axis=0)
+            for a0 in range(0,n,tile):
+                sl=pl.ds(a0,min(tile,n-a0))
+                wk=jnp.concatenate([weight[k//2,(k%2)*2+b//2,b%2,:,sl] for b in range(4)],axis=0)
+                total[:,sl]+=dot_tn(hk,wk)
+            return 0
+        lax.fori_loop(0,8,body,0)
+    over_blocks(acc,512,h1t,wv)
+    run(FWD_PROJ)
+    for a0 in range(0,2400,128):
+        piece=acc[:,a0:min(a0+128,2400)].T.astype(bf)
+        at=a0
+        while at<min(a0+128,2400):
+            t=at//800; end=min(a0+128,2400,(t+1)*800)
+            pt[t,at-800*t:end-800*t,:]=piece[at-a0:end-a0]
+            at=end
     lanes=pl.ds(pl.multiple_of(r*128,128),128)
     def full(fn):
         def body(k,_):
             i=(r+k)%24
-            fn(qkv_in.at[i%2,:,i//2+c],qkv.at[:,:,lanes],s_in.at[i],r_in,i==r,(d,i,c))
+            fn(pt.at[:,pl.ds(pl.multiple_of(64*(i//2)+32*c,32),64),pl.ds(pl.multiple_of((i%2)*128,128),128)],qkv.at[:,:,lanes],s_in.at[i],r_in,i==r,(d,i,c))
             return 0
         lax.fori_loop(0,24,body,0)
     def halves(fn):
         rows=pl.ds(pl.multiple_of(32*c,32),32)
         for s in range(2):
-            fn(qkv_in.at[s,:,12*(1-c),rows],qkv.at[:,rows,lanes],s_in.at[24+s],r_in,(r==24+s)&(c==0),(d,24+s,0))
+            fn(pt.at[:,pl.ds(pl.multiple_of(768*(1-c),32),32),pl.ds(s*128,128)],qkv.at[:,rows,lanes],s_in.at[24+s],r_in,(r==24+s)&(c==0),(d,24+s,0))
     full(push); halves(push)
-    steps[0]()
+    run(FWD_SENT)
     item=(r<24)|((c==0)&(r<26))
     head=r//2+13*c; seq=r%2
     def outs(qi,fn):
@@ -360,7 +430,6 @@
         for a in range(LEN//512):
             sl=pl.ds(a*512,512)
             knt[sl,:]=qkv[1,:,sl].T
-    steps[1]()
     def qloop(qi,_):
         @pl.when(item)
         def _():
@@ -390,38 +459,80 @@
             lse[:,qs]=m+jnp.log(l)
             obf[:,qs]=o.astype(jnp.bfloat16)
             outs(qi,push)
-        for at,f in FWD_AT:
-            pl.when(qi==at)(steps[f])
+        for at,k in FWD_AT:
+            pl.when(qi==at)(functools.partial(run,steps(k)))
         return 0
     lax.fori_loop(0,LEN//FQ,qloop,0)
-    for f in range(FWD_AT[-1][1]+1,6): steps[f]()
+    run(FWD_THEN)
+    loads=[pltpu.make_async_copy(dst[3],wov,w_sem.at[0]),pltpu.make_async_copy(dst[1],wv,w_sem.at[1])]
+    for cp in loads: cp.start()
+    arrived(o_recv,r_out)
+    for s in range(2): of[:,pl.ds(128*s,128)]=o_recv[s].reshape(1600,128).astype(jnp.float32)
+    for k in range(ROWS):
+        op[k,0:50,:]=of[50*k:50*k+50,:].astype(bf)
+        op[k,50:56,:]=jnp.zeros((6,TT),bf)
+    loads[0].wait()
+    mid[...]=jnp.zeros_like(mid)
+    over_blocks(mid,512,op,wov)
+    run(FWD_LATE)
+    for k in range(7):
+        sl=pl.ds(128*k,128)
+        mt[sl,:]=mid[:,sl].T+cols[sl,5:6]+xt[sl,:].astype(jnp.float32)
+        mid[:,sl]=mt[sl,:].T
+    norm(1,mt[...],cols[:,0:1],cols[:,4:5],norm2t,h2t).wait()
+    loads[1].wait()
+    over_blocks(pre,640,h2t,wv)
+    for a0 in range(0,3200,640):
+        p=pre[:,a0:a0+640]
+        a_own[:,a0:a0+640]=(p*(0.5*(1.0+jnp.tanh(GC*(p+0.044715*(p*p*p)))))).astype(bf)
+    sent=swap(4,a_own,a_other)
+    run(FWD_END)
+    sent.wait()
     @pl.when(item)
     def _():
         save.wait()
         for qi in range(LEN//FQ): outs(qi,pushed)
     full(pushed); halves(pushed)
-    arrived(o_recv,r_out)
-BWD_AT=((0,1),(1,2),(3,3),(5,4),(7,5))
+BWD_START="e0"
+BWD_AT=((0,"e1o0"),(1,"e2o1"),(2,"c0"),(3,"e3"),(4,"o2"),(5,"c1"),(7,"e4o3"))
+BWD_THEN="e5c2e6o4e7"
+BWD_LAST="q0**c3q1o5c4q2--q3c5o6q4c6q5c7o7q6++q7"
+BR=224
 KQ=2432
+def unpad_rows(dst,v):
+    for g in range(16): dst[50*g:50*g+50,:]=v[56*g:56*g+50,:]
+def token_sums(v):
+    if v.dtype==bf: return lax.dot_general(jnp.ones((8,TT),bf),v,(((1,),(1,)),((),())),preferred_element_type=jnp.float32)[:1]
+    v=v[:,:128]+v[:,128:]
+    return jnp.concatenate([jnp.sum(v[128*k:128*k+128,:].T,axis=0,keepdims=True) for k in range(v.shape[0]//128)],axis=1)
 def back_kernel(names,widths,*refs):
     it=iter(refs)
     take=lambda n:[next(it) for _ in range(n)]
     n=len(names)
-    do_in,qkv,oT,start,lse,h1t,normt,vec_in,wq=take(9)
+    dh2t,norm2t,gt,cols,recips,op,wo,qkv,oT,start,lse,h1t,normt,vec_in,wq=take(15)
     parts=take(n)
-    part_q,dh1t,sum_q,vec_out=take(4)
+    part_o,part_q,gtok,sum_o,sum_q,vec_out=take(6)
     sums=take(n)
-    doT,knt,vnt,dqa,delta,dout,dq,stage,wblk,dh_send,dh_recv=take(11)
+    doT,knt,vnt,dqa,delta,dout,dq,stage,wblk,dh_send,dh_recv,do_recv,lhs,nbuf,dh,gmid,gat,dflat,dot_,stat_s,stat_r=take(21)
     vbuf=take(3); vtmp=next(it)
-    s_in,s_out,r_in,r_out,q_sem,w_sem,x_sem,free=take(8)
+    s_in,s_out,r_in,r_out,q_sem,w_sem,x_sem,l_sem,free=take(9)
     v_sems=take(2)
-    bufs=[by_part(take(36)) for _ in range(n)]
-    chains=[scatter_steps(names[t],widths[t],parts[t],sums[t],bufs[t],take(3)) for t in range(n)]
-    chain_q=scatter_steps("q",KQ,part_q,sum_q,narrowed(bufs[0],"q",KQ),take(3))
-    ticks=staggered(chains,1)
+    chains={}
+    for t in range(n):
+        b=by_part(take(36))
+        if t==0: first_bufs=b
+        chains[names[t]]=scatter_steps(names[t],widths[t],parts[t],sums[t],b,take(3))
+    chains["o"]=scatter_steps("o",KH,part_o,sum_o,by_part(take(36)),take(3))
+    chains["q"]=scatter_steps("q",KQ,part_q,sum_q,narrowed(first_bufs,"q",KQ),take(3))
+    def run(which):
+        for k in steps(which):
+            for f in chains[k[0]][int(k[1])]: f()
     v_go,v_total,v_end=vector_steps(vbuf,v_sems)
     d=lax.axis_index("dev"); r=lax.axis_index("row"); c=lax.axis_index("col")
+    partner=(d,r,1-c)
     item=(r<24)|((c==0)&(r<26))
+    loads=[pltpu.make_async_copy(s,t,l_sem.at[k]) for k,(s,t) in enumerate(((dh2t,dh),(norm2t,nbuf),(op,lhs),(normt,nbuf),(h1t,lhs)))]
+    for cp in loads[:3]: cp.start()
     group_greet(d,r,c,[r+1-2*(r%2),r])
     @pl.when(item)
     def _():
@@ -431,22 +542,74 @@
             vnt[sl,:]=qkv[2,:,sl].T
         dqa[...]=jnp.zeros_like(dqa)
     stage[...]=jnp.zeros_like(stage)
+    vtmp[...]=jnp.zeros_like(vtmp)
+    vtmp[pl.ds(35,vec_in.shape[0]),:]=vec_in[...]
+    def vec_rows(at,row):
+        for k in range(row.shape[1]//128): vtmp[pl.ds(at+k,1),:]=row[:,128*k:128*k+128]
+    def norm_back(k,incoming,normed,gain,recip):
+        e=incoming*gain
+        stat_s[k,0:1,:]=jnp.sum(e,axis=0,keepdims=True)
+        stat_s[k,1:2,:]=jnp.sum(e*normed,axis=0,keepdims=True)
+        cp=pltpu.make_async_remote_copy(src_ref=stat_s.at[k],dst_ref=stat_r.at[k],send_sem=x_sem.at[2*k],recv_sem=x_sem.at[2*k+1],device_id=partner,device_id_type=MESH)
+        cp.start()
+        cp.wait()
+        s1=stat_s[k,0:1,:]+stat_r[k,0:1,:]
+        s2=stat_s[k,1:2,:]+stat_r[k,1:2,:]
+        return recip*(e-s1*(1.0/D)-normed*(s2*(1.0/D)))
     group_wait(2)
+    run(BWD_START)
+    loads[0].wait(); loads[1].wait()
+    vec_rows(14,token_sums(dh[...]*nbuf[...]))
+    vec_rows(21,token_sums(dh[...]))
+    gmid[...]=(gt[...].astype(jnp.float32)+norm_back(0,dh[...],nbuf[...],cols[:,0:1],recips[0:1,:]))*cols[:,2:3]
+    gat[...]=gmid[...].astype(bf)
+    vec_rows(28,token_sums(gat[...]))
+    loads[3].start()
+    half=lambda w,base,k:w.at[pl.ds(pl.multiple_of(base*KH+BR*k,32),BR)]
+    nb=KH//BR
+    def pair_product(w,wide,rhs,recv,sem):
+        blocks=[half(w,1-c,k) for k in range(nb)]+[half(w,c,k) for k in range(nb)]
+        slot=lambda k:wblk.at[k%2,:,pl.ds(0,wide)] if wide<QW else wblk.at[k%2]
+        ld=[pltpu.make_async_copy(blocks[k],slot(k),w_sem.at[k%2]) for k in range(2*nb)]
+        ld[0].start(); ld[1].start()
+        swap=pltpu.make_async_remote_copy(src_ref=dh_send,dst_ref=recv,send_sem=x_sem.at[sem],recv_sem=x_sem.at[sem+1],device_id=partner,device_id_type=MESH)
+        for k in range(2*nb):
+            ld[k].wait()
+            v=dot(wblk[k%2,:,0:rhs.shape[0]],rhs)
+            if k<nb: dh_send[pl.ds(BR*k,BR),:]=v.astype(bf)
+            else: dh[pl.ds(BR*(k-nb),BR),:]=v
+            if k<2*nb-2: ld[k+2].start()
+            if k==nb-1: swap.start()
+        return swap
+    swap=pair_product(wo,KH,gat[...],do_recv,4)
+    swap.wait()
+    unpad_rows(dflat,dh[...]+do_recv[...].astype(jnp.float32))
+    dot_[...]=dflat[...].astype(bf)
     lanes=pl.ds(pl.multiple_of(r*128,128),128)
     def full(fn):
         def body(k,_):
             i=(r+k)%24
-            fn(do_in.at[i%2,i//2+c],doT.at[:,lanes],s_in.at[i],r_in,i==r,(d,i,c))
+            fn(dot_.at[pl.ds(pl.multiple_of(64*(i//2)+32*c,32),64),pl.ds(pl.multiple_of((i%2)*128,128),128)],doT.at[:,lanes],s_in.at[i],r_in,i==r,(d,i,c))
             return 0
         lax.fori_loop(0,24,body,0)
     def halves(fn):
         rows=pl.ds(pl.multiple_of(32*c,32),32)
         for s in range(2):
-            fn(do_in.at[s,12*(1-c),rows],doT.at[rows,lanes],s_in.at[24+s],r_in,(r==24+s)&(c==0),(d,24+s,0))
+            fn(dot_.at[pl.ds(pl.multiple_of(768*(1-c),32),32),pl.ds(s*128,128)],doT.at[rows,lanes],s_in.at[24+s],r_in,(r==24+s)&(c==0),(d,24+s,0))
     full(push); halves(push)
-    def tick(k):
-        for f in ticks[k]: f()
-    tick(0)
+    def emit(part,cols_,rhs):
+        prev={}
+        for b in range(8):
+            slot=b%2
+            if b>=2: prev[slot].wait()
+            stage[slot,:,:,:,0:cols_]=dot_nt(lhs[pl.ds(224*b,224),:],rhs).reshape(2,2,56,cols_).astype(bf)
+            src=stage.at[slot] if cols_==2400 else stage.at[slot,:,:,:,pl.ds(0,cols_)]
+            prev[slot]=pltpu.make_async_copy(src,part.at[b//2,pl.ds(2*(b%2),2)],q_sem.at[slot])
+            prev[slot].start()
+        return prev
+    loads[2].wait()
+    for cp in emit(part_o,KH,gat[...]).values(): cp.wait()
+    loads[4].start()
     def outs(fn):
         seq=pl.ds(pl.multiple_of((r%2)*128,128),128)
         @pl.when(r<24)
@@ -496,8 +659,8 @@
             dk,dv=lax.fori_loop(kj+1,LEN//BQ,lambda qi,cr:step(qi,cr,False),carry)
             dout[1,:,ks]=dk.astype(jnp.bfloat16)
             dout[2,:,ks]=dv.astype(jnp.bfloat16)
-        for step,k in BWD_AT:
-            pl.when(kj==step)(functools.partial(tick,k))
+        for step,which in BWD_AT:
+            pl.when(kj==step)(functools.partial(run,which))
         return 0
     lax.fori_loop(0,LEN//BK,kloop,0)
     @pl.when(item)
@@ -506,92 +669,69 @@
             sl=pl.ds(a*512,512)
             dout[0,:,sl]=(dqa[:,sl]*0.125).astype(jnp.bfloat16)
         outs(push)
-    for k in range(BWD_AT[-1][1]+1,STAGES): tick(k)
+    run(BWD_THEN)
     for ax,k in RPEERS: pl.semaphore_signal(free,inc=1,device_id=peer_of(ax,k),device_id_type=MESH)
     arrived(dq,r_out)
     grads=dq[...].reshape(2400,TT)
-    prev={}
-    for b in range(8):
-        slot=b%2
-        if b>=2: prev[slot].wait()
-        stage[slot,:,:,:,pl.ds(0,2400)]=dot_nt(h1t[pl.ds(224*b,224),:],grads).reshape(2,2,56,2400).astype(bf)
-        prev[slot]=pltpu.make_async_copy(stage.at[slot],part_q.at[b//2,pl.ds(2*(b%2),2)],q_sem.at[slot])
-        prev[slot].start()
-    partner=(d,r,1-c)
-    half=lambda base,k:wq.at[pl.ds(pl.multiple_of(base*KH+128*k,128),128)]
-    blocks=[half(1-c,k) for k in range(7)]+[half(c,k) for k in range(7)]
-    loads=[pltpu.make_async_copy(blocks[k],wblk.at[k%2],w_sem.at[k%2]) for k in range(14)]
-    loads[0].start(); loads[1].start()
-    for cp in prev.values(): cp.wait()
+    loads[4].wait()
+    for cp in emit(part_q,2400,grads).values(): cp.wait()
     pl.semaphore_wait(free,len(RPEERS))
-    def go_q(k):
-        for f in chain_q[k]: f()
-    go_q(0)
-    swap=pltpu.make_async_remote_copy(src_ref=dh_send,dst_ref=dh_recv,send_sem=x_sem.at[0],recv_sem=x_sem.at[1],device_id=partner,device_id_type=MESH)
-    for k in range(14):
-        loads[k].wait()
-        v=dot(wblk[k%2],grads)
-        if k<7: dh_send[pl.ds(128*k,128),:]=v.astype(bf)
-        else: dh1t[pl.ds(128*(k-7),128),:]=v
-        if k<12: loads[k+2].start()
-        if k==6: swap.start()
-    go_q(1)
-    for k in range(STAGES,len(ticks)): tick(k)
-    swap.wait()
-    dh1t[...]=dh1t[...]+dh_recv[...].astype(jnp.float32)
-    def token_sums(v,precision=None):
-        return lax.dot_general(jnp.ones((8,TT),v.dtype),v,(((1,),(1,)),((),())),precision=precision,preferred_element_type=jnp.float32)[:1]
-    gain=token_sums(dh1t[...]*normt[...],lax.Precision.HIGHEST)
-    bias=token_sums(dh1t[...],lax.Precision.HIGHEST)
-    both=token_sums(grads)
-    both=jnp.concatenate((both,jnp.zeros((1,32),jnp.float32)),axis=1)
-    vtmp[pl.ds(0,40),:]=jnp.zeros((40,128),jnp.float32)
-    vtmp[pl.ds(40,vec_in.shape[0]),:]=vec_in[...]
-    for at,row,cnt in ((0,gain,7),(7,bias,7),(14,both,19)):
-        for k in range(cnt): vtmp[pl.ds(at+k,1),:]=row[:,128*k:128*k+128]
-    v_go(0,vtmp[...])
-    go_q(2); go_q(3)
-    v_go(1,v_total(0))
-    go_q(4)
-    v_go(2,v_total(1))
-    go_q(5); go_q(6)
+    def late_product():
+        chains["swap"]=pair_product(wq,QW,grads,dh_recv,6)
+    def late_norm():
+        chains["swap"].wait()
+        dh[...]=dh[...]+dh_recv[...].astype(jnp.float32)
+        loads[3].wait()
+        vec_rows(0,token_sums(dh[...]*nbuf[...]))
+        vec_rows(7,token_sums(dh[...]))
+        vec_rows(67,jnp.concatenate((token_sums(grads),jnp.zeros((1,32),jnp.float32)),axis=1))
+        v_go(0,vtmp[...])
+        gtok[...]=(gmid[...]+norm_back(1,dh[...],nbuf[...],cols[:,1:2],recips[1:2,:])).astype(bf)
+        v_go(1,v_total(0))
+    def late_vec():
+        v_go(2,v_total(1))
+    for k in steps(BWD_LAST):
+        if k=="**": late_product()
+        elif k=="--": late_norm()
+        elif k=="++": late_vec()
+        else: run(k)
     vec_out[...]=v_total(2)
-    go_q(7)
     v_end()
     pl.when(item)(lambda:outs(pushed))
     full(pushed); halves(pushed)
 VM=pl.BlockSpec(memory_space=pltpu.VMEM); ANY=pl.BlockSpec(memory_space=pl.ANY)
 bf=jnp.bfloat16
-def attend(qkv,start,names,arrs,cid=1):
-    S=jax.ShapeDtypeStruct; n=len(names)
+def attend(xt,cols,bias,eb,segs,names,arrs,cid=1):
+    S=jax.ShapeDtypeStruct; n=len(names); V=pltpu.VMEM; DM=pltpu.SemaphoreType.DMA; f=jnp.float32
+    FH=eb.shape[1]
     out=pl.pallas_call(functools.partial(attn_fwd_kernel,names,[a.shape[1] for a in arrs]),
-      out_shape=(S((2,25,HD,128),bf),S((3,HD,LEN),bf),S((HD,LEN),jnp.float32),S((1,LEN),jnp.float32))+gather_shapes(arrs),
-      in_specs=[VM,VM]+[ANY]*n,out_specs=(ANY,ANY,VM,VM)+(ANY,)*n,
-      scratch_shapes=[pltpu.VMEM((3,HD,LEN),bf),pltpu.VMEM((LEN,HD),bf),pltpu.VMEM((HD,LEN),bf),
-        pltpu.SemaphoreType.DMA((26,)),pltpu.SemaphoreType.DMA((64,)),pltpu.SemaphoreType.DMA,pltpu.SemaphoreType.DMA,pltpu.SemaphoreType.DMA]+gather_sems(n),
-      compiler_params=pltpu.CompilerParams(collective_id=cid,has_side_effects=True,vmem_limit_bytes=50<<20))(qkv,start,*arrs)
-    return out[0],out[1:4],out[4:]
-def attend_back(do,kept,start,h1t,normt,vec,wq,names,parts,cid=2):
+      out_shape=(S((3,HD,LEN),bf),S((HD,LEN),f),S((1,LEN),f),S((1,LEN),jnp.int32),S((32,56,TT),bf),S((32,56,TT),bf),S((KH,TT),f),S((KH,TT),f),S((8,TT),f),S((32,56,TT),bf),
+        S((TT,KH),f),S((TT,FH),f),S((TT,FH),bf),S((TT,FH),bf))+gather_shapes(arrs),
+      in_specs=[VM]*5+[ANY]*n,out_specs=(ANY,)+(VM,)*12+(ANY,)+(ANY,)*n,
+      scratch_shapes=[V((2,25,HD,128),bf),V((3,HD,LEN),bf),V((LEN,HD),bf),V((HD,LEN),bf),V((4,4,2,56,FH),bf),V((4,4,2,56,KH),bf),V((TT,2400),f),V((3,800,TT),bf),V((1600,TT),f),V((KH,TT),f),
+        V((2,8,TT),f),V((2,8,TT),f),DM((26,)),DM((64,)),DM,DM,DM,DM((2,)),DM((10,))]+gather_sems(n),
+      compiler_params=pltpu.CompilerParams(collective_id=cid,has_side_effects=True,vmem_limit_bytes=62<<20))(xt,cols,bias,eb,segs,*arrs)
+    return out[:4],out[4:14],out[14:]
+def attend_back(front,kept,h1t,normt,vec,wq,names,parts,cid=2):
     S=jax.ShapeDtypeStruct; n=len(names); f=jnp.float32; V=pltpu.VMEM; DM=pltpu.SemaphoreType.DMA
-    qkv,oT,lse=kept
-    rows=40+vec.shape[0]
+    qkv,oT,lse,start=kept
+    rows=88
     out=pl.pallas_call(functools.partial(back_kernel,names,[a.shape[4] for a in parts]),
-      out_shape=(S((4,4,2,56,KQ),bf),S((KH,TT),f),S((56,KQ),f),S((rows,128),f))+tuple(S(a.shape[3:],f) for a in parts),
-      in_specs=[VM]*8+[ANY]*(1+n),out_specs=(ANY,VM,VM,VM)+(VM,)*n,
+      out_shape=(S((4,4,2,56,KH),bf),S((4,4,2,56,KQ),bf),S((KH,TT),bf),S((50,KH),f),S((50,KQ),f),S((rows,128),f))+tuple(S((50 if a.shape[3]==56 else a.shape[3],a.shape[4]),f) for a in parts),
+      in_specs=[ANY,ANY,VM,VM,VM,ANY,ANY,VM,VM,VM,VM,ANY,ANY,VM]+[ANY]*(1+n),out_specs=(ANY,ANY,VM,VM,VM,VM)+(VM,)*n,
       scratch_shapes=[V((HD,LEN),bf),V((LEN,HD),bf),V((LEN,HD),bf),V((HD,LEN),f),V((1,LEN),f),V((3,HD,LEN),bf),
-        V((3,800,TT),bf),V((2,2,2,56,KQ),bf),V((2,128,2400),bf),V((KH,TT),bf),V((KH,TT),bf)]+[V((4,rows,128),f)]*3+[V((rows,128),f)]+
-        [DM((26,)),DM((64,)),DM,DM,DM((2,)),DM((2,)),DM((2,)),pltpu.SemaphoreType.REGULAR,DM((9,)),DM((9,))]+
-        sum([scatter_bufs(nm,*a.shape[3:]) for nm,a in zip(names,parts)],[])+scatter_sems()*(n+1),
-      compiler_params=pltpu.CompilerParams(collective_id=cid,has_side_effects=True,vmem_limit_bytes=VMEM_BACK))(do,qkv,oT,start,lse,h1t,normt,vec,wq,*parts)
-    return out[1],out[2],out[3],out[4:]
-VMEM_BACK=62<<20
-
-
-WC=800; FH=3200; TF=640
-GC=0.7978845608028654
-def dot_tn(a,b): return lax.dot_general(a,b,(((0,),(0,)),((),())),preferred_element_type=jnp.float32)
-def mlp_kernel(h2,we,eb,wc,mid,cb,g,result,part_c,part_e,dh2,dsum,
-        wev,wcv,pre,a_own,a_recv,da_send,da_recv,dpre,dh_send,dh_recv,stage_e,stage_c,w_sem,s_sem,r_sem,e_sem,c_sem):
+        V((3,800,TT),bf),V((2,2,2,56,KQ),bf),V((2,BR,QW),bf),V((KH,TT),bf),V((KH,TT),bf),V((KH,TT),bf),V((KP,TT),bf),
+        V((KH,TT),f),V((KH,TT),f),V((KH,TT),f),V((KH,TT),bf),V((800,TT),f),V((800,TT),bf),V((2,8,TT),f),V((2,8,TT),f)]+[V((4,rows,128),f)]*3+[V((rows,128),f)]+
+        [DM((26,)),DM((64,)),DM,DM,DM((2,)),DM((2,)),DM((8,)),DM((5,)),pltpu.SemaphoreType.REGULAR,DM((9,)),DM((9,))]+
+        sum([scatter_bufs(nm,*a.shape[3:])+scatter_sems() for nm,a in zip(names,parts)],[])+scatter_bufs("o",56,KH)+scatter_sems()*2,
+      compiler_params=pltpu.CompilerParams(collective_id=cid,has_side_effects=True,vmem_limit_bytes=VMEM_BACK))(*front,qkv,oT,start,lse,h1t,normt,vec,wq,*parts)
+    return out[2],out[3],out[4],out[5],out[6:]
+VMEM_BACK=63<<20
+
+
+FH=3200; TF=640
+def mlp_kernel(h2t,we,wc,pre,a_own,a_other,mid,cb,g,result,part_c,part_e,dh2,dsum,
+        wev,wcv,da_send,da_recv,dpre,dh_send,dh_recv,stage_e,stage_c,w_sem,s_sem,r_sem,e_sem,c_sem):
     c=lax.axis_index("col"); other=1-c
     partner=(lax.axis_index("dev"),lax.axis_index("row"),other)
     loads=[pltpu.make_async_copy(wc,wcv,w_sem.at[0]),pltpu.make_async_copy(we,wev,w_sem.at[1])]
@@ -601,9 +741,9 @@
     pl.semaphore_wait(bar,1)
     def swap(i,s,d):
         return pltpu.make_async_remote_copy(src_ref=s,dst_ref=d,send_sem=s_sem.at[i],recv_sem=r_sem.at[i],device_id=partner,device_id_type=MESH)
-    x_da,x_a,x_dh=swap(0,da_send,da_recv),swap(1,a_own,a_recv),swap(2,dh_send,dh_recv)
+    x_da,x_dh=swap(0,da_send,da_recv),swap(1,dh_send,dh_recv)
     lanes=lambda k,n:pl.ds(pl.multiple_of(k*n,128),n)
-    rows=lambda base,k,n:pl.ds(pl.multiple_of(base+k*n,128),n)
+    rows=lambda base,k,n:pl.ds(pl.multiple_of(base+k*n,64),n)
     f32=lambda v:v.astype(jnp.float32)
     NT=FH//TF
     def loop(n,f):
@@ -615,13 +755,17 @@
     def f(k): da_send[:,lanes(k,TF)]=dot_nt(g[...],wcv[rows(other*FH,k,TF),:]).astype(bf)
     loop(NT,f)
     x_da.start()
-    loads[1].wait()
-    def f(k):
-        p=dot(h2[...],wev[:,lanes(k,TF)])+eb[:,lanes(k,TF)]
-        pre[:,lanes(k,TF)]=p
-        a_own[:,lanes(k,TF)]=(p*(0.5*(1.0+jnp.tanh(GC*(p+0.044715*(p*p*p)))))).astype(bf)
-    loop(NT,f)
-    x_a.start()
+    def emit(i,stage,sem,dst,value):
+        slot=i%2
+        cp=pltpu.make_async_copy(stage.at[slot],dst,sem.at[slot])
+        if i>=2: prev[slot].wait()
+        stage[slot]=value
+        cp.start(); prev[slot]=cp
+    prev={}
+    for i in range(2*NT):
+        a,b,k=(a_own,c,i) if i<NT else (a_other,other,i-NT)
+        emit(i,stage_c,c_sem,part_c.at[rows(b*FH,k,TF)],dot_tn(a[:,k*TF:k*TF+TF],g[...]).astype(bf))
+    prev_c=prev
     x_da.wait_recv()
     def f(k):
         sl=lanes(k,TF)
@@ -633,97 +777,37 @@
         dpre[:,sl]=dp
         dsum[:,sl]=jnp.sum(f32(dp),axis=0,keepdims=True)
     loop(NT,f)
-    def f(k): dh_send[:,lanes(k,128)]=dot_nt(dpre[...],wev[rows(other*KH,k,128),:]).astype(bf)
-    loop(KH//128,f)
+    loads[1].wait()
+    def f(k): dh_send[rows(0,k,448),:]=dot_nt(wev[rows(other*KH,k,448),:],dpre[...]).astype(bf)
+    loop(2,f)
     x_dh.start()
-    def f(k): dh2[:,lanes(k,128)]=dot_nt(dpre[...],wev[rows(c*KH,k,128),:])
-    loop(KH//128,f)
-    def emit(i,stage,sem,dst,value):
-        slot=i%2
-        cp=pltpu.make_async_copy(stage.at[slot],dst,sem.at[slot])
-        if i>=2: prev[slot].wait()
-        stage[slot]=value
-        cp.start(); prev[slot]=cp
+    def f(k): dh2[rows(0,k,448),:]=dot_nt(wev[rows(c*KH,k,448),:],dpre[...])
+    loop(2,f)
     prev={}
     for j in range(KP//256):
-        emit(j,stage_e,e_sem,part_e.at[pl.ds(256*j,256)],dot_tn(h2[:,256*j:256*j+256],dpre[...]).astype(bf))
-    for cp in prev.values(): cp.wait()
-    x_a.wait_recv()
-    br=dot(a_own[...],wcv[rows(c*FH,0,FH),:])+dot(a_recv[...],wcv[rows(other*FH,0,FH),:])
+        emit(j,stage_e,e_sem,part_e.at[pl.ds(256*j,256)],dot(h2t[256*j:256*j+256,:],dpre[...]).astype(bf))
+    br=dot(a_own[...],wcv[rows(c*FH,0,FH),:])+dot(a_other[...],wcv[rows(other*FH,0,FH),:])
     result[...]=(mid[...]+(br+cb[...])).astype(bf)
-    prev={}
-    for i in range(2*NT):
-        a,b,k=(a_own,c,i) if i<NT else (a_recv,other,i-NT)
-        emit(i,stage_c,c_sem,part_c.at[rows(b*FH,k,TF)],dot_tn(a[:,k*TF:k*TF+TF],g[...]).astype(bf))
     x_dh.wait_recv()
     dh2[...]=dh2[...]+f32(dh_recv[...])
-    for cp in prev.values(): cp.wait()
-    for cp in (x_da,x_a,x_dh): cp.wait_send()
-def mlp(h2,we,eb,wc,mid,cb,g,cid=4):
+    for cp in list(prev.values())+list(prev_c.values()): cp.wait()
+    for cp in (x_da,x_dh): cp.wait_send()
+def mlp(h2t,we,wc,pre,a_own,a_other,mid,cb,g,cid=4):
     S=jax.ShapeDtypeStruct; f=jnp.float32; V=pltpu.VMEM
     return pl.pallas_call(mlp_kernel,
-      out_shape=(S((TT,WC),bf),S((6400,WC),bf),S((KP,FH),bf),S((TT,KH),f),S((1,FH),f)),
-      in_specs=[VM,ANY,VM,ANY,VM,VM,VM],out_specs=(VM,ANY,ANY,VM,VM),
-      scratch_shapes=[V((KP,FH),bf),V((6400,WC),bf),V((TT,FH),f)]+[V((TT,FH),bf)]*5+[V((TT,KH),bf)]*2+[V((2,256,FH),bf),V((2,TF,WC),bf)]+[pltpu.SemaphoreType.DMA((n,)) for n in (2,3,3,2,2)],
-      compiler_params=pltpu.CompilerParams(collective_id=cid,has_side_effects=True,vmem_limit_bytes=58<<20))(h2,we,eb,wc,mid,cb,g)
-def pair_dot_kernel(v,w,out,send,recv,s_sem,r_sem):
-    c=lax.axis_index("col"); other=1-c
-    partner=(lax.axis_index("dev"),lax.axis_index("row"),other)
-    bar=pltpu.get_barrier_semaphore()
-    pl.semaphore_signal(bar,inc=1,device_id=partner,device_id_type=MESH)
-    for k in range(KH//128):
-        send[:,128*k:128*k+128]=dot_nt(v[...],w[pl.ds(pl.multiple_of(other*KH+128*k,128),128),:]).astype(bf)
-    pl.semaphore_wait(bar,1)
-    cp=pltpu.make_async_remote_copy(src_ref=send,dst_ref=recv,send_sem=s_sem,recv_sem=r_sem,device_id=partner,device_id_type=MESH)
-    cp.start()
-    for k in range(KH//128):
-        out[:,128*k:128*k+128]=dot_nt(v[...],w[pl.ds(pl.multiple_of(c*KH+128*k,128),128),:])
-    cp.wait()
-    out[...]=out[...]+recv[...].astype(jnp.float32)
-def pair_dot(v,w,cid):
-    return pl.pallas_call(pair_dot_kernel,out_shape=jax.ShapeDtypeStruct((TT,KH),jnp.float32),in_specs=[VM,VM],out_specs=VM,
-      scratch_shapes=[pltpu.VMEM((TT,KH),bf)]*2+[pltpu.SemaphoreType.DMA]*2,
-      compiler_params=pltpu.CompilerParams(collective_id=cid,has_side_effects=True,vmem_limit_bytes=40<<20))(v,w)
-def outer_kernel(a,b,o):
-    o[...]=dot_tn(a[...],b[...]).astype(bf)
-def outer(a,b):
-    m=a.shape[1]; n=b.shape[1]
-    return pl.pallas_call(outer_kernel,out_shape=jax.ShapeDtypeStruct((m,n),bf),grid=(m//256,),
-      in_specs=[pl.BlockSpec((TT,256),lambda i:(0,i)),pl.BlockSpec((TT,n),lambda i:(0,0))],out_specs=pl.BlockSpec((256,n),lambda i:(i,0)),
-      compiler_params=pltpu.CompilerParams(vmem_limit_bytes=32<<20))(a,b)
-
-
-def width_sums(first_sum, second_sum):
-    return lax.psum((first_sum, second_sum), "col")
-
-
-def full_rows(values):
-    return lax.all_gather(values, "col", axis=1, tiled=True)
-
-
-def norm_forward(values, norm_gain, norm_bias):
-    totals = width_sums(jnp.sum(values, axis=1), jnp.sum(values * values, axis=1))
-    averages = totals[0] / D
-    reciprocal = lax.rsqrt(totals[1] / D - averages * averages + 1e-05)
-    normed = (values - averages[:, None]) * reciprocal[:, None]
-    return (normed, reciprocal, normed * norm_gain + norm_bias)
-
-
-def norm_backward(incoming, normed, reciprocal, norm_gain):
-    scaled = incoming * norm_gain
-    totals = width_sums(jnp.sum(scaled, axis=1), jnp.sum(scaled * normed, axis=1))
-    return reciprocal[:, None] * (
-        scaled - totals[0][:, None] / D - normed * (totals[1][:, None] / D)
-    )
+      out_shape=(S((TT,KH),bf),S((6400,KH),bf),S((KP,FH),bf),S((KH,TT),f),S((1,FH),f)),
+      in_specs=[VM,ANY,ANY]+[VM]*6,out_specs=(VM,ANY,ANY,VM,VM),
+      scratch_shapes=[V((KP,FH),bf),V((6400,KH),bf)]+[V((TT,FH),bf)]*3+[V((KH,TT),bf)]*2+[V((2,256,FH),bf),V((2,TF,KH),bf)]+[pltpu.SemaphoreType.DMA((n,)) for n in (2,2,2,2,2)],
+      compiler_params=pltpu.CompilerParams(collective_id=cid,has_side_effects=True,vmem_limit_bytes=58<<20))(h2t,we,wc,pre,a_own,a_other,mid,cb,g)
 
 
 def pad_rows(block):
     return jnp.pad(block, ((0, 6), (0, 0)))
 
 
-def pad_features(values):
+def pad_columns(values):
     n = values.shape[0]
-    return jnp.pad(values.reshape(n, 32, 50), ((0, 0), (0, 0), (0, 6))).reshape(n, KP)
+    return jnp.pad(values.reshape(n, 16, 50), ((0, 0), (0, 0), (0, 6))).reshape(n, KH)
 
 
 def unpad_features(values):
@@ -750,120 +834,90 @@
 ):
     seqs, block_len, width = tokens.shape
     row_total = seqs * block_len
-    row = lax.axis_index("row")
-    col = lax.axis_index("col")
-    weight_qkv, weight_expand = gather(
-        "qe", (pad_rows(attention_in.reshape(50, 3 * width)), pad_rows(expand_weight)), 0
+    grad_low = pad_columns(cotangent.reshape(row_total, width))
+    grad_sums = jnp.sum(grad_low.astype(jnp.float32), axis=0)
+    tokens_back = pad_columns(tokens.reshape(row_total, width)).T
+    zeros = jnp.zeros_like(first_gain)
+    small = jnp.concatenate(
+        (second_gain, first_gain, zeros + 1.0, first_bias, second_bias, output_bias, contract_bias, zeros)
     )
-    weight_qkv = weight_qkv.reshape(KP, 3 * width)
-
-    own_seg = lax.dynamic_index_in_dim(segments, row % 2, 0, keepdims=True)
-    positions = jnp.arange(LEN, dtype=jnp.int32)[None]
-    before = jnp.concatenate((own_seg[:, :1], own_seg[:, :-1]), axis=1)
-    start = lax.cummax(jnp.where(own_seg != before, positions, 0), axis=1)
-
-    float_tokens = tokens.astype(jnp.float32).reshape(row_total, width)
-    normed_one, recip_one, hidden_one = norm_forward(float_tokens, first_gain, first_bias)
-    rows_one = pad_features(full_rows(hidden_one.astype(jnp.bfloat16)))
-    bias_three = jnp.concatenate(
-        (attention_bias[0], jnp.zeros_like(attention_bias[0]), attention_bias[1])
-    )
-    projected = jnp.einsum(
-        "dm,snd->smn",
-        weight_qkv,
-        rows_one.reshape(seqs, block_len, KP),
-        preferred_element_type=jnp.float32,
-    )
-    projected = (projected + bias_three[None, :, None]).astype(jnp.bfloat16)
-    projected = projected.reshape(seqs, 3, width, block_len)
-
-    def head_slots(values):
-        lead = [(0, 0)] * (values.ndim - 2)
-        slots = jnp.where(
-            col == 0,
-            jnp.pad(values, lead + [(0, 32), (0, 0)]),
-            jnp.pad(values, lead + [(32, 0), (0, 0)]),
-        )
-        return slots.reshape(values.shape[:-2] + (13, HD, block_len))
-
-    attended, kept, gathered = attend(
-        head_slots(projected),
-        start,
-        "co",
-        (contract_weight, pad_rows(attention_out)),
+    small = pad_columns(small.reshape(8, width))
+    columns = small.T
+    bias_three = jnp.concatenate((attention_bias[0], zeros, attention_bias[1]))
+    kept, saved, gathered = attend(
+        tokens_back,
+        columns,
+        bias_three[None],
+        expand_bias[None],
+        segments,
+        "qeco",
+        (
+            jnp.pad(attention_in.reshape(50, 3 * width), ((0, 6), (0, 32))),
+            pad_rows(expand_weight),
+            pad_columns(contract_weight),
+            pad_rows(pad_columns(attention_out)),
+        ),
         1,
     )
-    weight_out = gathered[1].reshape(KP, width)
-    weight_expand = weight_expand.reshape(KP, 4 * width)
-    weight_contract = gathered[0].reshape(4 * D, width)
-    rows_attn = jnp.pad(
-        attended.reshape(seqs, 32, 50, block_len), ((0, 0), (0, 0), (0, 6), (0, 0))
-    ).reshape(seqs, KP, block_len)
-    middle = float_tokens + (
-        jnp.einsum(
-            "sfn,fd->snd", rows_attn, weight_out, preferred_element_type=jnp.float32
-        ).reshape(row_total, width)
-        + output_bias
+    rows_attn, rows_one, normed_one, normed_two, recips, rows_two, middle, pre_gelu, gelu_own, gelu_other = saved
+    weight_qkv = gathered[0].reshape(KP, QW)
+    weight_expand = gathered[1].reshape(KP, 4 * width)
+    weight_contract = gathered[2].reshape(4 * D, KH)
+    weight_out = gathered[3].reshape(KP, KH)
+    result, part_contract, part_expand, grad_two, expand_sums = mlp(
+        rows_two.reshape(KP, row_total),
+        weight_expand,
+        weight_contract,
+        pre_gelu,
+        gelu_own,
+        gelu_other,
+        middle,
+        small[6:7],
+        grad_low,
+        4,
     )
-    normed_two, recip_two, hidden_two = norm_forward(middle, second_gain, second_bias)
-    rows_two = pad_features(full_rows(hidden_two.astype(jnp.bfloat16)))
-    grad_low = cotangent.reshape(row_total, width)
-    grad_float = grad_low.astype(jnp.float32)
-    result, part_contract, part_expand, grad_two, expand_sums = mlp(
-        rows_two, weight_expand, expand_bias[None], weight_contract, middle, contract_bias[None], grad_low, 4
-    )
-    result = result.reshape(tokens.shape)
-    grad_two = unpad_features(grad_two)
-    grad_middle = grad_float + norm_backward(grad_two, normed_two, recip_two, second_gain)
-    grad_attn = grad_middle.astype(jnp.bfloat16)
-    part_out = outer(jnp.transpose(rows_attn, (0, 2, 1)).reshape(row_total, KP), grad_attn)
-    grad_mixed = unpad_features(pair_dot(grad_attn, weight_out, 5).astype(jnp.bfloat16))
-    grad_mixed = jnp.transpose(grad_mixed.reshape(seqs, block_len, width), (0, 2, 1))
-    sums_rest = (
-        jnp.sum(grad_attn.astype(jnp.float32), axis=0),
-        jnp.sum(grad_two * normed_two, axis=0),
-        jnp.sum(grad_two, axis=0),
-        jnp.sum(grad_float, axis=0),
-        expand_sums[0],
-    )
-    grad_one, sum_qkv, vector, (sum_expand, sum_contract, sum_out) = attend_back(
-        head_slots(grad_mixed),
+    result = unpad_features(result).reshape(tokens.shape)
+    gradient_tokens, sum_out, sum_qkv, vector, (sum_expand, sum_contract) = attend_back(
+        (
+            grad_two,
+            normed_two,
+            grad_low.T,
+            columns,
+            jnp.stack((recips[1], recips[0])),
+            rows_attn.reshape(KP, row_total),
+            weight_out,
+        ),
         kept,
-        start,
-        rows_one.T,
-        jnp.pad(normed_one.reshape(row_total, 16, 50), ((0, 0), (0, 0), (0, 6))).reshape(row_total, KH).T,
-        jnp.concatenate(sums_rest).reshape(50, 128),
+        rows_one.reshape(KP, row_total),
+        normed_one,
+        jnp.concatenate((grad_sums, expand_sums[0])).reshape(32, 128),
         weight_qkv,
-        "eco",
+        "ec",
         (
             part_expand.reshape(4, 4, 2, 56, 4 * width),
-            part_contract.reshape(4, 4, 2, 200, width),
-            part_out.reshape(4, 4, 2, 56, width),
+            part_contract.reshape(4, 4, 2, 200, KH),
         ),
         2,
     )
-    grad_one = unpad_features(grad_one.T)
-    grad_input = grad_middle + norm_backward(grad_one, normed_one, recip_one, first_gain)
-    gradient_tokens = grad_input.astype(jnp.bfloat16).reshape(tokens.shape)
-    first = unpad_features(vector[:14].reshape(2, KH))
-    qkv_sums = vector[14:33].reshape(-1)[: 3 * width].reshape(3, width)
-    rest = vector[40:].reshape(-1)
-    sums = [rest[width * k : width * (k + 1)] for k in range(4)] + [rest[4 * width :]]
+    gradient_tokens = unpad_features(gradient_tokens.T).reshape(tokens.shape)
+    padded = unpad_features(vector[:42].reshape(6, KH)).reshape(-1)
+    sums = [padded[width * k : width * (k + 1)] for k in range(6)]
+    qkv_sums = vector[67:86].reshape(-1)
     return (
         result,
         gradient_tokens,
-        first[0],
-        first[1],
-        sum_qkv[:50, : 3 * width].reshape(50, 3, width),
-        jnp.stack((qkv_sums[0], qkv_sums[2])),
-        sum_out[:50],
         sums[0],
         sums[1],
+        sum_qkv[:, : 3 * width].reshape(50, 3, width),
+        jnp.concatenate((qkv_sums[:width], qkv_sums[2 * width : 3 * width])).reshape(2, width),
+        unpad_features(sum_out),
+        sums[4],
         sums[2],
-        sum_expand[:50],
-        sums[4],
-        sum_contract,
         sums[3],
+        sum_expand,
+        vector[42:67].reshape(-1),
+        unpad_features(sum_contract),
+        sums[5],
     )
 
 

time: 556 us -> 512 us (0.921)
  blocking collectives: 16.7 us -> 0 us
  other arithmetic: 15.2 us -> 2.21 us
  matrix products: 10.2 us -> 0 us
  local copies, waits for them, and re-layouts: 49.7 us -> 42.3 us
    pallas_call x4 -> x1, Pallas kernels: 145 us -> 37.8 us  [mlp(): pl.pallas_call(mlp_kernel, out_shape=(S((TT, KH), bf), S((6400, KH), bf),...]
    pallas_call x1, Pallas kernels: 106 us -> 199 us  [attend(): pl.pallas_call(functools.partial(attn_fwd_kernel, names, [a.shape[1] for...]
    pallas_call x1, Pallas kernels: 203 us -> 223 us  [attend_back(): pl.pallas_call(functools.partial(back_kernel, names, [a.shape[4] for a in...]
    dot_general x2 -> x0, matrix products: 10.2 us -> none  [the longest x1 7.07 us: per_device(): jnp.einsum('dm,snd->smn', weight_qkv, rows_one.reshape(seqs, block_len, K...]
    psum x4 -> x0, blocking collectives: 10 us -> none  [width_sums(): return lax.psum((first_sum, second_sum), 'col')]
    reduce_sum x6 -> x1, other arithmetic: 10.1 us -> 0.19 us  [per_device(): grad_sums = jnp.sum(grad_low.astype(jnp.float32), axis=0)]
    all_gather x2 -> x0, blocking collectives: 6.63 us -> none  [full_rows(): return lax.all_gather(values, 'col', axis=1, tiled=True)]
    reshape x4 -> x3, local copies, waits for them, and re-layouts: 8.19 us -> 2.25 us  [unpad_features(): return values.reshape(n, 16, 56)[:, :, :50].reshape(n, 800)]
where the time goes in v4:
time: 512 us; the launch traced here: 505 us
  Pallas kernels  459 us (90%)
  local copies, waits for them, and re-layouts  42.3 us (8%)
    pallas_call x1, Pallas kernels, attend_back(): pl.pallas_call(functools.partial(back_kernel, names, [a.shape[4] for a in...  223 us
    pallas_call x1, Pallas kernels, attend(): pl.pallas_call(functools.partial(attn_fwd_kernel, names, [a.shape[1] for...  199 us
    pallas_call x1, Pallas kernels, mlp(): pl.pallas_call(mlp_kernel, out_shape=(S((TT, KH), bf), S((6400, KH), bf),...  37.8 us

profile of v4, /device:TPU:0, one launch (start us, length us, event | category | flops | bytes accessed | tf_op | source)
XLA Modules:
  0.0 505.3 jit_solution(14178439950539974380)
XLA Ops:
  0.7 0.8 concatenate.26
  1.5 0.8 concatenate.27
  2.2 0.8 concatenate.29
  3.0 0.8 concatenate.25
  3.8 0.8 concatenate.28
  4.6 0.8 concatenate.30
  5.3 0.8 slice_reduce_fusion
  6.2 0.1 concatenate.32
  6.2 0.6 broadcast_in_dim.13.refs_2_
  6.8 1.3 broadcast_in_dim.14.refs_3_
  8.2 0.7 slice.94.cb
  8.9 1.2 reshape.133
  10.2 0.2 reshape.134
  10.5 0.7 pad.37.refs_8_
  11.1 1.1 copy.34
  12.2 0.3 reshape.130
  12.6 0.7 pad.33.refs_5_
  13.3 1.7 pad.34.refs_6_
  15.0 0.2 copy.45
  15.3 0.8 pad.32.clone
  16.1 1.3 copy.32
  17.4 0.3 reshape_reshape.17
  17.7 0.8 pad.31
  18.5 1.2 copy.35
  19.6 0.1 reshape.131
  19.8 0.1 pad.35
  19.9 0.9 copy.36.refs_7_
  20.8 0.3 copy.37
  21.1 0.3 reshape_reshape.18
  21.4 0.2 convert_reduce_fusion
  21.6 0.1 reduce_sum.12
  21.7 1.0 copy.38.g
  22.7 198.6 %shard_map.254 = (bf16[3,64,4096]{2,1,0:T(8,128)(2,1)}, f32[64,4096]{1,0:T(8,128)}, f32[1,4096]{1,0:T(1,128)}, s32[1,4096]{1,0:T(1,128)}, bf16[32,56,256]{2,1,0:...) custom-call(bf16[896,256]{1,0:T(8,128)(2,1)} %bitcast.59, ...), custom_call_target="tpu_custom_call" | custom-call | tf_op jit(solution)/shard_map/pallas_call | solution.py:707
  221.3 37.8 %shard_map.255 = (bf16[256,896]{1,0:T(8,128)(2,1)}, bf16[6400,896]{1,0:T(8,128)(2,1)}, bf16[1792,3200]{1,0:T(8,128)(2,1)}, f32[896,256]{1,0:T(8,128)}, f32[1,3200]{1,0:T(1,128)}) custom-call(bf16[1792,256]{1,0:T(8,128)(2,1)} %bitcast.64, bf16[1792,3200]{1,0:T(8,128)(2,1)} %bitcast.49, bf16[6400,896]{1,0:T(8,128)(2,1)} %bitcast.50, ...), custom_call_target="tpu_custom_call" | custom-call | tf_op jit(solution)/shard_map/pallas_call | solution.py:797
  259.2 1.2 copy.39
  260.4 0.1 reshape_reshape.19
  260.5 0.8 copy.41
  261.3 0.8 fusion.2
  262.1 0.6 pad_maximum_fusion.1.refs_4_
  262.7 0.7 reduce.3
  263.4 0.6 maximum_bitcast_fusion.refs_13_
  264.1 222.9 %shard_map.256 = (bf16[4,4,2,56,896]{4,3,2,1,0:T(8,128)(2,1)}, bf16[4,4,2,56,2432]{4,3,2,1,0:T(8,128)(2,1)}, bf16[896,256]{1,0:T(8,128)(2,1)}, f32[50,896]{1,0:T...) custom-call(f32[896,256]{1,0:T(8,128)} %get-tuple-element.51.refs_0_, ...), custom_call_target="tpu_custom_call" | custom-call | tf_op jit(solution)/shard_map/pallas_call | solution.py:719
  487.0 1.2 reshape_reshape.20
  488.2 0.8 copy.42
  489.1 0.7 slice_bitcast_fusion.1
  489.8 0.1 pad_maximum_fusion
  489.9 0.7 reshape.150
  490.6 1.3 slice_bitcast_fusion
  491.9 0.7 slice.99
  492.7 0.1 reshape_reshape.21
  492.8 0.7 slice.118
  493.5 0.7 slice.114
  494.1 0.7 slice.112
  494.8 0.7 slice.110
  495.5 0.7 slice.103
  496.2 0.7 slice.101
  496.8 1.4 reshape.148
  498.3 0.9 copy.43
  499.1 1.2 reshape.151
  500.4 0.9 reshape.152
  501.3 1.4 copy.40
  502.7 0.1 reshape.155
  502.8 1.1 copy.44
  504.0 0.9 copy.54
  (20 shorter events, 0.2 us)
Async XLA Ops:
  0.6 20.1 %copy-start.2 = (bf16[2,128,800]{1,2,0:T(8,128)(2,1)S(1)}, bf16[2,128,800]{1,2,0:T(8,128)(2,1)}, u32[]{:S(2)}) copy-start(bf16[2,128,800]{1,2,0:T(8,128)(2,1)} %param.29) | copy-start | bytes 1228804
  21.7 237.4 %copy-start = (bf16[256,16,56]{0,2,1:T(8,128)(2,1)}, bf16[256,16,56]{0,2,1:T(8,128)(2,1)S(1)}, u32[]{:S(2)}) copy-start(bf16[256,16,56]{0,2,1:T(8,128)(2,1)S(1)} %pad.38) | copy-start | bytes 1376260
  487.0 17.0 %copy-start.1 = (f32[50,3200]{1,0:T(8,128)S(1)}, f32[50,3200]{1,0:T(8,128)}, u32[]{:S(2)}) copy-start(f32[50,3200]{1,0:T(8,128)} %get-tuple-element.136) | copy-start | bytes 1920004

commit v5 on v4

--- a/solution.py
+++ b/solution.py
@@ -418,10 +418,10 @@
     head=r//2+13*c; seq=r%2
     def outs(qi,fn):
         def body(i,_):
-            rr=qi*(FQ//128)+(r+i//2)%(FQ//128); cc=i%2
-            fn(obf.at[:,pl.ds(pl.multiple_of(rr*128,128),128)],o_recv.at[seq,head],s_out.at[rr*2+cc],r_out,(rr==r)&(cc==c),(d,rr,cc))
+            rr=qi*(FQ//128)+(r+i)%(FQ//128)
+            fn(obf.at[:,pl.ds(pl.multiple_of(rr*128,128),128)],o_recv.at[seq,head],s_out.at[rr],r_out,rr==r,(d,rr,c))
             return 0
-        lax.fori_loop(0,FQ//64,body,0)
+        lax.fori_loop(0,FQ//128,body,0)
     save=pltpu.make_async_copy(qkv,qkv_out,l_sem)
     @pl.when(item)
     def _():
@@ -466,7 +466,15 @@
     run(FWD_THEN)
     loads=[pltpu.make_async_copy(dst[3],wov,w_sem.at[0]),pltpu.make_async_copy(dst[1],wv,w_sem.at[1])]
     for cp in loads: cp.start()
-    arrived(o_recv,r_out)
+    shares=[o_recv.at[:,pl.ds(0,13)],o_recv.at[:,pl.ds(13,12)]]
+    def hand_over(mine):
+        arrived(shares[mine],r_out)
+        give=pltpu.make_async_remote_copy(src_ref=shares[mine],dst_ref=shares[mine],send_sem=x_sem.at[10],recv_sem=x_sem.at[11],device_id=partner,device_id_type=MESH)
+        give.start()
+        arrived(shares[1-mine],x_sem.at[11])
+        give.wait_send()
+    pl.when(c==0)(lambda:hand_over(0))
+    pl.when(c==1)(lambda:hand_over(1))
     for s in range(2): of[:,pl.ds(128*s,128)]=o_recv[s].reshape(1600,128).astype(jnp.float32)
     for k in range(ROWS):
         op[k,0:50,:]=of[50*k:50*k+50,:].astype(bf)
@@ -478,7 +486,7 @@
     for k in range(7):
         sl=pl.ds(128*k,128)
         mt[sl,:]=mid[:,sl].T+cols[sl,5:6]+xt[sl,:].astype(jnp.float32)
-        mid[:,sl]=mt[sl,:].T
+        mid[:,sl]=(mt[sl,:]+cols[sl,6:7]).T
     norm(1,mt[...],cols[:,0:1],cols[:,4:5],norm2t,h2t).wait()
     loads[1].wait()
     over_blocks(pre,640,h2t,wv)
@@ -494,9 +502,10 @@
         for qi in range(LEN//FQ): outs(qi,pushed)
     full(pushed); halves(pushed)
 BWD_START="e0"
-BWD_AT=((0,"e1o0"),(1,"e2o1"),(2,"c0"),(3,"e3"),(4,"o2"),(5,"c1"),(7,"e4o3"))
-BWD_THEN="e5c2e6o4e7"
-BWD_LAST="q0**c3q1o5c4q2--q3c5o6q4c6q5c7o7q6++q7"
+BWD_MID="e1o0c0"
+BWD_AT=((0,"e2o1"),(1,"c1e3"),(2,"o2"),(3,"e4c2o3"),(4,"c3"),(5,"e5o4"),(6,"c4e6"),(7,"o5"))
+BWD_THEN="e7"
+BWD_LAST="q0c5**o6q1c6q2o7--q3c7q4q5++q6q7"
 BR=224
 KQ=2432
 def unpad_rows(dst,v):
@@ -543,7 +552,6 @@
         dqa[...]=jnp.zeros_like(dqa)
     stage[...]=jnp.zeros_like(stage)
     vtmp[...]=jnp.zeros_like(vtmp)
-    vtmp[pl.ds(35,vec_in.shape[0]),:]=vec_in[...]
     def vec_rows(at,row):
         for k in range(row.shape[1]//128): vtmp[pl.ds(at+k,1),:]=row[:,128*k:128*k+128]
     def norm_back(k,incoming,normed,gain,recip):
@@ -561,9 +569,11 @@
     loads[0].wait(); loads[1].wait()
     vec_rows(14,token_sums(dh[...]*nbuf[...]))
     vec_rows(21,token_sums(dh[...]))
-    gmid[...]=(gt[...].astype(jnp.float32)+norm_back(0,dh[...],nbuf[...],cols[:,0:1],recips[0:1,:]))*cols[:,2:3]
+    gmid[...]=(gt[...].astype(jnp.float32)+norm_back(0,dh[...],nbuf[...],cols[:,0:1],recips[1:2,:]))*cols[:,2:3]
     gat[...]=gmid[...].astype(bf)
     vec_rows(28,token_sums(gat[...]))
+    vec_rows(35,token_sums(gt[...]))
+    vec_rows(42,vec_in[...])
     loads[3].start()
     half=lambda w,base,k:w.at[pl.ds(pl.multiple_of(base*KH+BR*k,32),BR)]
     nb=KH//BR
@@ -610,6 +620,7 @@
     loads[2].wait()
     for cp in emit(part_o,KH,gat[...]).values(): cp.wait()
     loads[4].start()
+    run(BWD_MID)
     def outs(fn):
         seq=pl.ds(pl.multiple_of((r%2)*128,128),128)
         @pl.when(r<24)
@@ -686,7 +697,7 @@
         vec_rows(7,token_sums(dh[...]))
         vec_rows(67,jnp.concatenate((token_sums(grads),jnp.zeros((1,32),jnp.float32)),axis=1))
         v_go(0,vtmp[...])
-        gtok[...]=(gmid[...]+norm_back(1,dh[...],nbuf[...],cols[:,1:2],recips[1:2,:])).astype(bf)
+        gtok[...]=(gmid[...]+norm_back(1,dh[...],nbuf[...],cols[:,1:2],recips[0:1,:])).astype(bf)
         v_go(1,v_total(0))
     def late_vec():
         v_go(2,v_total(1))
@@ -709,7 +720,7 @@
         S((TT,KH),f),S((TT,FH),f),S((TT,FH),bf),S((TT,FH),bf))+gather_shapes(arrs),
       in_specs=[VM]*5+[ANY]*n,out_specs=(ANY,)+(VM,)*12+(ANY,)+(ANY,)*n,
       scratch_shapes=[V((2,25,HD,128),bf),V((3,HD,LEN),bf),V((LEN,HD),bf),V((HD,LEN),bf),V((4,4,2,56,FH),bf),V((4,4,2,56,KH),bf),V((TT,2400),f),V((3,800,TT),bf),V((1600,TT),f),V((KH,TT),f),
-        V((2,8,TT),f),V((2,8,TT),f),DM((26,)),DM((64,)),DM,DM,DM,DM((2,)),DM((10,))]+gather_sems(n),
+        V((2,8,TT),f),V((2,8,TT),f),DM((26,)),DM((32,)),DM,DM,DM,DM((2,)),DM((12,))]+gather_sems(n),
       compiler_params=pltpu.CompilerParams(collective_id=cid,has_side_effects=True,vmem_limit_bytes=62<<20))(xt,cols,bias,eb,segs,*arrs)
     return out[:4],out[4:14],out[14:]
 def attend_back(front,kept,h1t,normt,vec,wq,names,parts,cid=2):
@@ -730,7 +741,7 @@
 
 
 FH=3200; TF=640
-def mlp_kernel(h2t,we,wc,pre,a_own,a_other,mid,cb,g,result,part_c,part_e,dh2,dsum,
+def mlp_kernel(h2t,we,wc,pre,a_own,a_other,mid,g,result,part_c,part_e,dh2,dsum,
         wev,wcv,da_send,da_recv,dpre,dh_send,dh_recv,stage_e,stage_c,w_sem,s_sem,r_sem,e_sem,c_sem):
     c=lax.axis_index("col"); other=1-c
     partner=(lax.axis_index("dev"),lax.axis_index("row"),other)
@@ -787,18 +798,18 @@
     for j in range(KP//256):
         emit(j,stage_e,e_sem,part_e.at[pl.ds(256*j,256)],dot(h2t[256*j:256*j+256,:],dpre[...]).astype(bf))
     br=dot(a_own[...],wcv[rows(c*FH,0,FH),:])+dot(a_other[...],wcv[rows(other*FH,0,FH),:])
-    result[...]=(mid[...]+(br+cb[...])).astype(bf)
+    result[...]=(mid[...]+br).astype(bf)
     x_dh.wait_recv()
     dh2[...]=dh2[...]+f32(dh_recv[...])
     for cp in list(prev.values())+list(prev_c.values()): cp.wait()
     for cp in (x_da,x_dh): cp.wait_send()
-def mlp(h2t,we,wc,pre,a_own,a_other,mid,cb,g,cid=4):
+def mlp(h2t,we,wc,pre,a_own,a_other,mid,g,cid=4):
     S=jax.ShapeDtypeStruct; f=jnp.float32; V=pltpu.VMEM
     return pl.pallas_call(mlp_kernel,
       out_shape=(S((TT,KH),bf),S((6400,KH),bf),S((KP,FH),bf),S((KH,TT),f),S((1,FH),f)),
-      in_specs=[VM,ANY,ANY]+[VM]*6,out_specs=(VM,ANY,ANY,VM,VM),
+      in_specs=[VM,ANY,ANY]+[VM]*5,out_specs=(VM,ANY,ANY,VM,VM),
       scratch_shapes=[V((KP,FH),bf),V((6400,KH),bf)]+[V((TT,FH),bf)]*3+[V((KH,TT),bf)]*2+[V((2,256,FH),bf),V((2,TF,KH),bf)]+[pltpu.SemaphoreType.DMA((n,)) for n in (2,2,2,2,2)],
-      compiler_params=pltpu.CompilerParams(collective_id=cid,has_side_effects=True,vmem_limit_bytes=58<<20))(h2t,we,wc,pre,a_own,a_other,mid,cb,g)
+      compiler_params=pltpu.CompilerParams(collective_id=cid,has_side_effects=True,vmem_limit_bytes=58<<20))(h2t,we,wc,pre,a_own,a_other,mid,g)
 
 
 def pad_rows(block):
@@ -835,14 +846,12 @@
     seqs, block_len, width = tokens.shape
     row_total = seqs * block_len
     grad_low = pad_columns(cotangent.reshape(row_total, width))
-    grad_sums = jnp.sum(grad_low.astype(jnp.float32), axis=0)
     tokens_back = pad_columns(tokens.reshape(row_total, width)).T
     zeros = jnp.zeros_like(first_gain)
     small = jnp.concatenate(
         (second_gain, first_gain, zeros + 1.0, first_bias, second_bias, output_bias, contract_bias, zeros)
     )
-    small = pad_columns(small.reshape(8, width))
-    columns = small.T
+    columns = pad_columns(small.reshape(8, width)).T
     bias_three = jnp.concatenate((attention_bias[0], zeros, attention_bias[1]))
     kept, saved, gathered = attend(
         tokens_back,
@@ -872,7 +881,6 @@
         gelu_own,
         gelu_other,
         middle,
-        small[6:7],
         grad_low,
         4,
     )
@@ -883,14 +891,14 @@
             normed_two,
             grad_low.T,
             columns,
-            jnp.stack((recips[1], recips[0])),
+            recips,
             rows_attn.reshape(KP, row_total),
             weight_out,
         ),
         kept,
         rows_one.reshape(KP, row_total),
         normed_one,
-        jnp.concatenate((grad_sums, expand_sums[0])).reshape(32, 128),
+        expand_sums,
         weight_qkv,
         "ec",
         (

time: 512 us -> 492 us (0.961)
  Pallas kernels: 459 us -> 446 us
    pallas_call x1, Pallas kernels: 223 us -> 214 us  [attend_back(): pl.pallas_call(functools.partial(back_kernel, names, [a.shape[4] for a in...]
where the time goes in v5:
time: 492 us; the launch traced here: 486 us
  Pallas kernels  446 us (91%)
  local copies, waits for them, and re-layouts  38.6 us (8%)
    pallas_call x1, Pallas kernels, attend_back(): pl.pallas_call(functools.partial(back_kernel, names, [a.shape[4] for a in...  214 us
    pallas_call x1, Pallas kernels, attend(): pl.pallas_call(functools.partial(attn_fwd_kernel, names, [a.shape[1] for...  194 us
    pallas_call x1, Pallas kernels, mlp(): pl.pallas_call(mlp_kernel, out_shape=(S((TT, KH), bf), S((6400, KH), bf),...  37.8 us

profile of v5, /device:TPU:0, one launch (start us, length us, event | category | flops | bytes accessed | tf_op | source)
XLA Modules:
  0.0 486.1 jit_solution(11465032671564321715)
XLA Ops:
  0.6 0.0 copy-start.4
  0.7 0.8 concatenate.23
  1.5 0.8 concatenate.24
  2.2 0.8 concatenate.26
  3.0 0.8 concatenate.22
  3.8 0.8 concatenate.25
  4.6 0.8 concatenate.27
  5.3 0.8 slice_reduce_fusion
  6.2 0.1 concatenate.29
  6.2 0.6 broadcast_in_dim.13.refs_2_
  6.8 1.3 broadcast_in_dim.14.refs_3_
  8.2 1.2 reshape.128
  9.5 0.2 reshape.129
  9.8 0.7 pad.37.refs_8_
  10.4 1.1 copy.34
  11.5 0.3 reshape.125
  11.9 0.7 pad.33.refs_5_
  12.6 1.7 pad.34.refs_6_
  14.4 0.2 copy.45
  14.6 0.8 pad.32.clone
  15.4 1.3 copy.32
  16.7 0.3 reshape_reshape.17
  17.0 0.8 pad.31
  17.8 1.2 copy.35
  19.0 0.1 reshape.126
  19.1 0.1 pad.35
  19.2 0.9 copy.36.refs_7_
  20.1 0.0 copy-done.4
  20.1 0.3 copy.37
  20.4 0.3 reshape_reshape.18
  20.8 0.0 copy-start
  20.8 1.0 copy.38.g
  21.7 194.4 %shard_map.254 = (bf16[3,64,4096]{2,1,0:T(8,128)(2,1)}, f32[64,4096]{1,0:T(8,128)}, f32[1,4096]{1,0:T(1,128)}, s32[1,4096]{1,0:T(1,128)}, bf16[32,56,256]{2,1,0:...) custom-call(bf16[896,256]{1,0:T(8,128)(2,1)} %bitcast.57, ...), custom_call_target="tpu_custom_call" | custom-call | tf_op jit(solution)/shard_map/pallas_call | solution.py:718
  216.1 37.8 %shard_map.255 = (bf16[256,896]{1,0:T(8,128)(2,1)}, bf16[6400,896]{1,0:T(8,128)(2,1)}, bf16[1792,3200]{1,0:T(8,128)(2,1)}, f32[896,256]{1,0:T(8,128)}, f32[1,3200]{1,0:T(1,128)}) custom-call(bf16[1792,256]{1,0:T(8,128)(2,1)} %bitcast.62, bf16[1792,3200]{1,0:T(8,128)(2,1)} %bitcast.47, bf16[6400,896]{1,0:T(8,128)(2,1)} %bitcast.48, ...), custom_call_target="tpu_custom_call" | custom-call | tf_op jit(solution)/shard_map/pallas_call | solution.py:808
  254.0 0.0 copy-done
  254.0 0.0 copy-start.3
  254.0 213.8 %shard_map.256 = (bf16[4,4,2,56,896]{4,3,2,1,0:T(8,128)(2,1)}, bf16[4,4,2,56,2432]{4,3,2,1,0:T(8,128)(2,1)}, bf16[896,256]{1,0:T(8,128)(2,1)}, f32[50,896]{1,0:T...) custom-call(f32[896,256]{1,0:T(8,128)} %get-tuple-element.51.refs_0_, ...), custom_call_target="tpu_custom_call" | custom-call | tf_op jit(solution)/shard_map/pallas_call | solution.py:730
  467.8 0.2 copy.39
  468.1 0.1 reshape_reshape.19
  468.2 0.8 copy.41
  469.0 1.2 reshape_reshape.20
  470.2 0.8 copy.42
  471.0 0.7 slice_bitcast_fusion.1
  471.7 0.1 fusion.1
  471.8 0.1 pad_maximum_fusion
  471.8 0.7 reshape.144
  472.5 1.3 slice_bitcast_fusion
  473.9 0.7 slice.83
  474.6 0.1 reshape_reshape.21
  474.7 0.7 slice.102
  475.4 0.7 slice.98
  476.1 0.7 slice.96
  476.7 0.7 slice.94
  477.4 0.7 slice.87
  478.1 0.7 slice.85
  478.8 1.4 reshape.142
  480.2 0.9 copy.43
  481.1 1.2 reshape.145
  482.3 0.9 reshape.146
  483.2 0.3 copy.40
  483.5 0.1 reshape.149
  483.6 1.1 copy.44
  484.8 0.0 copy-done.1
  484.8 0.9 copy.54
  (16 shorter events, 0.1 us)
Async XLA Ops:
  0.6 19.5 %copy-start.4 = (bf16[2,128,800]{1,2,0:T(8,128)(2,1)S(1)}, bf16[2,128,800]{1,2,0:T(8,128)(2,1)}, u32[]{:S(2)}) copy-start(bf16[2,128,800]{1,2,0:T(8,128)(2,1)} %param.29) | copy-start | bytes 1228804
  20.8 233.2 %copy-start = (bf16[256,16,56]{0,2,1:T(8,128)(2,1)}, bf16[256,16,56]{0,2,1:T(8,128)(2,1)S(1)}, u32[]{:S(2)}) copy-start(bf16[256,16,56]{0,2,1:T(8,128)(2,1)S(1)} %pad.38) | copy-start | bytes 1376260
  254.0 213.8 %copy-start.3 = (bf16[256,896]{1,0:T(8,128)(2,1)S(1)}, bf16[256,896]{1,0:T(8,128)(2,1)}, u32[]{:S(2)}) copy-start(bf16[256,896]{1,0:T(8,128)(2,1)} %get-tuple-element.50) | copy-start | bytes 1376260
  467.8 15.4 %copy-start.2 = (f32[200,896]{1,0:T(8,128)S(1)}, f32[200,896]{1,0:T(8,128)}, u32[]{:S(2)}) copy-start(f32[200,896]{1,0:T(8,128)} %get-tuple-element.71) | copy-start | bytes 2150404
  467.8 17.0 %copy-start.1 = (f32[50,3200]{1,0:T(8,128)S(1)}, f32[50,3200]{1,0:T(8,128)}, u32[]{:S(2)}) copy-start(f32[50,3200]{1,0:T(8,128)} %get-tuple-element.134) | copy-start | bytes 1920004

commit v6 on v5

--- a/solution.py
+++ b/solution.py
@@ -298,15 +298,26 @@
 def dot_nt(a,b): return lax.dot_general(a,b,(((1,),(1,)),((),())),preferred_element_type=jnp.float32)
 def group_greet(d,r,c,across):
     bar=pltpu.get_barrier_semaphore()
-    for rr in across: pl.semaphore_signal(bar,inc=1,device_id=(1-d,rr,c),device_id_type=MESH)
-    def body(i,_):
-        @pl.when(i!=r*2+c)
-        def _():
-            pl.semaphore_signal(bar,inc=1,device_id=(d,i//2,i%2),device_id_type=MESH)
+    def greet_one(*target):
+        pl.semaphore_signal(bar,inc=1,device_id=target,device_id_type=MESH)
+    for rr in across: greet_one(1-d,rr,c)
+    greet_one(d,r,1-c)
+    def column(i,_):
+        greet_one(d,(r+i)%ROWS,c)
         return 0
-    lax.fori_loop(0,2*ROWS,body,0)
-def group_wait(across):
-    pl.semaphore_wait(pltpu.get_barrier_semaphore(),2*ROWS-1+across)
+    lax.fori_loop(1,ROWS,column,0)
+    @pl.when(c==1)
+    def _():
+        greet_one(d,24,0); greet_one(d,25,0)
+    @pl.when((c==0)&(r//2==12))
+    def _():
+        def other_column(i,_):
+            greet_one(d,i,1)
+            return 0
+        lax.fori_loop(0,ROWS,other_column,0)
+def group_wait(r,c,across):
+    shared=(1-jnp.minimum(jnp.abs(r//2-12),1))*(1-c)
+    pl.semaphore_wait(pltpu.get_barrier_semaphore(),ROWS+across+2*c+ROWS*shared)
 def push(src,dst,send_sem,recv_sem,same,target):
     @pl.when(same)
     def _():
@@ -372,7 +383,7 @@
     for k in range(12):
         first=jnp.maximum(first,jnp.where(pos>=2**k,pltpu.roll(first,2**k,1),0))
     start[...]=first[0:1,:]
-    group_wait(1)
+    group_wait(r,c,1)
     run(["q0","e0"])
     sent=norm(0,xt[...].astype(jnp.float32),cols[:,1:2],cols[:,3:4],norm1t,h1t)
     run(FWD_BEFORE)
@@ -564,7 +575,7 @@
         s1=stat_s[k,0:1,:]+stat_r[k,0:1,:]
         s2=stat_s[k,1:2,:]+stat_r[k,1:2,:]
         return recip*(e-s1*(1.0/D)-normed*(s2*(1.0/D)))
-    group_wait(2)
+    group_wait(r,c,2)
     run(BWD_START)
     loads[0].wait(); loads[1].wait()
     vec_rows(14,token_sums(dh[...]*nbuf[...]))

time: 492 us -> 494 us (level)
  no operation moved by 1% of the time
where the time goes in v6:
time: 494 us; the launch traced here: 487 us
  Pallas kernels  447 us (90%)
  local copies, waits for them, and re-layouts  38.6 us (8%)
    pallas_call x1, Pallas kernels, attend_back(): pl.pallas_call(functools.partial(back_kernel, names, [a.shape[4] for a in...  216 us
    pallas_call x1, Pallas kernels, attend(): pl.pallas_call(functools.partial(attn_fwd_kernel, names, [a.shape[1] for...  193 us
    pallas_call x1, Pallas kernels, mlp(): pl.pallas_call(mlp_kernel, out_shape=(S((TT, KH), bf), S((6400, KH), bf),...  37.8 us

profile of v6, /device:TPU:0, one launch (start us, length us, event | category | flops | bytes accessed | tf_op | source)
XLA Modules:
  0.0 487.0 jit_solution(16641402912645358291)
XLA Ops:
  0.6 0.0 copy-start.4
  0.7 0.8 concatenate.23
  1.5 0.8 concatenate.24
  2.2 0.8 concatenate.26
  3.0 0.8 concatenate.22
  3.8 0.8 concatenate.25
  4.6 0.8 concatenate.27
  5.3 0.8 slice_reduce_fusion
  6.2 0.1 concatenate.29
  6.2 0.6 broadcast_in_dim.13.refs_2_
  6.8 1.3 broadcast_in_dim.14.refs_3_
  8.2 1.2 reshape.128
  9.5 0.2 reshape.129
  9.8 0.7 pad.37.refs_8_
  10.4 1.1 copy.34
  11.5 0.3 reshape.125
  11.9 0.7 pad.33.refs_5_
  12.6 1.7 pad.34.refs_6_
  14.4 0.2 copy.45
  14.6 0.8 pad.32.clone
  15.4 1.3 copy.32
  16.7 0.3 reshape_reshape.17
  17.0 0.8 pad.31
  17.8 1.2 copy.35
  19.0 0.1 reshape.126
  19.1 0.1 pad.35
  19.2 0.9 copy.36.refs_7_
  20.1 0.0 copy-done.4
  20.1 0.3 copy.37
  20.4 0.3 reshape_reshape.18
  20.8 0.0 copy-start
  20.8 1.0 copy.38.g
  21.7 192.8 %shard_map.254 = (bf16[3,64,4096]{2,1,0:T(8,128)(2,1)}, f32[64,4096]{1,0:T(8,128)}, f32[1,4096]{1,0:T(1,128)}, s32[1,4096]{1,0:T(1,128)}, bf16[32,56,256]{2,1,0:...) custom-call(bf16[896,256]{1,0:T(8,128)(2,1)} %bitcast.57, ...), custom_call_target="tpu_custom_call" | custom-call | tf_op jit(solution)/shard_map/pallas_call | solution.py:729
  214.5 37.8 %shard_map.255 = (bf16[256,896]{1,0:T(8,128)(2,1)}, bf16[6400,896]{1,0:T(8,128)(2,1)}, bf16[1792,3200]{1,0:T(8,128)(2,1)}, f32[896,256]{1,0:T(8,128)}, f32[1,3200]{1,0:T(1,128)}) custom-call(bf16[1792,256]{1,0:T(8,128)(2,1)} %bitcast.62, bf16[1792,3200]{1,0:T(8,128)(2,1)} %bitcast.47, bf16[6400,896]{1,0:T(8,128)(2,1)} %bitcast.48, ...), custom_call_target="tpu_custom_call" | custom-call | tf_op jit(solution)/shard_map/pallas_call | solution.py:819
  252.3 0.0 copy-done
  252.3 0.0 copy-start.3
  252.4 216.3 %shard_map.256 = (bf16[4,4,2,56,896]{4,3,2,1,0:T(8,128)(2,1)}, bf16[4,4,2,56,2432]{4,3,2,1,0:T(8,128)(2,1)}, bf16[896,256]{1,0:T(8,128)(2,1)}, f32[50,896]{1,0:T...) custom-call(f32[896,256]{1,0:T(8,128)} %get-tuple-element.51.refs_0_, ...), custom_call_target="tpu_custom_call" | custom-call | tf_op jit(solution)/shard_map/pallas_call | solution.py:741
  468.7 0.0 copy-start.2
  468.7 0.2 copy.39
  468.9 0.1 reshape_reshape.19
  469.1 0.8 copy.41
  469.9 1.2 reshape_reshape.20
  471.1 0.8 copy.42
  471.9 0.7 slice_bitcast_fusion.1
  472.6 0.1 fusion.1
  472.6 0.1 pad_maximum_fusion
  472.7 0.7 reshape.144
  473.4 1.3 slice_bitcast_fusion
  474.7 0.7 slice.83
  475.5 0.1 reshape_reshape.21
  475.6 0.7 slice.102
  476.3 0.7 slice.98
  476.9 0.7 slice.96
  477.6 0.7 slice.94
  478.3 0.7 slice.87
  479.0 0.7 slice.85
  479.6 1.4 reshape.142
  481.1 0.9 copy.43
  481.9 1.2 reshape.145
  483.2 0.9 reshape.146
  484.1 0.3 copy.40
  484.4 0.1 reshape.149
  484.5 1.1 copy.44
  485.7 0.9 copy.54
  (16 shorter events, 0.1 us)
Async XLA Ops:
  0.6 19.5 %copy-start.4 = (bf16[2,128,800]{1,2,0:T(8,128)(2,1)S(1)}, bf16[2,128,800]{1,2,0:T(8,128)(2,1)}, u32[]{:S(2)}) copy-start(bf16[2,128,800]{1,2,0:T(8,128)(2,1)} %param.29) | copy-start | bytes 1228804
  20.8 231.6 %copy-start = (bf16[256,16,56]{0,2,1:T(8,128)(2,1)}, bf16[256,16,56]{0,2,1:T(8,128)(2,1)S(1)}, u32[]{:S(2)}) copy-start(bf16[256,16,56]{0,2,1:T(8,128)(2,1)S(1)} %pad.38) | copy-start | bytes 1376260
  252.3 216.4 %copy-start.3 = (bf16[256,896]{1,0:T(8,128)(2,1)S(1)}, bf16[256,896]{1,0:T(8,128)(2,1)}, u32[]{:S(2)}) copy-start(bf16[256,896]{1,0:T(8,128)(2,1)} %get-tuple-element.50) | copy-start | bytes 1376260
  468.7 15.4 %copy-start.2 = (f32[200,896]{1,0:T(8,128)S(1)}, f32[200,896]{1,0:T(8,128)}, u32[]{:S(2)}) copy-start(f32[200,896]{1,0:T(8,128)} %get-tuple-element.71) | copy-start | bytes 2150404
  468.7 17.0 %copy-start.1 = (f32[50,3200]{1,0:T(8,128)S(1)}, f32[50,3200]{1,0:T(8,128)}, u32[]{:S(2)}) copy-start(f32[50,3200]{1,0:T(8,128)} %get-tuple-element.134) | copy-start | bytes 1920004

commit v7 on v5

--- a/solution.py
+++ b/solution.py
@@ -762,10 +762,6 @@
             f(k)
             return 0
         lax.fori_loop(0,n,body,0)
-    loads[0].wait()
-    def f(k): da_send[:,lanes(k,TF)]=dot_nt(g[...],wcv[rows(other*FH,k,TF),:]).astype(bf)
-    loop(NT,f)
-    x_da.start()
     def emit(i,stage,sem,dst,value):
         slot=i%2
         cp=pltpu.make_async_copy(stage.at[slot],dst,sem.at[slot])
@@ -774,6 +770,11 @@
         cp.start(); prev[slot]=cp
     prev={}
     for i in range(2*NT):
+        if i==NT:
+            loads[0].wait()
+            def f(k): da_send[:,lanes(k,TF)]=dot_nt(g[...],wcv[rows(other*FH,k,TF),:]).astype(bf)
+            loop(NT,f)
+            x_da.start()
         a,b,k=(a_own,c,i) if i<NT else (a_other,other,i-NT)
         emit(i,stage_c,c_sem,part_c.at[rows(b*FH,k,TF)],dot_tn(a[:,k*TF:k*TF+TF],g[...]).astype(bf))
     prev_c=prev

time: 492 us -> 491 us (level)
  no operation moved by 1% of the time
where the time goes in v7:
time: 491 us; the launch traced here: 485 us
  Pallas kernels  445 us (91%)
  local copies, waits for them, and re-layouts  38.6 us (8%)
    pallas_call x1, Pallas kernels, attend_back(): pl.pallas_call(functools.partial(back_kernel, names, [a.shape[4] for a in...  214 us
    pallas_call x1, Pallas kernels, attend(): pl.pallas_call(functools.partial(attn_fwd_kernel, names, [a.shape[1] for...  194 us
    pallas_call x1, Pallas kernels, mlp(): pl.pallas_call(mlp_kernel, out_shape=(S((TT, KH), bf), S((6400, KH), bf),...  36.7 us

profile of v7, /device:TPU:0, one launch (start us, length us, event | category | flops | bytes accessed | tf_op | source)
XLA Modules:
  0.0 484.9 jit_solution(208957932470329979)
XLA Ops:
  0.6 0.0 copy-start.4
  0.7 0.8 concatenate.23
  1.5 0.8 concatenate.24
  2.2 0.8 concatenate.26
  3.0 0.8 concatenate.22
  3.8 0.8 concatenate.25
  4.6 0.8 concatenate.27
  5.3 0.8 slice_reduce_fusion
  6.2 0.1 concatenate.29
  6.2 0.6 broadcast_in_dim.13.refs_2_
  6.8 1.3 broadcast_in_dim.14.refs_3_
  8.2 1.2 reshape.128
  9.5 0.2 reshape.129
  9.8 0.7 pad.37.refs_8_
  10.4 1.1 copy.34
  11.5 0.3 reshape.125
  11.9 0.7 pad.33.refs_5_
  12.6 1.7 pad.34.refs_6_
  14.4 0.2 copy.45
  14.6 0.8 pad.32.clone
  15.4 1.3 copy.32
  16.7 0.3 reshape_reshape.17
  17.0 0.8 pad.31
  17.8 1.2 copy.35
  19.0 0.1 reshape.126
  19.1 0.1 pad.35
  19.2 0.9 copy.36.refs_7_
  20.1 0.0 copy-done.4
  20.1 0.3 copy.37
  20.4 0.3 reshape_reshape.18
  20.8 0.0 copy-start
  20.8 1.0 copy.38.g
  21.7 194.4 %shard_map.254 = (bf16[3,64,4096]{2,1,0:T(8,128)(2,1)}, f32[64,4096]{1,0:T(8,128)}, f32[1,4096]{1,0:T(1,128)}, s32[1,4096]{1,0:T(1,128)}, bf16[32,56,256]{2,1,0:...) custom-call(bf16[896,256]{1,0:T(8,128)(2,1)} %bitcast.57, ...), custom_call_target="tpu_custom_call" | custom-call | tf_op jit(solution)/shard_map/pallas_call | solution.py:718
  216.1 36.7 %shard_map.255 = (bf16[256,896]{1,0:T(8,128)(2,1)}, bf16[6400,896]{1,0:T(8,128)(2,1)}, bf16[1792,3200]{1,0:T(8,128)(2,1)}, f32[896,256]{1,0:T(8,128)}, f32[1,3200]{1,0:T(1,128)}) custom-call(bf16[1792,256]{1,0:T(8,128)(2,1)} %bitcast.62, bf16[1792,3200]{1,0:T(8,128)(2,1)} %bitcast.47, bf16[6400,896]{1,0:T(8,128)(2,1)} %bitcast.48, ...), custom_call_target="tpu_custom_call" | custom-call | tf_op jit(solution)/shard_map/pallas_call | solution.py:809
  252.8 0.0 copy-done
  252.8 0.0 copy-start.3
  252.8 213.8 %shard_map.256 = (bf16[4,4,2,56,896]{4,3,2,1,0:T(8,128)(2,1)}, bf16[4,4,2,56,2432]{4,3,2,1,0:T(8,128)(2,1)}, bf16[896,256]{1,0:T(8,128)(2,1)}, f32[50,896]{1,0:T...) custom-call(f32[896,256]{1,0:T(8,128)} %get-tuple-element.51.refs_0_, ...), custom_call_target="tpu_custom_call" | custom-call | tf_op jit(solution)/shard_map/pallas_call | solution.py:730
  466.6 0.0 copy-start.2
  466.6 0.2 copy.39
  466.9 0.1 reshape_reshape.19
  467.0 0.8 copy.41
  467.8 1.2 reshape_reshape.20
  469.0 0.8 copy.42
  469.8 0.7 slice_bitcast_fusion.1
  470.5 0.1 fusion.1
  470.6 0.1 pad_maximum_fusion
  470.7 0.7 reshape.144
  471.3 1.3 slice_bitcast_fusion
  472.7 0.7 slice.83
  473.4 0.1 reshape_reshape.21
  473.5 0.7 slice.102
  474.2 0.7 slice.98
  474.9 0.7 slice.96
  475.5 0.7 slice.94
  476.2 0.7 slice.87
  476.9 0.7 slice.85
  477.6 1.4 reshape.142
  479.0 0.9 copy.43
  479.9 1.2 reshape.145
  481.1 0.9 reshape.146
  482.0 0.3 copy.40
  482.3 0.1 reshape.149
  482.4 1.1 copy.44
  483.6 0.9 copy.54
  (16 shorter events, 0.1 us)
Async XLA Ops:
  0.6 19.5 %copy-start.4 = (bf16[2,128,800]{1,2,0:T(8,128)(2,1)S(1)}, bf16[2,128,800]{1,2,0:T(8,128)(2,1)}, u32[]{:S(2)}) copy-start(bf16[2,128,800]{1,2,0:T(8,128)(2,1)} %param.29) | copy-start | bytes 1228804
  20.8 232.1 %copy-start = (bf16[256,16,56]{0,2,1:T(8,128)(2,1)}, bf16[256,16,56]{0,2,1:T(8,128)(2,1)S(1)}, u32[]{:S(2)}) copy-start(bf16[256,16,56]{0,2,1:T(8,128)(2,1)S(1)} %pad.38) | copy-start | bytes 1376260
  252.8 213.8 %copy-start.3 = (bf16[256,896]{1,0:T(8,128)(2,1)S(1)}, bf16[256,896]{1,0:T(8,128)(2,1)}, u32[]{:S(2)}) copy-start(bf16[256,896]{1,0:T(8,128)(2,1)} %get-tuple-element.50) | copy-start | bytes 1376260
  466.6 15.4 %copy-start.2 = (f32[200,896]{1,0:T(8,128)S(1)}, f32[200,896]{1,0:T(8,128)}, u32[]{:S(2)}) copy-start(f32[200,896]{1,0:T(8,128)} %get-tuple-element.71) | copy-start | bytes 2150404
  466.6 17.0 %copy-start.1 = (f32[50,3200]{1,0:T(8,128)S(1)}, f32[50,3200]{1,0:T(8,128)}, u32[]{:S(2)}) copy-start(f32[50,3200]{1,0:T(8,128)} %get-tuple-element.134) | copy-start | bytes 1920004
